TPU v7x, 512 devices: a whole 4x8x8 slice. The times are simulated.
512 devices in a mesh: wide: 128 (over z, y, core), narrow: 4 (over x).
Axes of the slice: x: 4, y: 8, z: 8, core: 2. Of those that a mesh axis runs over, the one named last changes fastest.
Arguments:
- features: bfloat16 [131072, 128], P('wide'), may hold values from -6 to 6
- weight: bfloat16 [128, 256], replicated, may hold values from -0.5 to 0.5
- bias: float32 [256], replicated, may hold values from -3 to 3
- cotangent: bfloat16 [131072, 256], P(('wide', 'narrow')), may hold values from -0.032958984 to 0.032958984
- tile_values: bfloat16 [128, 4, 128, 128, 128], P('wide', 'narrow'), may hold values from 0 to 0.053955078
- tile_row: int32 [128, 4, 128], P('wide', 'narrow'), may hold values from 0 to 7
- tile_source: int32 [128, 4, 128], P('wide', 'narrow'), may hold values from 0 to 127
- tile_count: int32 [128, 4], P('wide', 'narrow'), may hold values from 32 to 128, as said below
- pick: int32 [128, 4, 128], P('wide', 'narrow'), may hold values from 0 to 1
Outputs:
- hidden: bfloat16 [131072, 256], P(('wide', 'narrow'))
- grad_weight: float32 [128, 256], replicated
- grad_bias: float32 [256], replicated
Inputs may be any that keep to these rules, and one draw needn't show every extreme that they name: `tile_count`: slots at or beyond a device's count are ignored; some device holds exactly 128 live slots.
All inputs are finite; a program needn't handle non-finite values.
Results may differ from a plain program's by a relative error of at most 0.0056.
Values may be sent and summed in bfloat16 or wider, within the bound.
No kernel may reach another device: no remote copies, remote signals or barrier semaphores. Data moves between devices by JAX's collectives and lax.ppermute only.
A program may use at most 64 MiB of HBM per device.

v0:
```python
import jax
import jax.numpy as jnp
from jax import lax
from jax.sharding import PartitionSpec as P

FIN = 128
TILE = 128
TR = 8


def local(features, weight, bias, cotangent, tile_values, tile_row, tile_source, tile_count, pick):
    tile_span = TR // lax.axis_size("narrow")
    narrow_pos = lax.axis_index("narrow")
    slot_values = tile_values[0, 0]
    tile_rows = tile_row[0, 0]
    sources = tile_source[0, 0]
    live_count = tile_count[0, 0]
    my_picks = pick[0, 0]
    own_tiles = features.reshape(TR, TILE, FIN)
    slice_tiles = lax.dynamic_slice_in_dim(own_tiles, narrow_pos * tile_span, tile_span, 0)
    gathered = lax.all_gather(slice_tiles, "wide", axis=0, tiled=True)
    needed = gathered[sources * tile_span + my_picks[sources]]
    products = jnp.einsum("tij,tjf->tif", slot_values, needed, preferred_element_type=jnp.float32)
    slot_index = jnp.arange(slot_values.shape[0], dtype=jnp.int32)
    live_mask = (slot_index < live_count).astype(jnp.float32)
    row_index = jnp.arange(TR, dtype=jnp.int32)
    selector = (tile_rows[None, :] == row_index[:, None]).astype(jnp.float32) * live_mask[None, :]
    partial_rows = jnp.einsum(
        "rt,tif->rif", selector, products, precision=lax.Precision.HIGHEST
    ).reshape(TR * TILE, FIN)
    aggregated = lax.psum_scatter(partial_rows, "narrow", scatter_dimension=0, tiled=True).astype(
        jnp.bfloat16
    )
    preact = jnp.dot(aggregated, weight, preferred_element_type=jnp.float32) + bias
    hidden = jax.nn.silu(preact).astype(jnp.bfloat16)
    sigmoid_pre = jax.nn.sigmoid(preact)
    dpreact = cotangent.astype(jnp.float32) * (sigmoid_pre * (1.0 + preact * (1.0 - sigmoid_pre)))
    weight_part = jnp.dot(
        aggregated.T, dpreact.astype(jnp.bfloat16), preferred_element_type=jnp.float32
    )
    bias_part = jnp.sum(dpreact, axis=0)
    grad_weight, grad_bias = lax.psum((weight_part, bias_part), ("wide", "narrow"))
    return (hidden, grad_weight, grad_bias)


def solution(mesh):
    placed = (
        P("wide", None),
        P(),
        P(),
        P(("wide", "narrow"), None),
        P("wide", "narrow", None, None, None),
        P("wide", "narrow", None),
        P("wide", "narrow", None),
        P("wide", "narrow"),
        P("wide", "narrow", None),
    )
    return jax.shard_map(
        local,
        mesh=mesh,
        in_specs=placed,
        out_specs=(P(("wide", "narrow"), None), P(), P()),
        check_vma=False,
    )
```

profile of v0, /device:TPU:1, one launch (start us, length us, event | category | flops | bytes accessed | tf_op | source)
XLA Modules:
  0.0 437.0 jit_solution(8336531581098484695)
XLA Ops:
  7.2 0.0 copy-start
  7.2 0.0 all-gather.2.cloned.1.call-start
  7.2 0.9 copy-done
  8.1 0.6 constant_dynamic-slice_fusion
  8.8 0.0 all-gather.2.cloned.1.call-update
  8.8 0.0 reduce-scatter.2.cloned.1.call-start
  9.5 0.7 fusion.15
  10.1 1.6 gather_fusion
  11.7 0.7 fusion.16
  12.4 93.4 %all-gather.2.cloned.1.call-done = bf16[256,128,128]{2,1,0:T(8,128)(2,1)} async-done(((bf16[2,128,128]{2,1,0:T(8,128)(2,1)}), bf16[256,128,128]{2,1,0:T(8,128)(2,1)}) %all-gather.2.cloned.1.call-update) | async-done | bytes 8388624 | tf_op jit(solution)/shard_map/all_gather | solution.py:21
  105.8 6.4 %gather_fusion.1 = bf16[128,128,128]{2,1,0:T(8,128)(2,1)} fusion(bf16[256,128,128]{2,1,0:T(8,128)(2,1)} %all-gather.2.cloned.1.call-done, s32[1024]{0:T(1024)S(1)} %pad_clamp_fusion), kind=kCustom, calls=%fused_computation.1 | custom fusion | bytes 8389120 | tf_op jit(solution)/shard_map/gather | solution.py:22
  112.2 9.8 %fusion.2 = f32[128,128,128]{1,2,0:T(8,128)} fusion(bf16[128,128,128]{2,1,0:T(8,128)(2,1)} %gather_fusion.1, bf16[1,1,128,128,128]{4,3,2,1,0:T(8,128)(2,1)} %param.13), kind=kOutput, calls=%fused_computation.4 | convolution fusion | flops 536870912 | bytes 16777216 | tf_op jit(solution)/shard_map/tij,tjf->tif/dot_general | solution.py:23
  121.9 0.0 copy-start.1
  122.0 9.3 %copy.14 = f32[128,128,128]{2,0,1:T(8,128)} copy(f32[128,128,128]{1,2,0:T(8,128)} %fusion.2) | data formatting | bytes 16777216 | tf_op jit(solution)/shard_map/tij,tjf->tif/dot_general | solution.py:23
  131.2 0.0 copy-done.1
  131.2 0.0 copy-start.2
  131.2 0.0 copy-start.3
  131.2 0.0 copy-start.4
  131.2 6.4 %fusion.9 = f32[8,128,128]{2,0,1:T(8,128)S(1)} fusion(f32[128,128,128]{2,0,1:T(8,128)} %copy.14, f32[128]{0:T(128)S(1)} %compare_convert_fusion, s32[128]{0:T(128)S(1)} %bitcast.35), kind=kOutput, calls=%fused_computation.15 | convolution fusion | flops 201328640 | bytes 8913920 | tf_op jit(solution)/shard_map/rt,tif->rif/dot_general | solution.py:28
  137.6 0.9 copy.15
  138.5 0.0 reduce-scatter.2.cloned.1.call-update
  138.5 0.0 all-reduce.2.cloned.1.call-start
  138.6 21.4 %reduce-scatter.2.cloned.1.call-done = f32[256,128]{1,0:T(8,128)} async-done(((f32[1024,128]{1,0:T(8,128)}), f32[256,128]{1,0:T(8,128)}) %reduce-scatter.2.cloned.1.call-update) | async-done | bytes 131088 | tf_op jit(solution)/shard_map/reduce_scatter | solution.py:31
  160.0 0.0 copy-done.2
  160.0 0.0 copy-done.3
  160.0 0.0 copy-done.4
  160.0 1.8 fusion.18
  161.9 1.8 fusion.5
  163.7 0.0 all-reduce.2.cloned.1.call-update
  163.7 99.3 %psum.15 = f32[256]{0:T(256)} all-reduce(f32[256]{0:T(256)S(1)} %get-tuple-element.3), channel_id=1, replica_groups=mesh['wide'=128,'narrow'=4] {'wide','narrow'}, use_global_device_ids=true, to_apply=%region_3.4 | all-reduce | flops 256 | bytes 2048 | tf_op jit(solution)/shard_map/psum | solution.py:42
  263.0 165.9 %all-reduce.2.cloned.1.call-done = f32[128,256]{1,0:T(8,128)} async-done(((f32[128,256]{1,0:T(8,128)}), f32[128,256]{1,0:T(8,128)}) %all-reduce.2.cloned.1.call-update) | async-done | bytes 131088 | tf_op jit(solution)/shard_map/psum | solution.py:42
  428.9 1.6 copy.19
  (3 shorter events, 0.0 us)
Async XLA Ops:
  7.2 1.0 copy-start
  7.2 98.6 %all-gather.2.cloned.1.call-start = ((), (), s32[]{:S(2)}) async-start(), calls=%async_computation.1 | async-start | bytes 8454144 | tf_op jit(solution)/shard_map/all_gather | solution.py:21
  8.8 151.3 %reduce-scatter.2.cloned.1.call-start = ((), (), s32[]{:S(2)}) async-start(), calls=%async_computation.2 | async-start | bytes 655360 | tf_op jit(solution)/shard_map/reduce_scatter | solution.py:31
  121.9 9.3 %copy-start.1 = (s32[1,1,128]{2,1,0:T(1,128)S(1)}, s32[1,1,128]{2,1,0:T(1,128)}, u32[]{:S(2)}) copy-start(s32[1,1,128]{2,1,0:T(1,128)} %param.14) | copy-start | bytes 1540
  131.2 28.8 %copy-start.2 = (bf16[256,256]{1,0:T(8,128)(2,1)S(1)}, bf16[256,256]{1,0:T(8,128)(2,1)}, u32[]{:S(2)}) copy-start(bf16[256,256]{1,0:T(8,128)(2,1)} %param.12) | copy-start | bytes 393220
  131.2 28.8 %copy-start.3 = (bf16[128,256]{1,0:T(8,128)(2,1)S(1)}, bf16[128,256]{1,0:T(8,128)(2,1)}, u32[]{:S(2)}) copy-start(bf16[128,256]{1,0:T(8,128)(2,1)} %param.10) | copy-start | bytes 196612
  131.2 28.8 %copy-start.4 = (f32[256]{0:T(256)S(1)}, f32[256]{0:T(256)}, u32[]{:S(2)}) copy-start(f32[256]{0:T(256)} %param.11) | copy-start | bytes 3076
  138.5 290.4 %all-reduce.2.cloned.1.call-start = ((), (), s32[]{:S(2)}) async-start(), calls=%async_computation.3 | async-start | bytes 262144 | tf_op jit(solution)/shard_map/psum | solution.py:42
Sparse Core Ops, SparseCore 0:
  11.7 94.0 all-gather.1
  138.7 21.3 reduce-scatter.1
  165.6 263.2 all-reduce.1
where the time goes:
time: 437 us
  waiting for transfers between devices  281 us (64%)
  blocking collectives  99.3 us (23%)
  local copies, waits for them, and re-layouts  21.3 us (5%)
  matrix products  19.8 us (5%)
  between operations  14.4 us (3%)
    psum x1, waiting for transfers between devices, local(): lax.psum((weight_part, bias_part), ('wide', 'narrow'))  166 us
    psum x1, blocking collectives, local(): lax.psum((weight_part, bias_part), ('wide', 'narrow'))  99.3 us
    all_gather x1, waiting for transfers between devices, local(): gathered = lax.all_gather(slice_tiles, 'wide', axis=0, tiled=True)  93.4 us
    reduce_scatter x1, waiting for transfers between devices, local(): lax.psum_scatter(partial_rows, 'narrow', scatter_dimension=0, tiled=True)  21.4 us
    dot_general x1, matrix products, local(): jnp.einsum('tij,tjf->tif', slot_values, needed, preferred_element_type=jn...  9.76 us
    dot_general x1, local copies, waits for them, and re-layouts, local(): jnp.einsum('tij,tjf->tif', slot_values, needed, preferred_element_type=jn...  9.27 us
  transfers between devices with their start and end apart: 3, of which 3 were waited for; matrix products, arithmetic and copies ran while one was open for 1% of the time, Pallas kernels for 0%

commit v1 on v0

v1 whole, which is shorter than its diff:
```python
import jax
import jax.numpy as jnp
from jax import lax
from jax.experimental import pallas as pl
from jax.experimental.pallas import tpu as pltpu
from jax.sharding import PartitionSpec as P

FIN = 128
HID = 256
TILE = 128
TR = 8
CT = 2
SIDE = 8
NARROW = 4
SLOTS = 128
LIST = SLOTS + TR
BF16 = jnp.bfloat16
F32 = jnp.float32


def wide_index(z, y, core):
    return (z * SIDE + y) * 2 + core


RANGE = range(SIDE)
ALONG_Y = [[[wide_index(z, y, c) for y in RANGE] for z in RANGE] for c in (0, 1)]
ALONG_Z = [[[wide_index(z, y, c) for z in RANGE] for y in RANGE] for c in (0, 1)]
FIRST = ALONG_Y[0] + ALONG_Z[1]
SECOND = ALONG_Z[0] + ALONG_Y[1]
GROUPS_Y = ALONG_Y[0] + ALONG_Y[1]
GROUPS_Z = ALONG_Z[0] + ALONG_Z[1]
COLUMN = [
    [wide_index(z, y, c) * NARROW + x for c in (0, 1) for x in range(NARROW)] for z in RANGE for y in RANGE
]
OTHER_CORE = [(i, i ^ 1) for i in range(2 * SIDE * SIDE)]


def to_all(block, axes, groups):
    return lax.all_to_all(jnp.broadcast_to(block[None], (8, *block.shape)), axes, 0, 0, axis_index_groups=groups)


def slot_list(code, core):
    source = code // 16
    valid = (code >= 0) & (source % 2 == core)
    row = code % 8
    z, y = source // 16, (source // 2) % 8
    held = jnp.where(core == 0, z * 8 + y, y * 8 + z) * 2 + (code // 8) % 2
    slot = jnp.arange(SLOTS, dtype=jnp.int32)
    rows = jnp.arange(TR, dtype=jnp.int32)
    same = (row[:, None] == row[None, :]) & valid[None, :] & (slot[None, :] < slot[:, None])
    rank = jnp.sum(same.astype(jnp.int32), axis=1)
    in_row = jnp.sum(((row[None, :] == rows[:, None]) & valid[None, :]).astype(jnp.int32), axis=1)
    padded = (in_row + 1) // 2 * 2
    place = rank + jnp.sum(jnp.where(rows[None, :] < row[:, None], padded[None, :], 0), axis=1)
    entry = 1 + slot + SLOTS * held + SLOTS * SLOTS * row
    at = jnp.arange(LIST, dtype=jnp.int32)
    hit = (place[None, :] == at[:, None]) & valid[None, :]
    entries = jnp.sum(jnp.where(hit, entry[None, :], 0), axis=1)
    return entries, jnp.sum(padded) // 2


def aggregate_kernel(core_ref, pairs_ref, own_list, other_list, own_values, other_values, held, out_ref, acc):
    core = core_ref[0]

    def run(which, entries, values):
        acc[...] = jnp.zeros_like(acc)

        def part(q):
            e = entries[q]
            live = (e > 0).astype(F32)
            e = jnp.maximum(e - 1, 0)
            tile = values[e & 127] * live.astype(BF16)
            return tile, held[(e >> 7) & 127], e >> 14

        def pair(q):
            a0, f0, row = part(2 * q)
            a1, f1, _ = part(2 * q + 1)
            prod = jnp.dot(
                jnp.concatenate([a0, a1], axis=1),
                jnp.concatenate([f0, f1], axis=0),
                preferred_element_type=F32,
            )
            return prod, row

        def step(i, carry):
            done = [pair(2 * i + u) for u in range(2)]
            for prod, row in done:
                acc[row] += prod
            return carry

        lax.fori_loop(0, (pairs_ref[which] + 1) // 2, step, 0)
        out_ref[jnp.where(which == 0, core, 1 - core)] = acc[...].astype(BF16)

    run(0, own_list, own_values)
    run(1, other_list, other_values)


def dense_kernel(parts, weight, bias, cotangent, hidden, grads):
    total = parts[0].astype(F32)
    for i in range(1, 8):
        total += parts[i].astype(F32)
    aggregated = total.astype(BF16)
    preact = jnp.dot(aggregated, weight[...], preferred_element_type=F32) + bias[...]
    sig = jax.nn.sigmoid(preact)
    hidden[...] = (preact * sig).astype(BF16)
    dpreact = cotangent[...].astype(F32) * (sig * (1.0 + preact * (1.0 - sig)))
    weight_part = lax.dot_general(
        aggregated, dpreact.astype(BF16), (((0,), (0,)), ((), ())), preferred_element_type=F32
    )
    bias_part = jnp.broadcast_to(jnp.sum(dpreact, axis=0, keepdims=True), (8, HID))
    for i in range(8):
        grads[i, 0:16, :] = weight_part[16 * i : 16 * i + 16]
        grads[i, 16:24, :] = bias_part


VMEM = pl.BlockSpec(memory_space=pltpu.VMEM)
SMEM = pl.BlockSpec(memory_space=pltpu.SMEM)


def local(features, weight, bias, cotangent, tile_values, tile_row, tile_source, tile_count, pick):
    core = lax.rem(lax.axis_index("wide"), 2)
    both = ("wide", "narrow")
    mine = lax.dynamic_slice_in_dim(features, lax.axis_index("narrow") * (CT * TILE), CT * TILE, 0)
    first = to_all(mine, "wide", FIRST).reshape(SIDE * CT * TILE, FIN)
    held = lax.all_gather(first, "wide", axis=0, tiled=True, axis_index_groups=SECOND)
    held = held.reshape(SLOTS, TILE, FIN)

    own_values = tile_values[0, 0]
    other_values = lax.ppermute(own_values, "wide", OTHER_CORE)
    source = tile_source[0, 0]
    which = source[:, None] == jnp.arange(SLOTS, dtype=jnp.int32)[None, :]
    picked = jnp.sum(jnp.where(which, pick[0, 0][None, :], 0), axis=1)
    live = jnp.arange(SLOTS, dtype=jnp.int32) < tile_count[0, 0]
    code = jnp.where(live, tile_row[0, 0] + 8 * picked + 16 * source, -1)
    other_code = lax.ppermute(code, "wide", OTHER_CORE)
    own_list, own_pairs = slot_list(code, core)
    other_list, other_pairs = slot_list(other_code, core)

    partial = pl.pallas_call(
        aggregate_kernel,
        out_shape=jax.ShapeDtypeStruct((2, TR, TILE, FIN), BF16),
        in_specs=[SMEM] * 4 + [VMEM] * 3,
        out_specs=VMEM,
        scratch_shapes=[pltpu.VMEM((TR, TILE, FIN), F32)],
        compiler_params=pltpu.CompilerParams(vmem_limit_bytes=24 << 20),
        cost_estimate=pl.CostEstimate(flops=2 * SLOTS * TILE**3, bytes_accessed=12 << 20, transcendentals=0),
        name="aggregate",
    )(core.reshape(1), jnp.stack([own_pairs, other_pairs]), own_list, other_list, own_values, other_values, held)

    rows = TR * TILE // NARROW
    parts = lax.all_to_all(partial.reshape(8, rows, FIN), both, 0, 0, axis_index_groups=COLUMN)
    hidden, grads = pl.pallas_call(
        dense_kernel,
        out_shape=(
            jax.ShapeDtypeStruct((rows, HID), BF16),
            jax.ShapeDtypeStruct((8, 24, HID), F32),
        ),
        in_specs=[VMEM] * 4,
        out_specs=(VMEM, VMEM),
        compiler_params=pltpu.CompilerParams(vmem_limit_bytes=16 << 20),
        cost_estimate=pl.CostEstimate(flops=4 * rows * FIN * HID, bytes_accessed=2 << 20, transcendentals=rows * HID),
        name="dense",
    )(parts, weight, bias.reshape(1, HID), cotangent)

    share = jnp.sum(lax.all_to_all(grads, both, 0, 0, axis_index_groups=COLUMN), axis=0)
    share = jnp.sum(to_all(share, "wide", GROUPS_Y), axis=0)
    share = jnp.sum(to_all(share, "wide", GROUPS_Z), axis=0)
    grad_weight = to_all(share[:16], both, COLUMN).reshape(FIN, HID)
    return hidden, grad_weight, share[16]


def solution(mesh):
    placed = (
        P("wide", None),
        P(),
        P(),
        P(("wide", "narrow"), None),
        P("wide", "narrow", None, None, None),
        P("wide", "narrow", None),
        P("wide", "narrow", None),
        P("wide", "narrow"),
        P("wide", "narrow", None),
    )
    return jax.shard_map(
        local,
        mesh=mesh,
        in_specs=placed,
        out_specs=(P(("wide", "narrow"), None), P(), P()),
        check_vma=False,
    )
```

time: 437 us -> 161 us (0.37)
  waiting for transfers between devices: 281 us -> 29.9 us
  matrix products: 19.8 us -> 0 us
  blocking collectives: 99.3 us -> 81.2 us
  local copies, waits for them, and re-layouts: 21.3 us -> 7.27 us
  starting transfers between devices: 0.12 us -> 11 us
  Pallas kernels: 0 us -> 7.37 us
  between operations: 14.4 us -> 20 us
    psum x1 -> x0, waiting for transfers between devices: 166 us -> none  [local(): lax.psum((weight_part, bias_part), ('wide', 'narrow'))]
    psum x1 -> x0, blocking collectives: 99.3 us -> none  [local(): lax.psum((weight_part, bias_part), ('wide', 'narrow'))]
    all_to_all x0 -> x5, blocking collectives: none -> 81.2 us  [the longest x3 52.9 us: to_all(): lax.all_to_all(jnp.broadcast_to(block[None], (8, *block.shape)), axes, 0,...]
    all_gather x1, waiting for transfers between devices: 93.4 us -> 23.1 us  [local(): lax.all_gather(first, 'wide', axis=0, tiled=True, axis_index_groups=SECOND)]
    reduce_scatter x1 -> x0, waiting for transfers between devices: 21.4 us -> none  [local(): lax.psum_scatter(partial_rows, 'narrow', scatter_dimension=0, tiled=True)]
    dot_general x4 -> x0, matrix products: 19.8 us -> none  [the longest x1 9.76 us: local(): jnp.einsum('tij,tjf->tif', slot_values, needed, preferred_element_type=jn...]
    dot_general x2 -> x0, local copies, waits for them, and re-layouts: 10.2 us -> none  [the longest x1 9.27 us: local(): jnp.einsum('tij,tjf->tif', slot_values, needed, preferred_element_type=jn...]
    gather x2 -> x0, local copies, waits for them, and re-layouts: 7.99 us -> none  [local(): needed = gathered[sources * tile_span + my_picks[sources]]]
  transfers between devices with their start and end apart: 3 -> 4, of which waited for: 3 -> 3; matrix products, arithmetic and copies ran while one was open for 1% -> 2% of each run, Pallas kernels for 0% -> 0%
where the time goes in v1:
time: 161 us; the launch traced here: 160 us
  blocking collectives  81.2 us (50%)
  waiting for transfers between devices  29.9 us (19%)
  between operations  20 us (12%)
  starting transfers between devices  11 us (7%)
  Pallas kernels  7.37 us (5%)
  local copies, waits for them, and re-layouts  7.27 us (5%)
  other arithmetic  3.38 us (2%)
    all_to_all x3, blocking collectives, to_all(): lax.all_to_all(jnp.broadcast_to(block[None], (8, *block.shape)), axes, 0,...  52.9 us
    all_gather x1, waiting for transfers between devices, local(): lax.all_gather(first, 'wide', axis=0, tiled=True, axis_index_groups=SECOND)  23.1 us
    all_to_all x1, blocking collectives, local(): lax.all_to_all(partial.reshape(8, rows, FIN), both, 0, 0, axis_index_grou...  19.2 us
    all_to_all x1, blocking collectives, local(): lax.all_to_all(grads, both, 0, 0, axis_index_groups=COLUMN)  9.1 us
    all_to_all x1, starting transfers between devices, to_all(): lax.all_to_all(jnp.broadcast_to(block[None], (8, *block.shape)), axes, 0,...  6.62 us
    pallas_call x1, Pallas kernels, local(): pl.pallas_call(aggregate_kernel, out_shape=jax.ShapeDtypeStruct((2, TR, T...  6.48 us
    unnamed x13, local copies, waits for them, and re-layouts  5.94 us
    all_to_all x1, waiting for transfers between devices, to_all(): lax.all_to_all(jnp.broadcast_to(block[None], (8, *block.shape)), axes, 0,...  4.59 us
  transfers between devices with their start and end apart: 4, of which 3 were waited for; matrix products, arithmetic and copies ran while one was open for 2% of the time, Pallas kernels for 0%

profile of v1, /device:TPU:1, one launch (start us, length us, event | category | flops | bytes accessed | tf_op | source)
XLA Modules:
  0.0 160.1 jit_solution(3405916795453162407)
XLA Ops:
  7.2 0.9 copy-done
  8.1 0.1 broadcast_in_dim.72
  8.2 22.9 %all_to_all.30 = bf16[8,256,128]{2,1,0:T(8,128)(2,1)} all-to-all(bf16[8,256,128]{2,1,0:T(8,128)(2,1)S(1)} %broadcast_in_dim.72), channel_id=1, replica_groups={{0,8,16,24,32,40,48,56},{64,72,80,88,96,104,112,120},{128,136,144,152,1..., dimensions={0} | all-to-all | bytes 1048576 | tf_op jit(solution)/shard_map/all_to_all | solution.py:39
  31.1 2.3 %collective-permute-start.1 = (bf16[128,128,128]{2,1,0:T(8,128)(2,1)}, bf16[128,128,128]{2,1,0:T(8,128)(2,1)}, u32[]{:S(2)}, u32[]{:S(2)}) collective-permute-start(bf16[128,128,128]{2,1,0:T(8,128)(2,1)} %bitcast.23), channel_id=1, source_target_pairs={{0,4},{4,0},{8,12},{12,8},{16,20},{20,16},{24,28},{28,24},{32,36},... | collective-permute-start | bytes 12582920 | tf_op jit(solution)/shard_map/ppermute | solution.py:129
  34.1 0.8 select_reduce_fusion.2
  34.9 0.7 multiply_add_fusion.1
  35.6 2.1 %collective-permute-start = (s32[128]{0:T(128)S(1)}, s32[128]{0:T(128)S(1)}, u32[]{:S(2)}, u32[]{:S(2)}) collective-permute-start(s32[128]{0:T(128)S(1)} %get-tuple-element.13), channel_id=1, source_target_pairs={{0,4},{4,0},{8,12},{12,8},{16,20},{20,16},{24,28},{28,24},{32,36},... | collective-permute-start | bytes 1544 | tf_op jit(solution)/shard_map/ppermute | solution.py:135
  37.7 0.2 convert_reduce_fusion.1
  37.9 0.1 convert_reduce_fusion.3
  38.0 2.2 %collective-permute-done = s32[128]{0:T(128)S(1)} collective-permute-done((s32[128]{0:T(128)S(1)}, s32[128]{0:T(128)S(1)}, u32[]{:S(2)}, u32[]{:S(2)}) %collective-permute-start) | collective-permute-done | bytes 544 | tf_op jit(solution)/shard_map/ppermute | solution.py:135
  40.2 0.1 convert_reduce_fusion.2
  40.3 0.6 fusion.17
  46.2 0.1 select_reduce_fusion.4
  46.3 0.1 select_reduce_fusion.3
  46.4 0.2 convert_reduce_fusion
  46.5 0.1 pad_add_fusion.pairs_ref
  46.6 0.1 select_reduce_fusion.1.own_list
  46.7 0.1 select_reduce_fusion.other_list
  46.9 23.1 %all-gather.2.cloned.1.call-done = bf16[16384,128]{1,0:T(8,128)(2,1)} async-done(((bf16[2048,128]{1,0:T(8,128)(2,1)}), bf16[16384,128]{1,0:T(8,128)(2,1)}) %all-gather.2.cloned.1.call-update) | async-done | bytes 4194320 | tf_op jit(solution)/shard_map/all_gather | solution.py:125
  70.0 2.2 %copy-done.1 = bf16[1,1,128,128,128]{4,3,2,1,0:T(8,128)(2,1)S(1)} copy-done((bf16[1,1,128,128,128]{4,3,2,1,0:T(8,128)(2,1)S(1)}, bf16[1,1,128,128,128]{4,3,2,1,0:T(8,128)(2,1)}, u32[]{:S(2)}) %copy-start.1) | copy-done | bytes 4194328
  72.2 2.2 %copy-done.2 = bf16[16384,128]{1,0:T(8,128)(2,1)S(1)} copy-done((bf16[16384,128]{1,0:T(8,128)(2,1)S(1)}, bf16[16384,128]{1,0:T(8,128)(2,1)}, u32[]{:S(2)}) %copy-start.2) | copy-done | bytes 4194328
  74.4 6.5 %aggregate.1 = bf16[2,8,128,128]{3,2,1,0:T(8,128)(2,1)S(1)} custom-call(s32[1]{0:T(128)} %bitcast.core_ref, s32[2]{0:T(128)S(1)} %pad_add_fusion.pairs_ref, s32[136]{0:T(256)S(1)} %select_reduce_fusion.1.own_list, s32[136]{0:T(256)S(1)} %select_reduce_fusion.other_list, bf16[128,128,128]{2,1,0:T(8,128)(2,1)S(1)} %bitcast.24, ...), custom_call_target="tpu_custom_call" | custom-call | flops 536870912 | bytes 12582912 | tf_op jit(solution)/shard_map/aggregate/pallas_call | solution.py:139
  80.9 19.2 %all_to_all.31.parts = bf16[8,256,128]{2,1,0:T(8,128)(2,1)S(1)} all-to-all(bf16[8,256,128]{2,1,0:T(8,128)(2,1)S(1)} %bitcast.26), channel_id=1, replica_groups={{0,1,2,3,4,5,6,7},{8,9,10,11,12,13,14,15},{16,17,18,19,20,21,22,23},{24..., dimensions={0} | all-to-all | bytes 1048576 | tf_op jit(solution)/shard_map/all_to_all | solution.py:151
  100.1 0.9 dense.1
  101.0 9.1 %all_to_all.32 = f32[8,24,256]{2,1,0:T(8,128)S(1)} all-to-all(f32[8,24,256]{2,1,0:T(8,128)S(1)} %get-tuple-element.6), channel_id=1, replica_groups={{0,1,2,3,4,5,6,7},{8,9,10,11,12,13,14,15},{16,17,18,19,20,21,22,23},{24..., dimensions={0} | all-to-all | bytes 393216 | tf_op jit(solution)/shard_map/all_to_all | solution.py:165
  110.1 16.0 %all_to_all.33 = f32[8,24,256]{2,1,0:T(8,128)S(1)} all-to-all(f32[8,24,256]{2,1,0:T(8,128)S(1)} %broadcast_in_dim.120), channel_id=1, replica_groups={{0,8,16,24,32,40,48,56},{64,72,80,88,96,104,112,120},{128,136,144,152,1..., dimensions={0} | all-to-all | bytes 393216 | tf_op jit(solution)/shard_map/all_to_all | solution.py:39
  126.2 14.0 %all_to_all.34 = f32[8,24,256]{2,1,0:T(8,128)S(1)} all-to-all(f32[8,24,256]{2,1,0:T(8,128)S(1)} %broadcast_in_dim.121), channel_id=1, replica_groups={{0,64,128,192,256,320,384,448},{8,72,136,200,264,328,392,456},{16,80,14..., dimensions={0} | all-to-all | bytes 393216 | tf_op jit(solution)/shard_map/all_to_all | solution.py:39
  140.2 0.7 broadcast_in_dim.122
  140.8 6.6 %all-to-all-start.5 = ((f32[8,16,256]{2,1,0:T(8,128)}), f32[8,16,256]{2,1,0:T(8,128)S(1)}, u32[]{:S(2)}, u32[]{:S(2)}) async-start(f32[8,16,256]{2,1,0:T(8,128)} %broadcast_in_dim.122), calls=%async_computation.5 | async-start | bytes 262144 | tf_op jit(solution)/shard_map/all_to_all | solution.py:39
  147.5 0.6 slice.9
  148.0 4.6 %all-to-all-done.5 = f32[8,16,256]{2,1,0:T(8,128)S(1)} async-done(((f32[8,16,256]{2,1,0:T(8,128)}), f32[8,16,256]{2,1,0:T(8,128)S(1)}, u32[]{:S(2)}, u32[]{:S(2)}) %all-to-all-start.5) | async-done | bytes 131104 | tf_op jit(solution)/shard_map/all_to_all | solution.py:39
  152.6 0.7 copy.14
  (24 shorter events, 0.2 us)
Async XLA Ops:
  7.2 1.0 copy-start
  7.2 62.8 %all-gather.2.cloned.1.call-start = ((), (), s32[]{:S(2)}) async-start(), calls=%async_computation.6 | async-start | bytes 4718592 | tf_op jit(solution)/shard_map/all_gather | solution.py:125
  31.1 15.7 %collective-permute-start.1 = (bf16[128,128,128]{2,1,0:T(8,128)(2,1)}, bf16[128,128,128]{2,1,0:T(8,128)(2,1)}, u32[]{:S(2)}, u32[]{:S(2)}) collective-permute-start(bf16[128,128,128]{2,1,0:T(8,128)(2,1)} %bitcast.23), channel_id=1, source_target_pairs={{0,4},{4,0},{8,12},{12,8},{16,20},{20,16},{24,28},{28,24},{32,36},... | collective-permute-start | bytes 12582920 | tf_op jit(solution)/shard_map/ppermute | solution.py:129
  35.6 4.5 %collective-permute-start = (s32[128]{0:T(128)S(1)}, s32[128]{0:T(128)S(1)}, u32[]{:S(2)}, u32[]{:S(2)}) collective-permute-start(s32[128]{0:T(128)S(1)} %get-tuple-element.13), channel_id=1, source_target_pairs={{0,4},{4,0},{8,12},{12,8},{16,20},{20,16},{24,28},{28,24},{32,36},... | collective-permute-start | bytes 1544 | tf_op jit(solution)/shard_map/ppermute | solution.py:135
  70.0 2.2 %copy-start.1 = (bf16[1,1,128,128,128]{4,3,2,1,0:T(8,128)(2,1)S(1)}, bf16[1,1,128,128,128]{4,3,2,1,0:T(8,128)(2,1)}, u32[]{:S(2)}) copy-start(bf16[1,1,128,128,128]{4,3,2,1,0:T(8,128)(2,1)} %param.13) | copy-start | bytes 12582916
  72.2 2.2 %copy-start.2 = (bf16[16384,128]{1,0:T(8,128)(2,1)S(1)}, bf16[16384,128]{1,0:T(8,128)(2,1)}, u32[]{:S(2)}) copy-start(bf16[16384,128]{1,0:T(8,128)(2,1)} %all-gather.2.cloned.1.call-done) | copy-start | bytes 12582916
  74.4 25.7 %copy-start.3 = (bf16[256,256]{1,0:T(8,128)(2,1)S(1)}, bf16[256,256]{1,0:T(8,128)(2,1)}, u32[]{:S(2)}) copy-start(bf16[256,256]{1,0:T(8,128)(2,1)} %cotangent.1) | copy-start | bytes 393220
  74.4 25.7 %copy-start.4 = (bf16[128,256]{1,0:T(8,128)(2,1)S(1)}, bf16[128,256]{1,0:T(8,128)(2,1)}, u32[]{:S(2)}) copy-start(bf16[128,256]{1,0:T(8,128)(2,1)} %weight.1) | copy-start | bytes 196612
  74.4 25.7 %copy-start.5 = (f32[256]{0:T(256)S(1)}, f32[256]{0:T(256)}, u32[]{:S(2)}) copy-start(f32[256]{0:T(256)} %param.11) | copy-start | bytes 3076
  140.8 11.8 %all-to-all-start.5 = ((f32[8,16,256]{2,1,0:T(8,128)}), f32[8,16,256]{2,1,0:T(8,128)S(1)}, u32[]{:S(2)}, u32[]{:S(2)}) async-start(f32[8,16,256]{2,1,0:T(8,128)} %broadcast_in_dim.122), calls=%async_computation.5 | async-start | bytes 262144 | tf_op jit(solution)/shard_map/all_to_all | solution.py:39
Sparse Core Ops, SparseCore 0:
  31.3 38.6 all-gather.1

commit v2 on v1

v2 whole, which is shorter than its diff:
```python
import jax
import jax.numpy as jnp
from jax import lax
from jax.experimental import pallas as pl
from jax.experimental.pallas import tpu as pltpu
from jax.sharding import PartitionSpec as P

FIN = 128
HID = 256
TILE = 128
TR = 8
CT = 2
SIDE = 8
NARROW = 4
SLOTS = 128
BLOCK = SIDE * CT
STEP = 4
SEGMENTS = 9
LIST = 256
SPARE = TR
BF16 = jnp.bfloat16
F32 = jnp.float32
I32 = jnp.int32


def wide_index(z, y, core):
    return (z * SIDE + y) * 2 + core


RANGE = range(SIDE)
ALONG_Y = [[[wide_index(z, y, c) for y in RANGE] for z in RANGE] for c in (0, 1)]
ALONG_Z = [[[wide_index(z, y, c) for z in RANGE] for y in RANGE] for c in (0, 1)]
FIRST = ALONG_Y[0] + ALONG_Z[1]
SECOND = ALONG_Z[0] + ALONG_Y[1]
GROUPS_Y = ALONG_Y[0] + ALONG_Y[1]
GROUPS_Z = ALONG_Z[0] + ALONG_Z[1]
COLUMN = [
    [wide_index(z, y, c) * NARROW + x for c in (0, 1) for x in range(NARROW)] for z in RANGE for y in RANGE
]
OTHER_CORE = [(i, i ^ 1) for i in range(2 * SIDE * SIDE)]


def to_all(block, axes, groups):
    return lax.all_to_all(jnp.broadcast_to(block[None], (8, *block.shape)), axes, 0, 0, axis_index_groups=groups)


def shift(block, by):
    pairs = [(ring[i], ring[(i + by) % SIDE]) for ring in SECOND for i in RANGE]
    return lax.ppermute(block, "wide", pairs)


def column(vector):
    n = vector.shape[1]
    eye = lax.broadcasted_iota(I32, (n, n), 0) == lax.broadcasted_iota(I32, (n, n), 1)
    return jnp.sum(jnp.where(eye, vector, 0), axis=1, keepdims=True)


def list_kernel(place_ref, code_ref, list_ref, start_ref):
    core, at = place_ref[0], place_ref[1]
    starts = []
    for owner in range(2):
        code = code_ref[owner : owner + 1, :]
        source = lax.shift_right_arithmetic(code, 4)
        valid = (code >= 0) & ((source & 1) == core)
        z, y = lax.shift_right_arithmetic(source, 4), lax.shift_right_arithmetic(source, 1) & 7
        along, across = jnp.where(core == 0, z, y), jnp.where(core == 0, y, z)
        tile = across * 2 + (lax.shift_right_arithmetic(code, 3) & 1)
        ahead = (along - at) & 7
        behind = 8 - ahead
        segment = jnp.where(ahead < 4, 2 * ahead, 2 * behind - 1)
        segment = jnp.where(ahead == 0, 0, segment)
        segment = jnp.where(ahead == 4, jnp.where(tile < SIDE, 7, 8), segment)
        segment = jnp.where(valid, segment, SEGMENTS)
        entry = lax.broadcasted_iota(I32, (1, SLOTS), 1) + SLOTS * tile + SLOTS * BLOCK * (code & 7)
        segments = column(segment)
        kinds = lax.broadcasted_iota(I32, (SLOTS, SLOTS), 1)
        member = (segments == kinds).astype(I32)
        sizes = jnp.sum(member, axis=0, keepdims=True)
        sizes = lax.shift_right_arithmetic(sizes + STEP - 1, 2) * STEP
        sizes = jnp.where(lax.broadcasted_iota(I32, (1, SLOTS), 1) < SEGMENTS, sizes, 0)
        size = column(sizes)
        rows = lax.broadcasted_iota(I32, (SLOTS, SLOTS), 0)
        start = jnp.sum(jnp.where(rows < kinds, size, 0), axis=0, keepdims=True)
        earlier = (segments == segment) & (rows < kinds)
        place = jnp.sum(earlier.astype(I32), axis=0, keepdims=True)
        place += jnp.sum(jnp.where(rows == segment, column(start), 0), axis=0, keepdims=True)
        place = jnp.where(valid, place, LIST)
        spare = SLOTS * BLOCK * SPARE
        places, entries = column(place), column(entry)
        slots = lax.broadcasted_iota(I32, (SLOTS, LIST), 1)
        hit = places == slots
        list_ref[owner : owner + 1, :] = spare + jnp.sum(jnp.where(hit, entries - spare, 0), axis=0, keepdims=True)
        starts.append(lax.shift_right_arithmetic(start, 2))
    for owner in range(2):
        start_ref[owner : owner + 1, :] = starts[owner]


def add_products(lists, starts, values, blocks, first, acc):
    for owner in range(2):
        for i, (block, offset) in enumerate(blocks):
            segment = first + i

            def step(k, carry, owner=owner, block=block, offset=offset):
                done = []
                for u in range(STEP):
                    e = lists[owner, k * STEP + u]
                    tile, row = (e >> 7) & (BLOCK - 1), e >> 11
                    product = jnp.dot(
                        values[owner][e & (SLOTS - 1)],
                        block[jnp.maximum(tile - offset, 0)],
                        preferred_element_type=F32,
                    )
                    done.append((row, product))
                for row, product in done:
                    acc[owner, row] += product
                return carry

            lax.fori_loop(starts[owner, segment], starts[owner, segment + 1], step, 0)


def early_kernel(lists, starts, own, other, b0, b1, b2, b3, b4, acc):
    acc[...] = jnp.zeros_like(acc)
    blocks = [(b0, 0), (b1, 0), (b2, 0), (b3, 0), (b4, 0)]
    add_products(lists, starts, (own, other), blocks, 0, acc)


def late_kernel(place, lists, starts, own, other, b5, b6, b7, b8, before, out, acc):
    acc[...] = before[...]
    blocks = [(b5, 0), (b6, 0), (b7, 0), (b8, SIDE)]
    add_products(lists, starts, (own, other), blocks, 5, acc)
    core = place[0]
    out[core] = acc[0, 0:TR].astype(BF16)
    out[1 - core] = acc[1, 0:TR].astype(BF16)


def dense_kernel(parts, weight, bias, cotangent, hidden, grads):
    total = parts[0].astype(F32)
    for i in range(1, 8):
        total += parts[i].astype(F32)
    aggregated = total.astype(BF16)
    preact = jnp.dot(aggregated, weight[...], preferred_element_type=F32) + bias[...]
    sig = jax.nn.sigmoid(preact)
    hidden[...] = (preact * sig).astype(BF16)
    dpreact = cotangent[...].astype(F32) * (sig * (1.0 + preact * (1.0 - sig)))
    weight_part = lax.dot_general(
        aggregated, dpreact.astype(BF16), (((0,), (0,)), ((), ())), preferred_element_type=F32
    ).astype(BF16)
    bias_part = jnp.sum(dpreact, axis=0, keepdims=True)
    rows = lax.broadcasted_iota(I32, (16, TILE), 0)
    left = jnp.broadcast_to(bias_part[:, :TILE], (16, TILE))
    right = jnp.broadcast_to(bias_part[:, TILE:], (16, TILE))
    biases = jnp.where(rows == 0, left, jnp.where(rows == 1, right, 0.0)).astype(BF16)
    for i in range(8):
        grads[i, 0:16, :] = weight_part[16 * i : 16 * i + 16, :TILE]
        grads[i, 16:32, :] = weight_part[16 * i : 16 * i + 16, TILE:]
        grads[i, 32:48, :] = biases


VMEM = pl.BlockSpec(memory_space=pltpu.VMEM)
SMEM = pl.BlockSpec(memory_space=pltpu.SMEM)


def total(shares):
    return jnp.sum(shares.astype(F32), axis=0)


def local(features, weight, bias, cotangent, tile_values, tile_row, tile_source, tile_count, pick):
    index = lax.axis_index("wide")
    core = lax.rem(index, 2)
    both = ("wide", "narrow")
    mine = lax.dynamic_slice_in_dim(features, lax.axis_index("narrow") * (CT * TILE), CT * TILE, 0)
    own = to_all(mine, "wide", FIRST).reshape(BLOCK, TILE, FIN)
    up2, down2 = shift(own, 2), shift(own, -2)
    up1, down1 = shift(own, 1), shift(own, -1)
    up3, down3 = shift(up2, 1), shift(down2, -1)
    up4, down4 = shift(up2[:SIDE], 2), shift(down2[SIDE:], -2)

    own_values = tile_values[0, 0]
    other_values = lax.ppermute(own_values, "wide", OTHER_CORE)
    source = tile_source[0, 0]
    which = source[:, None] == jnp.arange(SLOTS, dtype=I32)[None, :]
    picked = jnp.sum(jnp.where(which, pick[0, 0][None, :], 0), axis=1)
    live = jnp.arange(SLOTS, dtype=I32) < tile_count[0, 0]
    code = jnp.where(live, tile_row[0, 0] + 8 * picked + 16 * source, -1)[None]
    codes = jnp.concatenate([code, lax.ppermute(code, "wide", OTHER_CORE)], axis=0)
    place = jnp.stack([core, jnp.where(core == 0, index // 16, lax.rem(index // 2, 8))])
    lists, starts = pl.pallas_call(
        list_kernel,
        out_shape=(jax.ShapeDtypeStruct((2, LIST), I32), jax.ShapeDtypeStruct((2, SLOTS), I32)),
        in_specs=[SMEM, VMEM],
        out_specs=(VMEM, VMEM),
        compiler_params=pltpu.CompilerParams(vmem_limit_bytes=8 << 20),
        name="lists",
    )(place, codes)

    sums = jax.ShapeDtypeStruct((2, TR + 1, TILE, FIN), F32)
    partial = pl.pallas_call(
        early_kernel,
        out_shape=sums,
        in_specs=[SMEM] * 2 + [VMEM] * 7,
        out_specs=VMEM,
        compiler_params=pltpu.CompilerParams(vmem_limit_bytes=16 << 20),
        cost_estimate=pl.CostEstimate(flops=SLOTS * TILE**3, bytes_accessed=8 << 20, transcendentals=0),
        name="early",
    )(lists, starts, own_values, other_values, own, up1, down1, up2, down2)
    partial = pl.pallas_call(
        late_kernel,
        out_shape=jax.ShapeDtypeStruct((2, TR, TILE, FIN), BF16),
        in_specs=[SMEM] * 3 + [VMEM] * 7,
        out_specs=VMEM,
        scratch_shapes=[pltpu.VMEM(sums.shape, F32)],
        compiler_params=pltpu.CompilerParams(vmem_limit_bytes=16 << 20),
        cost_estimate=pl.CostEstimate(flops=SLOTS * TILE**3, bytes_accessed=8 << 20, transcendentals=0),
        name="late",
    )(place, lists, starts, own_values, other_values, up3, down3, up4, down4, partial)

    rows = TR * TILE // NARROW
    parts = lax.all_to_all(partial.reshape(8, rows, FIN), both, 0, 0, axis_index_groups=COLUMN)
    hidden, grads = pl.pallas_call(
        dense_kernel,
        out_shape=(
            jax.ShapeDtypeStruct((rows, HID), BF16),
            jax.ShapeDtypeStruct((8, 48, TILE), BF16),
        ),
        in_specs=[VMEM] * 4,
        out_specs=(VMEM, VMEM),
        compiler_params=pltpu.CompilerParams(vmem_limit_bytes=16 << 20),
        cost_estimate=pl.CostEstimate(flops=4 * rows * FIN * HID, bytes_accessed=2 << 20, transcendentals=rows * HID),
        name="dense",
    )(parts, weight, bias.reshape(1, HID), cotangent)

    share = total(lax.all_to_all(grads, both, 0, 0, axis_index_groups=COLUMN)).astype(BF16)
    share = total(to_all(share, "wide", GROUPS_Y)).astype(BF16)
    share = total(to_all(share, "wide", GROUPS_Z))
    chunk = jnp.concatenate([share[0:16], share[16:32]], axis=1)
    grad_weight = to_all(chunk, both, COLUMN).reshape(FIN, HID)
    return hidden, grad_weight, share[32:34].reshape(HID)


def solution(mesh):
    placed = (
        P("wide", None),
        P(),
        P(),
        P(("wide", "narrow"), None),
        P("wide", "narrow", None, None, None),
        P("wide", "narrow", None),
        P("wide", "narrow", None),
        P("wide", "narrow"),
        P("wide", "narrow", None),
    )
    return jax.shard_map(
        local,
        mesh=mesh,
        in_specs=placed,
        out_specs=(P(("wide", "narrow"), None), P(), P()),
        check_vma=False,
    )
```

time: 161 us -> 140 us (0.87)
  starting transfers between devices: 11 us -> 49 us
  waiting for transfers between devices: 29.9 us -> 4.62 us
  blocking collectives: 81.2 us -> 62.1 us
  between operations: 20 us -> 1.63 us
  Pallas kernels: 7.37 us -> 12.4 us
  other arithmetic: 3.38 us -> 1.67 us
    ppermute x1 -> x9, starting transfers between devices: 2.07 us -> 33.3 us  [the longest x8 28.1 us: shift(): return lax.ppermute(block, 'wide', pairs)]
    all_gather x1 -> x0, waiting for transfers between devices: 23.1 us -> none  [local(): lax.all_gather(first, 'wide', axis=0, tiled=True, axis_index_groups=SECOND)]
    all_to_all x3, blocking collectives: 52.9 us -> 38.2 us  [to_all(): lax.all_to_all(jnp.broadcast_to(block[None], (8, *block.shape)), axes, 0,...]
    ppermute x1, starting transfers between devices: 2.26 us -> 8.92 us  [local(): other_values = lax.ppermute(own_values, 'wide', OTHER_CORE)]
    pallas_call x1 -> x3, Pallas kernels: 6.48 us -> 11.5 us  [the longest x1 5.66 us: local(): pl.pallas_call(early_kernel, out_shape=sums, in_specs=[SMEM] * 2 + [VMEM]...]
    all_to_all x1, blocking collectives: 19.2 us -> 15.7 us  [local(): lax.all_to_all(partial.reshape(8, rows, FIN), both, 0, 0, axis_index_grou...]
    ppermute x1 -> x9, waiting for transfers between devices: 2.15 us -> 0.02 us  [the longest x8 0.02 us: shift(): return lax.ppermute(block, 'wide', pairs)]
    reduce_sum x12 -> x3, other arithmetic: 1.67 us -> 0.06 us  [total(): return jnp.sum(shares.astype(F32), axis=0)]
  transfers between devices with their start and end apart: 4 -> 11, of which waited for: 3 -> 1; matrix products, arithmetic and copies ran while one was open for 2% -> 3% of each run, Pallas kernels for 0% -> 5%
where the time goes in v2:
time: 140 us; the launch traced here: 139 us
  blocking collectives  62.1 us (44%)
  starting transfers between devices  49 us (35%)
  Pallas kernels  12.4 us (9%)
  local copies, waits for them, and re-layouts  7.49 us (5%)
  waiting for transfers between devices  4.62 us (3%)
  other arithmetic  1.67 us (1%)
  between operations  1.63 us (1%)
    all_to_all x3, blocking collectives, to_all(): lax.all_to_all(jnp.broadcast_to(block[None], (8, *block.shape)), axes, 0,...  38.2 us
    ppermute x8, starting transfers between devices, shift(): return lax.ppermute(block, 'wide', pairs)  28.1 us
    all_to_all x1, blocking collectives, local(): lax.all_to_all(partial.reshape(8, rows, FIN), both, 0, 0, axis_index_grou...  15.7 us
    ppermute x1, starting transfers between devices, local(): other_values = lax.ppermute(own_values, 'wide', OTHER_CORE)  8.92 us
    all_to_all x1, blocking collectives, local(): lax.all_to_all(grads, both, 0, 0, axis_index_groups=COLUMN)  8.22 us
    all_to_all x1, starting transfers between devices, to_all(): lax.all_to_all(jnp.broadcast_to(block[None], (8, *block.shape)), axes, 0,...  6.71 us
    pallas_call x1, Pallas kernels, local(): pl.pallas_call(early_kernel, out_shape=sums, in_specs=[SMEM] * 2 + [VMEM]...  5.66 us
    ppermute x1, starting transfers between devices, local(): lax.ppermute(code, 'wide', OTHER_CORE)  5.18 us
  transfers between devices with their start and end apart: 11, of which 1 were waited for; matrix products, arithmetic and copies ran while one was open for 3% of the time, Pallas kernels for 5%

profile of v2, /device:TPU:1, one launch (start us, length us, event | category | flops | bytes accessed | tf_op | source)
XLA Modules:
  0.0 138.9 jit_solution(8532542235122956844)
XLA Ops:
  0.6 8.9 %collective-permute-start.1 = (bf16[128,128,128]{2,1,0:T(8,128)(2,1)}, bf16[128,128,128]{2,1,0:T(8,128)(2,1)}, u32[]{:S(2)}, u32[]{:S(2)}) collective-permute-start(bf16[128,128,128]{2,1,0:T(8,128)(2,1)} %bitcast.23), channel_id=1, source_target_pairs={{0,4},{4,0},{8,12},{12,8},{16,20},{20,16},{24,28},{28,24},{32,36},... | collective-permute-start | bytes 12582920 | tf_op jit(solution)/shard_map/ppermute | solution.py:179
  9.7 16.6 %all_to_all.30 = bf16[8,256,128]{2,1,0:T(8,128)(2,1)S(1)} all-to-all(bf16[8,256,128]{2,1,0:T(8,128)(2,1)S(1)} %broadcast_in_dim.48), channel_id=1, replica_groups={{0,8,16,24,32,40,48,56},{64,72,80,88,96,104,112,120},{128,136,144,152,1..., dimensions={0} | all-to-all | bytes 1048576 | tf_op jit(solution)/shard_map/all_to_all | solution.py:44
  26.3 4.2 %collective-permute-start.2 = (bf16[16,128,128]{2,1,0:T(8,128)(2,1)S(1)}, bf16[16,128,128]{2,1,0:T(8,128)(2,1)S(1)}, u32[]{:S(2)}, u32[]{:S(2)}) collective-permute-start(bf16[16,128,128]{2,1,0:T(8,128)(2,1)S(1)} %bitcast.26), channel_id=1, source_target_pairs={{0,128},{64,192},{128,256},{192,320},{256,384},{320,448},{384,0},{... | collective-permute-start | bytes 1572872 | tf_op jit(solution)/shard_map/ppermute | solution.py:49
  30.5 3.6 %collective-permute-start.4 = (bf16[16,128,128]{2,1,0:T(8,128)(2,1)S(1)}, bf16[16,128,128]{2,1,0:T(8,128)(2,1)S(1)}, u32[]{:S(2)}, u32[]{:S(2)}) collective-permute-start(bf16[16,128,128]{2,1,0:T(8,128)(2,1)S(1)} %bitcast.27), channel_id=1, source_target_pairs={{0,384},{64,448},{128,0},{192,64},{256,128},{320,192},{384,256},{4... | collective-permute-start | bytes 1572872 | tf_op jit(solution)/shard_map/ppermute | solution.py:49
  34.1 0.8 select_reduce_fusion
  35.6 0.7 compare_select_fusion
  36.3 5.2 %collective-permute-start = (s32[1,128]{1,0:T(1,128)S(1)}, s32[1,128]{1,0:T(1,128)S(1)}, u32[]{:S(2)}, u32[]{:S(2)}) collective-permute-start(s32[1,128]{1,0:T(1,128)S(1)} %compare_select_fusion), channel_id=1, source_target_pairs={{0,4},{4,0},{8,12},{12,8},{16,20},{20,16},{24,28},{28,24},{32,36},... | collective-permute-start | bytes 1544 | tf_op jit(solution)/shard_map/ppermute | solution.py:185
  41.5 2.2 %collective-permute-start.8 = (bf16[16,128,128]{2,1,0:T(8,128)(2,1)S(1)}, bf16[16,128,128]{2,1,0:T(8,128)(2,1)S(1)}, u32[]{:S(2)}, u32[]{:S(2)}) collective-permute-start(bf16[16,128,128]{2,1,0:T(8,128)(2,1)S(1)} %bitcast.28), channel_id=1, source_target_pairs={{0,64},{64,128},{128,192},{192,256},{256,320},{320,384},{384,448},... | collective-permute-start | bytes 1572872 | tf_op jit(solution)/shard_map/ppermute | solution.py:49
  43.7 4.3 %collective-permute-start.9 = (bf16[16,128,128]{2,1,0:T(8,128)(2,1)S(1)}, bf16[16,128,128]{2,1,0:T(8,128)(2,1)S(1)}, u32[]{:S(2)}, u32[]{:S(2)}) collective-permute-start(bf16[16,128,128]{2,1,0:T(8,128)(2,1)S(1)} %bitcast.29), channel_id=1, source_target_pairs={{0,448},{64,0},{128,64},{192,128},{256,192},{320,256},{384,320},{4... | collective-permute-start | bytes 1572872 | tf_op jit(solution)/shard_map/ppermute | solution.py:49
  48.0 1.9 %collective-permute-start.3 = (bf16[16,128,128]{2,1,0:T(8,128)(2,1)S(1)}, bf16[16,128,128]{2,1,0:T(8,128)(2,1)S(1)}, u32[]{:S(2)}, u32[]{:S(2)}) collective-permute-start(bf16[16,128,128]{2,1,0:T(8,128)(2,1)S(1)} %collective-permute-done.2.b3), channel_id=1, source_target_pairs={{0,64},{64,128},{128,192},{192,256},{256,320},{320,384},{384,448},... | collective-permute-start | bytes 1572872 | tf_op jit(solution)/shard_map/ppermute | solution.py:49
  49.9 4.6 %collective-permute-start.5 = (bf16[16,128,128]{2,1,0:T(8,128)(2,1)S(1)}, bf16[16,128,128]{2,1,0:T(8,128)(2,1)S(1)}, u32[]{:S(2)}, u32[]{:S(2)}) collective-permute-start(bf16[16,128,128]{2,1,0:T(8,128)(2,1)S(1)} %collective-permute-done.4.b4), channel_id=1, source_target_pairs={{0,448},{64,0},{128,64},{192,128},{256,192},{320,256},{384,320},{4... | collective-permute-start | bytes 1572872 | tf_op jit(solution)/shard_map/ppermute | solution.py:49
  54.5 0.7 slice.20
  55.2 0.7 slice.21
  56.0 1.9 %collective-permute-start.6 = (bf16[8,128,128]{2,1,0:T(8,128)(2,1)}, bf16[8,128,128]{2,1,0:T(8,128)(2,1)}, u32[]{:S(2)}, u32[]{:S(2)}) collective-permute-start(bf16[8,128,128]{2,1,0:T(8,128)(2,1)} %slice.20), channel_id=1, source_target_pairs={{0,128},{64,192},{128,256},{192,320},{256,384},{320,448},{384,0},{... | collective-permute-start | bytes 786440 | tf_op jit(solution)/shard_map/ppermute | solution.py:49
  57.9 0.8 copy-done.3
  58.7 5.5 %collective-permute-start.7 = (bf16[8,128,128]{2,1,0:T(8,128)(2,1)}, bf16[8,128,128]{2,1,0:T(8,128)(2,1)}, u32[]{:S(2)}, u32[]{:S(2)}) collective-permute-start(bf16[8,128,128]{2,1,0:T(8,128)(2,1)} %slice.21), channel_id=1, source_target_pairs={{0,384},{64,448},{128,0},{192,64},{256,128},{320,192},{384,256},{4... | collective-permute-start | bytes 786440 | tf_op jit(solution)/shard_map/ppermute | solution.py:49
  64.2 0.1 pad_add_fusion.1.place_ref.place
  64.3 1.1 lists.1
  65.4 2.2 %copy-done.1 = bf16[1,1,128,128,128]{4,3,2,1,0:T(8,128)(2,1)S(1)} copy-done((bf16[1,1,128,128,128]{4,3,2,1,0:T(8,128)(2,1)S(1)}, bf16[1,1,128,128,128]{4,3,2,1,0:T(8,128)(2,1)}, u32[]{:S(2)}) %copy-start.1) | copy-done | bytes 4194328
  67.6 1.0 copy-done.4
  68.6 5.7 %early.1.before = f32[2,9,128,128]{3,2,1,0:T(8,128)S(1)} custom-call(s32[2,256]{1,0:T(2,128)S(1)} %get-tuple-element.7.lists, s32[2,128]{1,0:T(2,128)S(1)} %get-tuple-element.8.starts, bf16[128,128,128]{2,1,0:T(8,128)(2,1)S(1)} %bitcast.24, bf16[128,128,128]{2,1,0:T(8,128)(2,1)} %collective-permute-done.1.other, bf16[16,128,128]{2,1,0:T(8,128)(2,1)S(1)} %bitcast.30, ...), custom_call_target="tpu_custom_call" | custom-call | flops 268435456 | bytes 8388608 | tf_op jit(solution)/shard_map/early/pallas_call | solution.py:197
  74.4 4.8 %late.1 = bf16[2,8,128,128]{3,2,1,0:T(8,128)(2,1)S(1)} custom-call(s32[2]{0:T(128)S(1)} %pad_add_fusion.1.place_ref.place, s32[2,256]{1,0:T(2,128)S(1)} %get-tuple-element.7.lists, s32[2,128]{1,0:T(2,128)S(1)} %get-tuple-element.8.starts, bf16[128,128,128]{2,1,0:T(8,128)(2,1)S(1)} %bitcast.25, bf16[128,128,128]{2,1,0:T(8,128)(2,1)} %collective-permute-done.1.other, ...), custom_call_target="tpu_custom_call" | custom-call | flops 268435456 | bytes 8388608 | tf_op jit(solution)/shard_map/late/pallas_call | solution.py:206
  79.1 15.7 %all_to_all.31.parts = bf16[8,256,128]{2,1,0:T(8,128)(2,1)S(1)} all-to-all(bf16[8,256,128]{2,1,0:T(8,128)(2,1)S(1)} %bitcast.31), channel_id=1, replica_groups={{0,1,2,3,4,5,6,7},{8,9,10,11,12,13,14,15},{16,17,18,19,20,21,22,23},{24..., dimensions={0} | all-to-all | bytes 1048576 | tf_op jit(solution)/shard_map/all_to_all | solution.py:218
  94.9 0.9 dense.1
  95.8 8.2 %all_to_all.32 = bf16[8,48,128]{2,1,0:T(8,128)(2,1)S(1)} all-to-all(bf16[8,48,128]{2,1,0:T(8,128)(2,1)S(1)} %get-tuple-element.10), channel_id=1, replica_groups={{0,1,2,3,4,5,6,7},{8,9,10,11,12,13,14,15},{16,17,18,19,20,21,22,23},{24..., dimensions={0} | all-to-all | bytes 196608 | tf_op jit(solution)/shard_map/all_to_all | solution.py:232
  104.0 10.3 %all_to_all.33 = bf16[8,48,128]{2,1,0:T(8,128)(2,1)S(1)} all-to-all(bf16[8,48,128]{2,1,0:T(8,128)(2,1)S(1)} %broadcast_in_dim.49), channel_id=1, replica_groups={{0,8,16,24,32,40,48,56},{64,72,80,88,96,104,112,120},{128,136,144,152,1..., dimensions={0} | all-to-all | bytes 196608 | tf_op jit(solution)/shard_map/all_to_all | solution.py:44
  114.4 11.3 %all_to_all.34 = bf16[8,48,128]{2,1,0:T(8,128)(2,1)S(1)} all-to-all(bf16[8,48,128]{2,1,0:T(8,128)(2,1)S(1)} %broadcast_in_dim.50), channel_id=1, replica_groups={{0,64,128,192,256,320,384,448},{8,72,136,200,264,328,392,456},{16,80,14..., dimensions={0} | all-to-all | bytes 196608 | tf_op jit(solution)/shard_map/all_to_all | solution.py:44
  125.7 0.7 broadcast_in_dim.51
  126.4 6.7 %all-to-all-start.5 = ((f32[8,16,256]{2,1,0:T(8,128)}), f32[8,16,256]{2,1,0:T(8,128)S(1)}, u32[]{:S(2)}, u32[]{:S(2)}) async-start(f32[8,16,256]{2,1,0:T(8,128)} %broadcast_in_dim.51), calls=%async_computation.5 | async-start | bytes 262144 | tf_op jit(solution)/shard_map/all_to_all | solution.py:44
  133.1 0.6 slice_bitcast_fusion
  133.7 4.6 %all-to-all-done.5 = f32[8,16,256]{2,1,0:T(8,128)S(1)} async-done(((f32[8,16,256]{2,1,0:T(8,128)}), f32[8,16,256]{2,1,0:T(8,128)S(1)}, u32[]{:S(2)}, u32[]{:S(2)}) %all-to-all-start.5) | async-done | bytes 131104 | tf_op jit(solution)/shard_map/all_to_all | solution.py:44
  138.3 0.7 copy.14
  (33 shorter events, 0.3 us)
Async XLA Ops:
  0.6 9.0 %copy-start = (bf16[1024,128]{1,0:T(8,128)(2,1)S(1)}, bf16[1024,128]{1,0:T(8,128)(2,1)}, u32[]{:S(2)}) copy-start(bf16[1024,128]{1,0:T(8,128)(2,1)} %param.9) | copy-start | bytes 786436
  0.6 64.7 %collective-permute-start.1 = (bf16[128,128,128]{2,1,0:T(8,128)(2,1)}, bf16[128,128,128]{2,1,0:T(8,128)(2,1)}, u32[]{:S(2)}, u32[]{:S(2)}) collective-permute-start(bf16[128,128,128]{2,1,0:T(8,128)(2,1)} %bitcast.23), channel_id=1, source_target_pairs={{0,4},{4,0},{8,12},{12,8},{16,20},{20,16},{24,28},{28,24},{32,36},... | collective-permute-start | bytes 12582920 | tf_op jit(solution)/shard_map/ppermute | solution.py:179
  26.3 21.7 %collective-permute-start.2 = (bf16[16,128,128]{2,1,0:T(8,128)(2,1)S(1)}, bf16[16,128,128]{2,1,0:T(8,128)(2,1)S(1)}, u32[]{:S(2)}, u32[]{:S(2)}) collective-permute-start(bf16[16,128,128]{2,1,0:T(8,128)(2,1)S(1)} %bitcast.26), channel_id=1, source_target_pairs={{0,128},{64,192},{128,256},{192,320},{256,384},{320,448},{384,0},{... | collective-permute-start | bytes 1572872 | tf_op jit(solution)/shard_map/ppermute | solution.py:49
  30.5 19.4 %collective-permute-start.4 = (bf16[16,128,128]{2,1,0:T(8,128)(2,1)S(1)}, bf16[16,128,128]{2,1,0:T(8,128)(2,1)S(1)}, u32[]{:S(2)}, u32[]{:S(2)}) collective-permute-start(bf16[16,128,128]{2,1,0:T(8,128)(2,1)S(1)} %bitcast.27), channel_id=1, source_target_pairs={{0,384},{64,448},{128,0},{192,64},{256,128},{320,192},{384,256},{4... | collective-permute-start | bytes 1572872 | tf_op jit(solution)/shard_map/ppermute | solution.py:49
  36.3 7.4 %collective-permute-start = (s32[1,128]{1,0:T(1,128)S(1)}, s32[1,128]{1,0:T(1,128)S(1)}, u32[]{:S(2)}, u32[]{:S(2)}) collective-permute-start(s32[1,128]{1,0:T(1,128)S(1)} %compare_select_fusion), channel_id=1, source_target_pairs={{0,4},{4,0},{8,12},{12,8},{16,20},{20,16},{24,28},{28,24},{32,36},... | collective-permute-start | bytes 1544 | tf_op jit(solution)/shard_map/ppermute | solution.py:185
  41.5 14.5 %collective-permute-start.8 = (bf16[16,128,128]{2,1,0:T(8,128)(2,1)S(1)}, bf16[16,128,128]{2,1,0:T(8,128)(2,1)S(1)}, u32[]{:S(2)}, u32[]{:S(2)}) collective-permute-start(bf16[16,128,128]{2,1,0:T(8,128)(2,1)S(1)} %bitcast.28), channel_id=1, source_target_pairs={{0,64},{64,128},{128,192},{192,256},{256,320},{320,384},{384,448},... | collective-permute-start | bytes 1572872 | tf_op jit(solution)/shard_map/ppermute | solution.py:49
  43.7 14.2 %collective-permute-start.9 = (bf16[16,128,128]{2,1,0:T(8,128)(2,1)S(1)}, bf16[16,128,128]{2,1,0:T(8,128)(2,1)S(1)}, u32[]{:S(2)}, u32[]{:S(2)}) collective-permute-start(bf16[16,128,128]{2,1,0:T(8,128)(2,1)S(1)} %bitcast.29), channel_id=1, source_target_pairs={{0,448},{64,0},{128,64},{192,128},{256,192},{320,256},{384,320},{4... | collective-permute-start | bytes 1572872 | tf_op jit(solution)/shard_map/ppermute | solution.py:49
  48.0 26.4 %collective-permute-start.3 = (bf16[16,128,128]{2,1,0:T(8,128)(2,1)S(1)}, bf16[16,128,128]{2,1,0:T(8,128)(2,1)S(1)}, u32[]{:S(2)}, u32[]{:S(2)}) collective-permute-start(bf16[16,128,128]{2,1,0:T(8,128)(2,1)S(1)} %collective-permute-done.2.b3), channel_id=1, source_target_pairs={{0,64},{64,128},{128,192},{192,256},{256,320},{320,384},{384,448},... | collective-permute-start | bytes 1572872 | tf_op jit(solution)/shard_map/ppermute | solution.py:49
  49.9 24.4 %collective-permute-start.5 = (bf16[16,128,128]{2,1,0:T(8,128)(2,1)S(1)}, bf16[16,128,128]{2,1,0:T(8,128)(2,1)S(1)}, u32[]{:S(2)}, u32[]{:S(2)}) collective-permute-start(bf16[16,128,128]{2,1,0:T(8,128)(2,1)S(1)} %collective-permute-done.4.b4), channel_id=1, source_target_pairs={{0,448},{64,0},{128,64},{192,128},{256,192},{320,256},{384,320},{4... | collective-permute-start | bytes 1572872 | tf_op jit(solution)/shard_map/ppermute | solution.py:49
  56.0 18.4 %collective-permute-start.6 = (bf16[8,128,128]{2,1,0:T(8,128)(2,1)}, bf16[8,128,128]{2,1,0:T(8,128)(2,1)}, u32[]{:S(2)}, u32[]{:S(2)}) collective-permute-start(bf16[8,128,128]{2,1,0:T(8,128)(2,1)} %slice.20), channel_id=1, source_target_pairs={{0,128},{64,192},{128,256},{192,320},{256,384},{320,448},{384,0},{... | collective-permute-start | bytes 786440 | tf_op jit(solution)/shard_map/ppermute | solution.py:49
  57.9 0.8 copy-start.3
  58.7 15.7 %collective-permute-start.7 = (bf16[8,128,128]{2,1,0:T(8,128)(2,1)}, bf16[8,128,128]{2,1,0:T(8,128)(2,1)}, u32[]{:S(2)}, u32[]{:S(2)}) collective-permute-start(bf16[8,128,128]{2,1,0:T(8,128)(2,1)} %slice.21), channel_id=1, source_target_pairs={{0,384},{64,448},{128,0},{192,64},{256,128},{320,192},{384,256},{4... | collective-permute-start | bytes 786440 | tf_op jit(solution)/shard_map/ppermute | solution.py:49
  65.4 2.2 %copy-start.1 = (bf16[1,1,128,128,128]{4,3,2,1,0:T(8,128)(2,1)S(1)}, bf16[1,1,128,128,128]{4,3,2,1,0:T(8,128)(2,1)}, u32[]{:S(2)}) copy-start(bf16[1,1,128,128,128]{4,3,2,1,0:T(8,128)(2,1)} %param.13) | copy-start | bytes 12582916
  67.6 1.0 copy-start.4
  68.6 5.8 %copy-start.2 = (bf16[1,1,128,128,128]{4,3,2,1,0:T(8,128)(2,1)S(1)}, bf16[1,1,128,128,128]{4,3,2,1,0:T(8,128)(2,1)}, u32[]{:S(2)}) copy-start(bf16[1,1,128,128,128]{4,3,2,1,0:T(8,128)(2,1)} %param.13) | copy-start | bytes 12582916
  74.3 20.6 %copy-start.5 = (bf16[256,256]{1,0:T(8,128)(2,1)S(1)}, bf16[256,256]{1,0:T(8,128)(2,1)}, u32[]{:S(2)}) copy-start(bf16[256,256]{1,0:T(8,128)(2,1)} %cotangent.1) | copy-start | bytes 393220
  74.3 20.6 %copy-start.6 = (bf16[128,256]{1,0:T(8,128)(2,1)S(1)}, bf16[128,256]{1,0:T(8,128)(2,1)}, u32[]{:S(2)}) copy-start(bf16[128,256]{1,0:T(8,128)(2,1)} %weight.1) | copy-start | bytes 196612
  74.3 20.6 %copy-start.7 = (f32[256]{0:T(256)S(1)}, f32[256]{0:T(256)}, u32[]{:S(2)}) copy-start(f32[256]{0:T(256)} %param.11) | copy-start | bytes 3076
  126.4 11.9 %all-to-all-start.5 = ((f32[8,16,256]{2,1,0:T(8,128)}), f32[8,16,256]{2,1,0:T(8,128)S(1)}, u32[]{:S(2)}, u32[]{:S(2)}) async-start(f32[8,16,256]{2,1,0:T(8,128)} %broadcast_in_dim.51), calls=%async_computation.5 | async-start | bytes 262144 | tf_op jit(solution)/shard_map/all_to_all | solution.py:44

commit v3 on v2

--- a/solution.py
+++ b/solution.py
@@ -15,8 +15,9 @@
 SLOTS = 128
 BLOCK = SIDE * CT
 STEP = 4
-SEGMENTS = 9
+SEGMENTS = 8
 LIST = 256
+HELD = SLOTS + (STEP - 1) * SEGMENTS + STEP
 SPARE = TR
 BF16 = jnp.bfloat16
 F32 = jnp.float32
@@ -69,7 +70,7 @@
         behind = 8 - ahead
         segment = jnp.where(ahead < 4, 2 * ahead, 2 * behind - 1)
         segment = jnp.where(ahead == 0, 0, segment)
-        segment = jnp.where(ahead == 4, jnp.where(tile < SIDE, 7, 8), segment)
+        segment = jnp.where(ahead == 4, 7, segment)
         segment = jnp.where(valid, segment, SEGMENTS)
         entry = lax.broadcasted_iota(I32, (1, SLOTS), 1) + SLOTS * tile + SLOTS * BLOCK * (code & 7)
         segments = column(segment)
@@ -95,39 +96,56 @@
         start_ref[owner : owner + 1, :] = starts[owner]
 
 
-def add_products(lists, starts, values, blocks, first, acc):
-    for owner in range(2):
-        for i, (block, offset) in enumerate(blocks):
-            segment = first + i
-
-            def step(k, carry, owner=owner, block=block, offset=offset):
-                done = []
-                for u in range(STEP):
-                    e = lists[owner, k * STEP + u]
-                    tile, row = (e >> 7) & (BLOCK - 1), e >> 11
-                    product = jnp.dot(
-                        values[owner][e & (SLOTS - 1)],
-                        block[jnp.maximum(tile - offset, 0)],
-                        preferred_element_type=F32,
-                    )
-                    done.append((row, product))
-                for row, product in done:
-                    acc[owner, row] += product
-                return carry
-
-            lax.fori_loop(starts[owner, segment], starts[owner, segment + 1], step, 0)
-
-
-def early_kernel(lists, starts, own, other, b0, b1, b2, b3, b4, acc):
-    acc[...] = jnp.zeros_like(acc)
-    blocks = [(b0, 0), (b1, 0), (b2, 0), (b3, 0), (b4, 0)]
-    add_products(lists, starts, (own, other), blocks, 0, acc)
-
-
-def late_kernel(place, lists, starts, own, other, b5, b6, b7, b8, before, out, acc):
-    acc[...] = before[...]
-    blocks = [(b5, 0), (b6, 0), (b7, 0), (b8, SIDE)]
-    add_products(lists, starts, (own, other), blocks, 5, acc)
+def add_products(lists, starts, values, blocks, first, acc, held, sems):
+    def tiles(owner, i, wait):
+        base = starts[owner, first]
+
+        def step(k, carry):
+            for u in range(STEP):
+                slot = lists[owner, k * STEP + u] & (SLOTS - 1)
+                at = (k - base) * STEP + u
+                copy = pltpu.make_async_copy(values[owner].at[slot], held.at[owner, at], sems.at[owner, i])
+                if wait:
+                    copy.wait()
+                else:
+                    copy.start()
+            return carry
+
+        lax.fori_loop(starts[owner, first + i], starts[owner, first + i + 1], step, 0)
+
+    def multiply(owner, i, block):
+        base = starts[owner, first]
+
+        def step(k, carry):
+            done = []
+            for u in range(STEP):
+                e = lists[owner, k * STEP + u]
+                tile, row = (e >> 7) & (BLOCK - 1), e >> 11
+                product = jnp.dot(held[owner, (k - base) * STEP + u], block[tile], preferred_element_type=F32)
+                done.append((row, product))
+            for row, product in done:
+                acc[owner, row] += product
+            return carry
+
+        lax.fori_loop(starts[owner, first + i], starts[owner, first + i + 1], step, 0)
+
+    todo = [(owner, i, block) for i, block in enumerate(blocks) for owner in range(2)]
+    for owner, i, _ in todo:
+        tiles(owner, i, False)
+    yield
+    for owner, i, block in todo:
+        tiles(owner, i, True)
+        multiply(owner, i, block)
+
+
+def early_kernel(lists, starts, own, other, b0, b1, b2, b3, b4, acc, held, sems):
+    for _ in add_products(lists, starts, (own, other), (b0, b1, b2, b3, b4), 0, acc, held, sems):
+        acc[...] = jnp.zeros_like(acc)
+
+
+def late_kernel(place, lists, starts, own, other, b5, b6, b7, before, out, acc, held, sems):
+    for _ in add_products(lists, starts, (own, other), (b5, b6, b7), 5, acc, held, sems):
+        acc[...] = before[...]
     core = place[0]
     out[core] = acc[0, 0:TR].astype(BF16)
     out[1 - core] = acc[1, 0:TR].astype(BF16)
@@ -158,6 +176,7 @@
 
 VMEM = pl.BlockSpec(memory_space=pltpu.VMEM)
 SMEM = pl.BlockSpec(memory_space=pltpu.SMEM)
+HBM = pl.BlockSpec(memory_space=pltpu.HBM)
 
 
 def total(shares):
@@ -169,14 +188,15 @@
     core = lax.rem(index, 2)
     both = ("wide", "narrow")
     mine = lax.dynamic_slice_in_dim(features, lax.axis_index("narrow") * (CT * TILE), CT * TILE, 0)
+    own_values = tile_values[0, 0]
+    other_values = lax.ppermute(own_values, "wide", OTHER_CORE)
     own = to_all(mine, "wide", FIRST).reshape(BLOCK, TILE, FIN)
+    own, other_values = lax.optimization_barrier((own, other_values))
     up2, down2 = shift(own, 2), shift(own, -2)
     up1, down1 = shift(own, 1), shift(own, -1)
     up3, down3 = shift(up2, 1), shift(down2, -1)
-    up4, down4 = shift(up2[:SIDE], 2), shift(down2[SIDE:], -2)
-
-    own_values = tile_values[0, 0]
-    other_values = lax.ppermute(own_values, "wide", OTHER_CORE)
+    far = shift(own, 4)
+
     source = tile_source[0, 0]
     which = source[:, None] == jnp.arange(SLOTS, dtype=I32)[None, :]
     picked = jnp.sum(jnp.where(which, pick[0, 0][None, :], 0), axis=1)
@@ -197,22 +217,27 @@
     partial = pl.pallas_call(
         early_kernel,
         out_shape=sums,
-        in_specs=[SMEM] * 2 + [VMEM] * 7,
+        in_specs=[SMEM] * 2 + [HBM] * 2 + [VMEM] * 5,
         out_specs=VMEM,
-        compiler_params=pltpu.CompilerParams(vmem_limit_bytes=16 << 20),
+        scratch_shapes=[pltpu.VMEM((2, HELD, TILE, TILE), BF16), pltpu.SemaphoreType.DMA((2, 5))],
+        compiler_params=pltpu.CompilerParams(vmem_limit_bytes=24 << 20),
         cost_estimate=pl.CostEstimate(flops=SLOTS * TILE**3, bytes_accessed=8 << 20, transcendentals=0),
         name="early",
     )(lists, starts, own_values, other_values, own, up1, down1, up2, down2)
     partial = pl.pallas_call(
         late_kernel,
         out_shape=jax.ShapeDtypeStruct((2, TR, TILE, FIN), BF16),
-        in_specs=[SMEM] * 3 + [VMEM] * 7,
+        in_specs=[SMEM] * 3 + [HBM] * 2 + [VMEM] * 4,
         out_specs=VMEM,
-        scratch_shapes=[pltpu.VMEM(sums.shape, F32)],
-        compiler_params=pltpu.CompilerParams(vmem_limit_bytes=16 << 20),
+        scratch_shapes=[
+            pltpu.VMEM(sums.shape, F32),
+            pltpu.VMEM((2, HELD, TILE, TILE), BF16),
+            pltpu.SemaphoreType.DMA((2, 3)),
+        ],
+        compiler_params=pltpu.CompilerParams(vmem_limit_bytes=24 << 20),
         cost_estimate=pl.CostEstimate(flops=SLOTS * TILE**3, bytes_accessed=8 << 20, transcendentals=0),
         name="late",
-    )(place, lists, starts, own_values, other_values, up3, down3, up4, down4, partial)
+    )(place, lists, starts, own_values, other_values, up3, down3, far, partial)
 
     rows = TR * TILE // NARROW
     parts = lax.all_to_all(partial.reshape(8, rows, FIN), both, 0, 0, axis_index_groups=COLUMN)
@@ -229,8 +254,8 @@
         name="dense",
     )(parts, weight, bias.reshape(1, HID), cotangent)
 
-    share = total(lax.all_to_all(grads, both, 0, 0, axis_index_groups=COLUMN)).astype(BF16)
-    share = total(to_all(share, "wide", GROUPS_Y)).astype(BF16)
+    share = total(lax.all_to_all(grads, both, 0, 0, axis_index_groups=COLUMN))[:40]
+    share = total(to_all(share, "wide", GROUPS_Y))
     share = total(to_all(share, "wide", GROUPS_Z))
     chunk = jnp.concatenate([share[0:16], share[16:32]], axis=1)
     grad_weight = to_all(chunk, both, COLUMN).reshape(FIN, HID)

time: 140 us -> 140 us (level)
  waiting for transfers between devices: 4.62 us -> 9.59 us
  starting transfers between devices: 49 us -> 45.3 us
  local copies, waits for them, and re-layouts: 7.49 us -> 4.21 us
  blocking collectives: 62.1 us -> 65.3 us
    ppermute x8 -> x7, waiting for transfers between devices: 0.02 us -> 4.2 us  [shift(): return lax.ppermute(block, 'wide', pairs)]
    ppermute x8 -> x7, starting transfers between devices: 28.1 us -> 24.3 us  [shift(): return lax.ppermute(block, 'wide', pairs)]
    all_to_all x3, blocking collectives: 38.2 us -> 40.9 us  [to_all(): lax.all_to_all(jnp.broadcast_to(block[None], (8, *block.shape)), axes, 0,...]
    unnamed x17 -> x13, local copies, waits for them, and re-layouts: 4.7 us -> 2.87 us
    slice x2 -> x1, local copies, waits for them, and re-layouts: 1.44 us -> 0.01 us  [local(): total(lax.all_to_all(grads, both, 0, 0, axis_index_groups=COLUMN))[:40]]
  transfers between devices with their start and end apart: 11 -> 10, of which waited for: 1 -> 4; matrix products, arithmetic and copies ran while one was open for 3% -> 2% of each run, Pallas kernels for 5% -> 5%
where the time goes in v3:
time: 140 us; the launch traced here: 139 us
  blocking collectives  65.3 us (47%)
  starting transfers between devices  45.3 us (32%)
  Pallas kernels  11.7 us (8%)
  waiting for transfers between devices  9.59 us (7%)
  local copies, waits for them, and re-layouts  4.21 us (3%)
  other arithmetic  1.66 us (1%)
  between operations  1.57 us (1%)
    all_to_all x3, blocking collectives, to_all(): lax.all_to_all(jnp.broadcast_to(block[None], (8, *block.shape)), axes, 0,...  40.9 us
    ppermute x7, starting transfers between devices, shift(): return lax.ppermute(block, 'wide', pairs)  24.3 us
    all_to_all x1, blocking collectives, local(): lax.all_to_all(partial.reshape(8, rows, FIN), both, 0, 0, axis_index_grou...  16.1 us
    ppermute x1, starting transfers between devices, local(): other_values = lax.ppermute(own_values, 'wide', OTHER_CORE)  8.92 us
    all_to_all x1, blocking collectives, local(): lax.all_to_all(grads, both, 0, 0, axis_index_groups=COLUMN)  8.22 us
    all_to_all x1, starting transfers between devices, to_all(): lax.all_to_all(jnp.broadcast_to(block[None], (8, *block.shape)), axes, 0,...  6.34 us
    ppermute x1, starting transfers between devices, local(): lax.ppermute(code, 'wide', OTHER_CORE)  5.74 us
    pallas_call x1, Pallas kernels, local(): pl.pallas_call(early_kernel, out_shape=sums, in_specs=[SMEM] * 2 + [HBM]...  5.66 us
  transfers between devices with their start and end apart: 10, of which 4 were waited for; matrix products, arithmetic and copies ran while one was open for 2% of the time, Pallas kernels for 5%

profile of v3, /device:TPU:1, one launch (start us, length us, event | category | flops | bytes accessed | tf_op | source)
XLA Modules:
  0.0 139.3 jit_solution(9522104010836959665)
XLA Ops:
  0.6 0.0 copy-start
  0.6 8.9 %collective-permute-start.1 = (bf16[128,128,128]{2,1,0:T(8,128)(2,1)}, bf16[128,128,128]{2,1,0:T(8,128)(2,1)}, u32[]{:S(2)}, u32[]{:S(2)}) collective-permute-start(bf16[128,128,128]{2,1,0:T(8,128)(2,1)} %bitcast.23), channel_id=1, source_target_pairs={{0,4},{4,0},{8,12},{12,8},{16,20},{20,16},{24,28},{28,24},{32,36},... | collective-permute-start | bytes 12582920 | tf_op jit(solution)/shard_map/ppermute | solution.py:192
  9.6 0.1 broadcast_in_dim.48
  9.7 16.6 %all_to_all.30 = bf16[8,256,128]{2,1,0:T(8,128)(2,1)S(1)} all-to-all(bf16[8,256,128]{2,1,0:T(8,128)(2,1)S(1)} %broadcast_in_dim.48), channel_id=1, replica_groups={{0,8,16,24,32,40,48,56},{64,72,80,88,96,104,112,120},{128,136,144,152,1..., dimensions={0} | all-to-all | bytes 1048576 | tf_op jit(solution)/shard_map/all_to_all | solution.py:45
  26.3 4.2 %collective-permute-start.2 = (bf16[16,128,128]{2,1,0:T(8,128)(2,1)S(1)}, bf16[16,128,128]{2,1,0:T(8,128)(2,1)S(1)}, u32[]{:S(2)}, u32[]{:S(2)}) collective-permute-start(bf16[16,128,128]{2,1,0:T(8,128)(2,1)S(1)} %bitcast.26), channel_id=1, source_target_pairs={{0,128},{64,192},{128,256},{192,320},{256,384},{320,448},{384,0},{... | collective-permute-start | bytes 1572872 | tf_op jit(solution)/shard_map/ppermute | solution.py:50
  30.5 3.6 %collective-permute-start.4 = (bf16[16,128,128]{2,1,0:T(8,128)(2,1)S(1)}, bf16[16,128,128]{2,1,0:T(8,128)(2,1)S(1)}, u32[]{:S(2)}, u32[]{:S(2)}) collective-permute-start(bf16[16,128,128]{2,1,0:T(8,128)(2,1)S(1)} %bitcast.27), channel_id=1, source_target_pairs={{0,384},{64,448},{128,0},{192,64},{256,128},{320,192},{384,256},{4... | collective-permute-start | bytes 1572872 | tf_op jit(solution)/shard_map/ppermute | solution.py:50
  34.7 0.8 select_reduce_fusion
  35.6 2.8 %collective-permute-start.7 = (bf16[16,128,128]{2,1,0:T(8,128)(2,1)S(1)}, bf16[16,128,128]{2,1,0:T(8,128)(2,1)S(1)}, u32[]{:S(2)}, u32[]{:S(2)}) collective-permute-start(bf16[16,128,128]{2,1,0:T(8,128)(2,1)S(1)} %bitcast.28), channel_id=1, source_target_pairs={{0,64},{64,128},{128,192},{192,256},{256,320},{320,384},{384,448},... | collective-permute-start | bytes 1572872 | tf_op jit(solution)/shard_map/ppermute | solution.py:50
  38.4 3.7 %collective-permute-start.8 = (bf16[16,128,128]{2,1,0:T(8,128)(2,1)S(1)}, bf16[16,128,128]{2,1,0:T(8,128)(2,1)S(1)}, u32[]{:S(2)}, u32[]{:S(2)}) collective-permute-start(bf16[16,128,128]{2,1,0:T(8,128)(2,1)S(1)} %bitcast.29), channel_id=1, source_target_pairs={{0,448},{64,0},{128,64},{192,128},{256,192},{320,256},{384,320},{4... | collective-permute-start | bytes 1572872 | tf_op jit(solution)/shard_map/ppermute | solution.py:50
  42.1 0.7 compare_select_fusion
  42.8 5.7 %collective-permute-start = (s32[1,128]{1,0:T(1,128)S(1)}, s32[1,128]{1,0:T(1,128)S(1)}, u32[]{:S(2)}, u32[]{:S(2)}) collective-permute-start(s32[1,128]{1,0:T(1,128)S(1)} %compare_select_fusion), channel_id=1, source_target_pairs={{0,4},{4,0},{8,12},{12,8},{16,20},{20,16},{24,28},{28,24},{32,36},... | collective-permute-start | bytes 1544 | tf_op jit(solution)/shard_map/ppermute | solution.py:205
  48.5 0.8 collective-permute-done
  49.3 3.5 %collective-permute-start.6 = (bf16[16,128,128]{2,1,0:T(8,128)(2,1)S(1)}, bf16[16,128,128]{2,1,0:T(8,128)(2,1)S(1)}, u32[]{:S(2)}, u32[]{:S(2)}) collective-permute-start(bf16[16,128,128]{2,1,0:T(8,128)(2,1)S(1)} %bitcast.30), channel_id=1, source_target_pairs={{0,256},{64,320},{128,384},{192,448},{256,0},{320,64},{384,128},{4... | collective-permute-start | bytes 1572872 | tf_op jit(solution)/shard_map/ppermute | solution.py:50
  52.8 1.9 %collective-permute-start.3 = (bf16[16,128,128]{2,1,0:T(8,128)(2,1)S(1)}, bf16[16,128,128]{2,1,0:T(8,128)(2,1)}, u32[]{:S(2)}, u32[]{:S(2)}) collective-permute-start(bf16[16,128,128]{2,1,0:T(8,128)(2,1)S(1)} %collective-permute-done.2.b3), channel_id=1, source_target_pairs={{0,64},{64,128},{128,192},{192,256},{256,320},{320,384},{384,448},... | collective-permute-start | bytes 1572872 | tf_op jit(solution)/shard_map/ppermute | solution.py:50
  54.8 4.6 %collective-permute-start.5 = (bf16[16,128,128]{2,1,0:T(8,128)(2,1)S(1)}, bf16[16,128,128]{2,1,0:T(8,128)(2,1)}, u32[]{:S(2)}, u32[]{:S(2)}) collective-permute-start(bf16[16,128,128]{2,1,0:T(8,128)(2,1)S(1)} %collective-permute-done.4.b4), channel_id=1, source_target_pairs={{0,448},{64,0},{128,64},{192,128},{256,192},{320,256},{384,320},{4... | collective-permute-start | bytes 1572872 | tf_op jit(solution)/shard_map/ppermute | solution.py:50
  59.4 0.1 pad_add_fusion.1.place_ref.place
  59.5 1.1 lists.1
  60.6 2.2 %copy-done.1 = bf16[1,1,128,128,128]{4,3,2,1,0:T(8,128)(2,1)S(1)} copy-done((bf16[1,1,128,128,128]{4,3,2,1,0:T(8,128)(2,1)S(1)}, bf16[1,1,128,128,128]{4,3,2,1,0:T(8,128)(2,1)}, u32[]{:S(2)}) %copy-start.1) | copy-done | bytes 4194328
  62.8 5.7 %early.1.before = f32[2,9,128,128]{3,2,1,0:T(8,128)S(1)} custom-call(s32[2,256]{1,0:T(2,128)S(1)} %get-tuple-element.9.lists, s32[2,128]{1,0:T(2,128)S(1)} %get-tuple-element.10.starts, bf16[128,128,128]{2,1,0:T(8,128)(2,1)S(1)} %bitcast.24, bf16[128,128,128]{2,1,0:T(8,128)(2,1)} %collective-permute-done.1.other, bf16[16,128,128]{2,1,0:T(8,128)(2,1)S(1)} %bitcast.31, ...), custom_call_target="tpu_custom_call" | custom-call | flops 268435456 | bytes 8388608 | tf_op jit(solution)/shard_map/early/pallas_call | solution.py:217
  68.5 0.4 collective-permute-done.6.b7
  68.9 3.8 %collective-permute-done.3.b5 = bf16[16,128,128]{2,1,0:T(8,128)(2,1)} collective-permute-done((bf16[16,128,128]{2,1,0:T(8,128)(2,1)S(1)}, bf16[16,128,128]{2,1,0:T(8,128)(2,1)}, u32[]{:S(2)}, u32[]{:S(2)}) %collective-permute-start.3) | collective-permute-done | bytes 524320 | tf_op jit(solution)/shard_map/ppermute | solution.py:50
  72.7 4.0 %late.1 = bf16[2,8,128,128]{3,2,1,0:T(8,128)(2,1)S(1)} custom-call(s32[2]{0:T(128)S(1)} %pad_add_fusion.1.place_ref.place, s32[2,256]{1,0:T(2,128)S(1)} %get-tuple-element.9.lists, s32[2,128]{1,0:T(2,128)S(1)} %get-tuple-element.10.starts, bf16[128,128,128]{2,1,0:T(8,128)(2,1)S(1)} %bitcast.25, bf16[128,128,128]{2,1,0:T(8,128)(2,1)} %collective-permute-done.1.other, ...), custom_call_target="tpu_custom_call" | custom-call | flops 268435456 | bytes 8388608 | tf_op jit(solution)/shard_map/late/pallas_call | solution.py:227
  76.7 16.1 %all_to_all.31.parts = bf16[8,256,128]{2,1,0:T(8,128)(2,1)S(1)} all-to-all(bf16[8,256,128]{2,1,0:T(8,128)(2,1)S(1)} %bitcast.32), channel_id=1, replica_groups={{0,1,2,3,4,5,6,7},{8,9,10,11,12,13,14,15},{16,17,18,19,20,21,22,23},{24..., dimensions={0} | all-to-all | bytes 1048576 | tf_op jit(solution)/shard_map/all_to_all | solution.py:243
  92.9 0.9 dense.1
  93.8 8.2 %all_to_all.32 = bf16[8,48,128]{2,1,0:T(8,128)(2,1)S(1)} all-to-all(bf16[8,48,128]{2,1,0:T(8,128)(2,1)S(1)} %get-tuple-element.14), channel_id=1, replica_groups={{0,1,2,3,4,5,6,7},{8,9,10,11,12,13,14,15},{16,17,18,19,20,21,22,23},{24..., dimensions={0} | all-to-all | bytes 196608 | tf_op jit(solution)/shard_map/all_to_all | solution.py:257
  102.0 11.4 %all_to_all.33 = f32[8,40,128]{2,1,0:T(8,128)S(1)} all-to-all(f32[8,40,128]{2,1,0:T(8,128)S(1)} %broadcast_in_dim.49), channel_id=1, replica_groups={{0,8,16,24,32,40,48,56},{64,72,80,88,96,104,112,120},{128,136,144,152,1..., dimensions={0} | all-to-all | bytes 327680 | tf_op jit(solution)/shard_map/all_to_all | solution.py:45
  113.5 12.9 %all_to_all.34 = f32[8,40,128]{2,1,0:T(8,128)S(1)} all-to-all(f32[8,40,128]{2,1,0:T(8,128)S(1)} %broadcast_in_dim.50), channel_id=1, replica_groups={{0,64,128,192,256,320,384,448},{8,72,136,200,264,328,392,456},{16,80,14..., dimensions={0} | all-to-all | bytes 327680 | tf_op jit(solution)/shard_map/all_to_all | solution.py:45
  126.4 0.7 broadcast_in_dim.51
  127.1 6.3 %all-to-all-start.5 = ((f32[8,16,256]{2,1,0:T(8,128)}), f32[8,16,256]{2,1,0:T(8,128)S(1)}, u32[]{:S(2)}, u32[]{:S(2)}) async-start(f32[8,16,256]{2,1,0:T(8,128)} %broadcast_in_dim.51), calls=%async_computation.5 | async-start | bytes 262144 | tf_op jit(solution)/shard_map/all_to_all | solution.py:45
  133.4 0.6 slice_bitcast_fusion
  134.0 4.6 %all-to-all-done.5 = f32[8,16,256]{2,1,0:T(8,128)S(1)} async-done(((f32[8,16,256]{2,1,0:T(8,128)}), f32[8,16,256]{2,1,0:T(8,128)S(1)}, u32[]{:S(2)}, u32[]{:S(2)}) %all-to-all-start.5) | async-done | bytes 131104 | tf_op jit(solution)/shard_map/all_to_all | solution.py:45
  138.6 0.7 copy.14
  (26 shorter events, 0.1 us)
Async XLA Ops:
  0.6 9.0 %copy-start = (bf16[1024,128]{1,0:T(8,128)(2,1)S(1)}, bf16[1024,128]{1,0:T(8,128)(2,1)}, u32[]{:S(2)}) copy-start(bf16[1024,128]{1,0:T(8,128)(2,1)} %param.9) | copy-start | bytes 786436
  0.6 25.6 %collective-permute-start.1 = (bf16[128,128,128]{2,1,0:T(8,128)(2,1)}, bf16[128,128,128]{2,1,0:T(8,128)(2,1)}, u32[]{:S(2)}, u32[]{:S(2)}) collective-permute-start(bf16[128,128,128]{2,1,0:T(8,128)(2,1)} %bitcast.23), channel_id=1, source_target_pairs={{0,4},{4,0},{8,12},{12,8},{16,20},{20,16},{24,28},{28,24},{32,36},... | collective-permute-start | bytes 12582920 | tf_op jit(solution)/shard_map/ppermute | solution.py:192
  26.3 26.5 %collective-permute-start.2 = (bf16[16,128,128]{2,1,0:T(8,128)(2,1)S(1)}, bf16[16,128,128]{2,1,0:T(8,128)(2,1)S(1)}, u32[]{:S(2)}, u32[]{:S(2)}) collective-permute-start(bf16[16,128,128]{2,1,0:T(8,128)(2,1)S(1)} %bitcast.26), channel_id=1, source_target_pairs={{0,128},{64,192},{128,256},{192,320},{256,384},{320,448},{384,0},{... | collective-permute-start | bytes 1572872 | tf_op jit(solution)/shard_map/ppermute | solution.py:50
  30.5 24.3 %collective-permute-start.4 = (bf16[16,128,128]{2,1,0:T(8,128)(2,1)S(1)}, bf16[16,128,128]{2,1,0:T(8,128)(2,1)S(1)}, u32[]{:S(2)}, u32[]{:S(2)}) collective-permute-start(bf16[16,128,128]{2,1,0:T(8,128)(2,1)S(1)} %bitcast.27), channel_id=1, source_target_pairs={{0,384},{64,448},{128,0},{192,64},{256,128},{320,192},{384,256},{4... | collective-permute-start | bytes 1572872 | tf_op jit(solution)/shard_map/ppermute | solution.py:50
  35.6 25.0 %collective-permute-start.7 = (bf16[16,128,128]{2,1,0:T(8,128)(2,1)S(1)}, bf16[16,128,128]{2,1,0:T(8,128)(2,1)S(1)}, u32[]{:S(2)}, u32[]{:S(2)}) collective-permute-start(bf16[16,128,128]{2,1,0:T(8,128)(2,1)S(1)} %bitcast.28), channel_id=1, source_target_pairs={{0,64},{64,128},{128,192},{192,256},{256,320},{320,384},{384,448},... | collective-permute-start | bytes 1572872 | tf_op jit(solution)/shard_map/ppermute | solution.py:50
  38.4 22.2 %collective-permute-start.8 = (bf16[16,128,128]{2,1,0:T(8,128)(2,1)S(1)}, bf16[16,128,128]{2,1,0:T(8,128)(2,1)S(1)}, u32[]{:S(2)}, u32[]{:S(2)}) collective-permute-start(bf16[16,128,128]{2,1,0:T(8,128)(2,1)S(1)} %bitcast.29), channel_id=1, source_target_pairs={{0,448},{64,0},{128,64},{192,128},{256,192},{320,256},{384,320},{4... | collective-permute-start | bytes 1572872 | tf_op jit(solution)/shard_map/ppermute | solution.py:50
  42.8 6.5 %collective-permute-start = (s32[1,128]{1,0:T(1,128)S(1)}, s32[1,128]{1,0:T(1,128)S(1)}, u32[]{:S(2)}, u32[]{:S(2)}) collective-permute-start(s32[1,128]{1,0:T(1,128)S(1)} %compare_select_fusion), channel_id=1, source_target_pairs={{0,4},{4,0},{8,12},{12,8},{16,20},{20,16},{24,28},{28,24},{32,36},... | collective-permute-start | bytes 1544 | tf_op jit(solution)/shard_map/ppermute | solution.py:205
  49.3 19.5 %collective-permute-start.6 = (bf16[16,128,128]{2,1,0:T(8,128)(2,1)S(1)}, bf16[16,128,128]{2,1,0:T(8,128)(2,1)S(1)}, u32[]{:S(2)}, u32[]{:S(2)}) collective-permute-start(bf16[16,128,128]{2,1,0:T(8,128)(2,1)S(1)} %bitcast.30), channel_id=1, source_target_pairs={{0,256},{64,320},{128,384},{192,448},{256,0},{320,64},{384,128},{4... | collective-permute-start | bytes 1572872 | tf_op jit(solution)/shard_map/ppermute | solution.py:50
  52.8 19.8 %collective-permute-start.3 = (bf16[16,128,128]{2,1,0:T(8,128)(2,1)S(1)}, bf16[16,128,128]{2,1,0:T(8,128)(2,1)}, u32[]{:S(2)}, u32[]{:S(2)}) collective-permute-start(bf16[16,128,128]{2,1,0:T(8,128)(2,1)S(1)} %collective-permute-done.2.b3), channel_id=1, source_target_pairs={{0,64},{64,128},{128,192},{192,256},{256,320},{320,384},{384,448},... | collective-permute-start | bytes 1572872 | tf_op jit(solution)/shard_map/ppermute | solution.py:50
  54.8 17.9 %collective-permute-start.5 = (bf16[16,128,128]{2,1,0:T(8,128)(2,1)S(1)}, bf16[16,128,128]{2,1,0:T(8,128)(2,1)}, u32[]{:S(2)}, u32[]{:S(2)}) collective-permute-start(bf16[16,128,128]{2,1,0:T(8,128)(2,1)S(1)} %collective-permute-done.4.b4), channel_id=1, source_target_pairs={{0,448},{64,0},{128,64},{192,128},{256,192},{320,256},{384,320},{4... | collective-permute-start | bytes 1572872 | tf_op jit(solution)/shard_map/ppermute | solution.py:50
  60.6 2.2 %copy-start.1 = (bf16[1,1,128,128,128]{4,3,2,1,0:T(8,128)(2,1)S(1)}, bf16[1,1,128,128,128]{4,3,2,1,0:T(8,128)(2,1)}, u32[]{:S(2)}) copy-start(bf16[1,1,128,128,128]{4,3,2,1,0:T(8,128)(2,1)} %param.13) | copy-start | bytes 12582916
  62.8 9.9 %copy-start.2 = (bf16[1,1,128,128,128]{4,3,2,1,0:T(8,128)(2,1)S(1)}, bf16[1,1,128,128,128]{4,3,2,1,0:T(8,128)(2,1)}, u32[]{:S(2)}) copy-start(bf16[1,1,128,128,128]{4,3,2,1,0:T(8,128)(2,1)} %param.13) | copy-start | bytes 12582916
  68.5 24.4 %copy-start.3 = (bf16[256,256]{1,0:T(8,128)(2,1)S(1)}, bf16[256,256]{1,0:T(8,128)(2,1)}, u32[]{:S(2)}) copy-start(bf16[256,256]{1,0:T(8,128)(2,1)} %cotangent.1) | copy-start | bytes 393220
  68.5 24.4 %copy-start.4 = (bf16[128,256]{1,0:T(8,128)(2,1)S(1)}, bf16[128,256]{1,0:T(8,128)(2,1)}, u32[]{:S(2)}) copy-start(bf16[128,256]{1,0:T(8,128)(2,1)} %weight.1) | copy-start | bytes 196612
  68.5 24.4 %copy-start.5 = (f32[256]{0:T(256)S(1)}, f32[256]{0:T(256)}, u32[]{:S(2)}) copy-start(f32[256]{0:T(256)} %param.11) | copy-start | bytes 3076
  127.1 11.5 %all-to-all-start.5 = ((f32[8,16,256]{2,1,0:T(8,128)}), f32[8,16,256]{2,1,0:T(8,128)S(1)}, u32[]{:S(2)}, u32[]{:S(2)}) async-start(f32[8,16,256]{2,1,0:T(8,128)} %broadcast_in_dim.51), calls=%async_computation.5 | async-start | bytes 262144 | tf_op jit(solution)/shard_map/all_to_all | solution.py:45

commit v4 on v3

--- a/solution.py
+++ b/solution.py
@@ -14,10 +14,10 @@
 NARROW = 4
 SLOTS = 128
 BLOCK = SIDE * CT
-STEP = 4
+STEP = 8
 SEGMENTS = 8
+FAR = 5
 LIST = 256
-HELD = SLOTS + (STEP - 1) * SEGMENTS + STEP
 SPARE = TR
 BF16 = jnp.bfloat16
 F32 = jnp.float32
@@ -38,6 +38,7 @@
 COLUMN = [
     [wide_index(z, y, c) * NARROW + x for c in (0, 1) for x in range(NARROW)] for z in RANGE for y in RANGE
 ]
+CHIP = [[2 * i, 2 * i + 1] for i in range(SIDE * SIDE)]
 OTHER_CORE = [(i, i ^ 1) for i in range(2 * SIDE * SIDE)]
 
 
@@ -60,7 +61,7 @@
     core, at = place_ref[0], place_ref[1]
     starts = []
     for owner in range(2):
-        code = code_ref[owner : owner + 1, :]
+        code = jnp.where(core == owner, code_ref[0:1, :], code_ref[1:2, :])
         source = lax.shift_right_arithmetic(code, 4)
         valid = (code >= 0) & ((source & 1) == core)
         z, y = lax.shift_right_arithmetic(source, 4), lax.shift_right_arithmetic(source, 1) & 7
@@ -70,14 +71,15 @@
         behind = 8 - ahead
         segment = jnp.where(ahead < 4, 2 * ahead, 2 * behind - 1)
         segment = jnp.where(ahead == 0, 0, segment)
-        segment = jnp.where(ahead == 4, 7, segment)
+        segment = jnp.where(segment < FAR, segment, segment + 1)
+        segment = jnp.where(ahead == 4, FAR, segment)
         segment = jnp.where(valid, segment, SEGMENTS)
         entry = lax.broadcasted_iota(I32, (1, SLOTS), 1) + SLOTS * tile + SLOTS * BLOCK * (code & 7)
         segments = column(segment)
         kinds = lax.broadcasted_iota(I32, (SLOTS, SLOTS), 1)
         member = (segments == kinds).astype(I32)
         sizes = jnp.sum(member, axis=0, keepdims=True)
-        sizes = lax.shift_right_arithmetic(sizes + STEP - 1, 2) * STEP
+        sizes = lax.shift_right_arithmetic(sizes + STEP - 1, 3) * STEP
         sizes = jnp.where(lax.broadcasted_iota(I32, (1, SLOTS), 1) < SEGMENTS, sizes, 0)
         size = column(sizes)
         rows = lax.broadcasted_iota(I32, (SLOTS, SLOTS), 0)
@@ -91,61 +93,41 @@
         slots = lax.broadcasted_iota(I32, (SLOTS, LIST), 1)
         hit = places == slots
         list_ref[owner : owner + 1, :] = spare + jnp.sum(jnp.where(hit, entries - spare, 0), axis=0, keepdims=True)
-        starts.append(lax.shift_right_arithmetic(start, 2))
+        starts.append(lax.shift_right_arithmetic(start, 3))
     for owner in range(2):
         start_ref[owner : owner + 1, :] = starts[owner]
 
 
-def add_products(lists, starts, values, blocks, first, acc, held, sems):
-    def tiles(owner, i, wait):
-        base = starts[owner, first]
-
-        def step(k, carry):
-            for u in range(STEP):
-                slot = lists[owner, k * STEP + u] & (SLOTS - 1)
-                at = (k - base) * STEP + u
-                copy = pltpu.make_async_copy(values[owner].at[slot], held.at[owner, at], sems.at[owner, i])
-                if wait:
-                    copy.wait()
-                else:
-                    copy.start()
-            return carry
-
-        lax.fori_loop(starts[owner, first + i], starts[owner, first + i + 1], step, 0)
-
-    def multiply(owner, i, block):
-        base = starts[owner, first]
-
-        def step(k, carry):
+def add_products(lists, starts, owner, values, blocks, first, acc):
+    for i, block in enumerate(blocks):
+
+        def step(k, carry, block=block):
             done = []
             for u in range(STEP):
                 e = lists[owner, k * STEP + u]
                 tile, row = (e >> 7) & (BLOCK - 1), e >> 11
-                product = jnp.dot(held[owner, (k - base) * STEP + u], block[tile], preferred_element_type=F32)
-                done.append((row, product))
+                done.append((row, jnp.dot(values[e & (SLOTS - 1)], block[tile], preferred_element_type=F32)))
             for row, product in done:
                 acc[owner, row] += product
             return carry
 
         lax.fori_loop(starts[owner, first + i], starts[owner, first + i + 1], step, 0)
 
-    todo = [(owner, i, block) for i, block in enumerate(blocks) for owner in range(2)]
-    for owner, i, _ in todo:
-        tiles(owner, i, False)
-    yield
-    for owner, i, block in todo:
-        tiles(owner, i, True)
-        multiply(owner, i, block)
-
-
-def early_kernel(lists, starts, own, other, b0, b1, b2, b3, b4, acc, held, sems):
-    for _ in add_products(lists, starts, (own, other), (b0, b1, b2, b3, b4), 0, acc, held, sems):
-        acc[...] = jnp.zeros_like(acc)
-
-
-def late_kernel(place, lists, starts, own, other, b5, b6, b7, before, out, acc, held, sems):
-    for _ in add_products(lists, starts, (own, other), (b5, b6, b7), 5, acc, held, sems):
-        acc[...] = before[...]
+
+def early_kernel(lists, starts, own, other, b0, b1, b2, b3, b4, b5, acc, other_here, sem):
+    copy = pltpu.make_async_copy(other, other_here, sem)
+    copy.start()
+    acc[...] = jnp.zeros_like(acc)
+    blocks = (b0, b1, b2, b3, b4, b5)
+    add_products(lists, starts, 0, own, blocks, 0, acc)
+    copy.wait()
+    add_products(lists, starts, 1, other_here, blocks, 0, acc)
+
+
+def late_kernel(place, lists, starts, own, other, b6, b7, before, out, acc):
+    acc[...] = before[...]
+    add_products(lists, starts, 0, own, (b6, b7), 6, acc)
+    add_products(lists, starts, 1, other, (b6, b7), 6, acc)
     core = place[0]
     out[core] = acc[0, 0:TR].astype(BF16)
     out[1 - core] = acc[1, 0:TR].astype(BF16)
@@ -202,7 +184,7 @@
     picked = jnp.sum(jnp.where(which, pick[0, 0][None, :], 0), axis=1)
     live = jnp.arange(SLOTS, dtype=I32) < tile_count[0, 0]
     code = jnp.where(live, tile_row[0, 0] + 8 * picked + 16 * source, -1)[None]
-    codes = jnp.concatenate([code, lax.ppermute(code, "wide", OTHER_CORE)], axis=0)
+    codes = lax.all_to_all(jnp.broadcast_to(code, (2, SLOTS)), "wide", 0, 0, axis_index_groups=CHIP)
     place = jnp.stack([core, jnp.where(core == 0, index // 16, lax.rem(index // 2, 8))])
     lists, starts = pl.pallas_call(
         list_kernel,
@@ -214,30 +196,26 @@
     )(place, codes)
 
     sums = jax.ShapeDtypeStruct((2, TR + 1, TILE, FIN), F32)
-    partial = pl.pallas_call(
+    partial, other_here = pl.pallas_call(
         early_kernel,
-        out_shape=sums,
-        in_specs=[SMEM] * 2 + [HBM] * 2 + [VMEM] * 5,
-        out_specs=VMEM,
-        scratch_shapes=[pltpu.VMEM((2, HELD, TILE, TILE), BF16), pltpu.SemaphoreType.DMA((2, 5))],
-        compiler_params=pltpu.CompilerParams(vmem_limit_bytes=24 << 20),
+        out_shape=(sums, jax.ShapeDtypeStruct(own_values.shape, BF16)),
+        in_specs=[SMEM] * 2 + [VMEM, HBM] + [VMEM] * 6,
+        out_specs=(VMEM, VMEM),
+        scratch_shapes=[pltpu.SemaphoreType.DMA],
+        compiler_params=pltpu.CompilerParams(vmem_limit_bytes=16 << 20),
         cost_estimate=pl.CostEstimate(flops=SLOTS * TILE**3, bytes_accessed=8 << 20, transcendentals=0),
         name="early",
-    )(lists, starts, own_values, other_values, own, up1, down1, up2, down2)
+    )(lists, starts, own_values, other_values, own, up1, down1, up2, down2, far)
     partial = pl.pallas_call(
         late_kernel,
         out_shape=jax.ShapeDtypeStruct((2, TR, TILE, FIN), BF16),
-        in_specs=[SMEM] * 3 + [HBM] * 2 + [VMEM] * 4,
+        in_specs=[SMEM] * 3 + [VMEM] * 5,
         out_specs=VMEM,
-        scratch_shapes=[
-            pltpu.VMEM(sums.shape, F32),
-            pltpu.VMEM((2, HELD, TILE, TILE), BF16),
-            pltpu.SemaphoreType.DMA((2, 3)),
-        ],
-        compiler_params=pltpu.CompilerParams(vmem_limit_bytes=24 << 20),
+        scratch_shapes=[pltpu.VMEM(sums.shape, F32)],
+        compiler_params=pltpu.CompilerParams(vmem_limit_bytes=16 << 20),
         cost_estimate=pl.CostEstimate(flops=SLOTS * TILE**3, bytes_accessed=8 << 20, transcendentals=0),
         name="late",
-    )(place, lists, starts, own_values, other_values, up3, down3, far, partial)
+    )(place, lists, starts, own_values, other_here, up3, down3, partial)
 
     rows = TR * TILE // NARROW
     parts = lax.all_to_all(partial.reshape(8, rows, FIN), both, 0, 0, axis_index_groups=COLUMN)

time: 140 us -> 139 us (level)
  starting transfers between devices: 45.3 us -> 49.6 us
  waiting for transfers between devices: 9.59 us -> 5.49 us
  Pallas kernels: 11.7 us -> 9.94 us
    all_to_all x0 -> x1, starting transfers between devices: none -> 6.55 us  [local(): lax.all_to_all(jnp.broadcast_to(code, (2, SLOTS)), 'wide', 0, 0, axis_ind...]
    ppermute x1 -> x0, starting transfers between devices: 5.74 us -> none  [local(): lax.ppermute(code, 'wide', OTHER_CORE)]
    ppermute x7, waiting for transfers between devices: 4.2 us -> 0.02 us  [shift(): return lax.ppermute(block, 'wide', pairs)]
    ppermute x7, starting transfers between devices: 24.3 us -> 27.8 us  [shift(): return lax.ppermute(block, 'wide', pairs)]
    pallas_call x1, Pallas kernels: 4.03 us -> 2.45 us  [local(): pl.pallas_call(late_kernel, out_shape=jax.ShapeDtypeStruct((2, TR, TILE,...]
    all_to_all x3, blocking collectives: 40.9 us -> 42.5 us  [to_all(): lax.all_to_all(jnp.broadcast_to(block[None], (8, *block.shape)), axes, 0,...]
  transfers between devices with their start and end apart: 10 -> 10, of which waited for: 4 -> 2; matrix products, arithmetic and copies ran while one was open for 2% -> 2% of each run, Pallas kernels for 5% -> 5%
where the time goes in v4:
time: 139 us
  blocking collectives  65.5 us (47%)
  starting transfers between devices  49.6 us (36%)
  Pallas kernels  9.94 us (7%)
  waiting for transfers between devices  5.49 us (4%)
  local copies, waits for them, and re-layouts  4.78 us (3%)
  other arithmetic  1.65 us (1%)
  between operations  1.56 us (1%)
    all_to_all x3, blocking collectives, to_all(): lax.all_to_all(jnp.broadcast_to(block[None], (8, *block.shape)), axes, 0,...  42.5 us
    ppermute x7, starting transfers between devices, shift(): return lax.ppermute(block, 'wide', pairs)  27.8 us
    all_to_all x1, blocking collectives, local(): lax.all_to_all(partial.reshape(8, rows, FIN), both, 0, 0, axis_index_grou...  14.8 us
    ppermute x1, starting transfers between devices, local(): other_values = lax.ppermute(own_values, 'wide', OTHER_CORE)  8.92 us
    all_to_all x1, blocking collectives, local(): lax.all_to_all(grads, both, 0, 0, axis_index_groups=COLUMN)  8.22 us
    all_to_all x1, starting transfers between devices, local(): lax.all_to_all(jnp.broadcast_to(code, (2, SLOTS)), 'wide', 0, 0, axis_ind...  6.55 us
    all_to_all x1, starting transfers between devices, to_all(): lax.all_to_all(jnp.broadcast_to(block[None], (8, *block.shape)), axes, 0,...  6.34 us
    pallas_call x1, Pallas kernels, local(): pl.pallas_call(early_kernel, out_shape=(sums, jax.ShapeDtypeStruct(own_va...  5.49 us
  transfers between devices with their start and end apart: 10, of which 2 were waited for; matrix products, arithmetic and copies ran while one was open for 2% of the time, Pallas kernels for 5%

profile of v4, /device:TPU:1, one launch (start us, length us, event | category | flops | bytes accessed | tf_op | source)
XLA Modules:
  0.0 138.6 jit_solution(8888464854690743586)
XLA Ops:
  0.6 0.0 copy-start
  0.6 8.9 %collective-permute-start = (bf16[128,128,128]{2,1,0:T(8,128)(2,1)}, bf16[128,128,128]{2,1,0:T(8,128)(2,1)}, u32[]{:S(2)}, u32[]{:S(2)}) collective-permute-start(bf16[128,128,128]{2,1,0:T(8,128)(2,1)} %bitcast.21), channel_id=1, source_target_pairs={{0,4},{4,0},{8,12},{12,8},{16,20},{20,16},{24,28},{28,24},{32,36},... | collective-permute-start | bytes 12582920 | tf_op jit(solution)/shard_map/ppermute | solution.py:174
  9.6 0.1 broadcast_in_dim.54
  9.7 16.6 %all_to_all.38 = bf16[8,256,128]{2,1,0:T(8,128)(2,1)S(1)} all-to-all(bf16[8,256,128]{2,1,0:T(8,128)(2,1)S(1)} %broadcast_in_dim.54), channel_id=1, replica_groups={{0,8,16,24,32,40,48,56},{64,72,80,88,96,104,112,120},{128,136,144,152,1..., dimensions={0} | all-to-all | bytes 1048576 | tf_op jit(solution)/shard_map/all_to_all | solution.py:46
  26.3 4.2 %collective-permute-start.3 = (bf16[16,128,128]{2,1,0:T(8,128)(2,1)S(1)}, bf16[16,128,128]{2,1,0:T(8,128)(2,1)S(1)}, u32[]{:S(2)}, u32[]{:S(2)}) collective-permute-start(bf16[16,128,128]{2,1,0:T(8,128)(2,1)S(1)} %bitcast.24), channel_id=1, source_target_pairs={{0,128},{64,192},{128,256},{192,320},{256,384},{320,448},{384,0},{... | collective-permute-start | bytes 1572872 | tf_op jit(solution)/shard_map/ppermute | solution.py:51
  30.5 3.6 %collective-permute-start.4 = (bf16[16,128,128]{2,1,0:T(8,128)(2,1)S(1)}, bf16[16,128,128]{2,1,0:T(8,128)(2,1)S(1)}, u32[]{:S(2)}, u32[]{:S(2)}) collective-permute-start(bf16[16,128,128]{2,1,0:T(8,128)(2,1)S(1)} %bitcast.25), channel_id=1, source_target_pairs={{0,384},{64,448},{128,0},{192,64},{256,128},{320,192},{384,256},{4... | collective-permute-start | bytes 1572872 | tf_op jit(solution)/shard_map/ppermute | solution.py:51
  34.1 2.8 %collective-permute-start.1 = (bf16[16,128,128]{2,1,0:T(8,128)(2,1)S(1)}, bf16[16,128,128]{2,1,0:T(8,128)(2,1)S(1)}, u32[]{:S(2)}, u32[]{:S(2)}) collective-permute-start(bf16[16,128,128]{2,1,0:T(8,128)(2,1)S(1)} %bitcast.26), channel_id=1, source_target_pairs={{0,64},{64,128},{128,192},{192,256},{256,320},{320,384},{384,448},... | collective-permute-start | bytes 1572872 | tf_op jit(solution)/shard_map/ppermute | solution.py:51
  36.9 3.7 %collective-permute-start.2 = (bf16[16,128,128]{2,1,0:T(8,128)(2,1)S(1)}, bf16[16,128,128]{2,1,0:T(8,128)(2,1)S(1)}, u32[]{:S(2)}, u32[]{:S(2)}) collective-permute-start(bf16[16,128,128]{2,1,0:T(8,128)(2,1)S(1)} %bitcast.27), channel_id=1, source_target_pairs={{0,448},{64,0},{128,64},{192,128},{256,192},{320,256},{384,320},{4... | collective-permute-start | bytes 1572872 | tf_op jit(solution)/shard_map/ppermute | solution.py:51
  40.6 7.0 %collective-permute-start.5 = (bf16[16,128,128]{2,1,0:T(8,128)(2,1)S(1)}, bf16[16,128,128]{2,1,0:T(8,128)(2,1)}, u32[]{:S(2)}, u32[]{:S(2)}) collective-permute-start(bf16[16,128,128]{2,1,0:T(8,128)(2,1)S(1)} %bitcast.28), channel_id=1, source_target_pairs={{0,256},{64,320},{128,384},{192,448},{256,0},{320,64},{384,128},{4... | collective-permute-start | bytes 1572872 | tf_op jit(solution)/shard_map/ppermute | solution.py:51
  47.7 1.9 %collective-permute-start.6 = (bf16[16,128,128]{2,1,0:T(8,128)(2,1)S(1)}, bf16[16,128,128]{2,1,0:T(8,128)(2,1)S(1)}, u32[]{:S(2)}, u32[]{:S(2)}) collective-permute-start(bf16[16,128,128]{2,1,0:T(8,128)(2,1)S(1)} %collective-permute-done.3.b3), channel_id=1, source_target_pairs={{0,64},{64,128},{128,192},{192,256},{256,320},{320,384},{384,448},... | collective-permute-start | bytes 1572872 | tf_op jit(solution)/shard_map/ppermute | solution.py:51
  49.6 4.6 %collective-permute-start.7 = (bf16[16,128,128]{2,1,0:T(8,128)(2,1)S(1)}, bf16[16,128,128]{2,1,0:T(8,128)(2,1)}, u32[]{:S(2)}, u32[]{:S(2)}) collective-permute-start(bf16[16,128,128]{2,1,0:T(8,128)(2,1)S(1)} %collective-permute-done.4.b4), channel_id=1, source_target_pairs={{0,448},{64,0},{128,64},{192,128},{256,192},{320,256},{384,320},{4... | collective-permute-start | bytes 1572872 | tf_op jit(solution)/shard_map/ppermute | solution.py:51
  54.8 0.8 select_reduce_fusion
  55.7 0.7 compare_select_fusion
  56.4 0.6 broadcast_in_dim.53
  56.9 6.6 %all-to-all-start = ((s32[2,1,128]{2,1,0:T(1,128)}), s32[2,1,128]{2,1,0:T(1,128)S(1)}, u32[]{:S(2)}, u32[]{:S(2)}) async-start(s32[2,1,128]{2,1,0:T(1,128)} %broadcast_in_dim.53), calls=%async_computation | async-start | bytes 2048 | tf_op jit(solution)/shard_map/all_to_all | solution.py:187
  63.5 0.1 pad_add_fusion.place_ref.place
  63.6 0.9 all-to-all-done
  64.4 1.1 lists.1
  65.6 0.0 copy-start.1
  65.6 2.2 %copy-done.1 = bf16[1,1,128,128,128]{4,3,2,1,0:T(8,128)(2,1)S(1)} copy-done((bf16[1,1,128,128,128]{4,3,2,1,0:T(8,128)(2,1)S(1)}, bf16[1,1,128,128,128]{4,3,2,1,0:T(8,128)(2,1)}, u32[]{:S(2)}) %copy-start.1) | copy-done | bytes 4194328
  67.8 5.5 %early.1 = (f32[2,9,128,128]{3,2,1,0:T(8,128)S(1)}, bf16[128,128,128]{2,1,0:T(8,128)(2,1)S(1)}) custom-call(s32[2,256]{1,0:T(2,128)S(1)} %get-tuple-element.11.lists, s32[2,128]{1,0:T(2,128)S(1)} %get-tuple-element.12.starts, bf16[128,128,128]{2,1,0:T(8,128)(2,1)S(1)} %bitcast.22, bf16[128,128,128]{2,1,0:T(8,128)(2,1)} %collective-permute-done.other, ...), custom_call_target="tpu_custom_call" | custom-call | flops 268435456 | bytes 8388608 | tf_op jit(solution)/shard_map/early/pallas_call | solution.py:199
  73.3 2.4 %late.1 = bf16[2,8,128,128]{3,2,1,0:T(8,128)(2,1)S(1)} custom-call(s32[2]{0:T(128)S(1)} %pad_add_fusion.place_ref.place, s32[2,256]{1,0:T(2,128)S(1)} %get-tuple-element.11.lists, s32[2,128]{1,0:T(2,128)S(1)} %get-tuple-element.12.starts, bf16[128,128,128]{2,1,0:T(8,128)(2,1)S(1)} %bitcast.23, bf16[128,128,128]{2,1,0:T(8,128)(2,1)S(1)} %get-tuple-element.15.other, ...), custom_call_target="tpu_custom_call" | custom-call | flops 268435456 | bytes 8388608 | tf_op jit(solution)/shard_map/late/pallas_call | solution.py:209
  75.8 14.8 %all_to_all.39.parts = bf16[8,256,128]{2,1,0:T(8,128)(2,1)S(1)} all-to-all(bf16[8,256,128]{2,1,0:T(8,128)(2,1)S(1)} %bitcast.30), channel_id=1, replica_groups={{0,1,2,3,4,5,6,7},{8,9,10,11,12,13,14,15},{16,17,18,19,20,21,22,23},{24..., dimensions={0} | all-to-all | bytes 1048576 | tf_op jit(solution)/shard_map/all_to_all | solution.py:221
  90.6 0.9 dense.1
  91.5 8.2 %all_to_all.40 = bf16[8,48,128]{2,1,0:T(8,128)(2,1)S(1)} all-to-all(bf16[8,48,128]{2,1,0:T(8,128)(2,1)S(1)} %get-tuple-element.18), channel_id=1, replica_groups={{0,1,2,3,4,5,6,7},{8,9,10,11,12,13,14,15},{16,17,18,19,20,21,22,23},{24..., dimensions={0} | all-to-all | bytes 196608 | tf_op jit(solution)/shard_map/all_to_all | solution.py:235
  99.8 11.4 %all_to_all.41 = f32[8,40,128]{2,1,0:T(8,128)S(1)} all-to-all(f32[8,40,128]{2,1,0:T(8,128)S(1)} %broadcast_in_dim.55), channel_id=1, replica_groups={{0,8,16,24,32,40,48,56},{64,72,80,88,96,104,112,120},{128,136,144,152,1..., dimensions={0} | all-to-all | bytes 327680 | tf_op jit(solution)/shard_map/all_to_all | solution.py:46
  111.2 14.5 %all_to_all.42 = f32[8,40,128]{2,1,0:T(8,128)S(1)} all-to-all(f32[8,40,128]{2,1,0:T(8,128)S(1)} %broadcast_in_dim.56), channel_id=1, replica_groups={{0,64,128,192,256,320,384,448},{8,72,136,200,264,328,392,456},{16,80,14..., dimensions={0} | all-to-all | bytes 327680 | tf_op jit(solution)/shard_map/all_to_all | solution.py:46
  125.7 0.7 broadcast_in_dim.57
  126.4 6.3 %all-to-all-start.6 = ((f32[8,16,256]{2,1,0:T(8,128)}), f32[8,16,256]{2,1,0:T(8,128)S(1)}, u32[]{:S(2)}, u32[]{:S(2)}) async-start(f32[8,16,256]{2,1,0:T(8,128)} %broadcast_in_dim.57), calls=%async_computation.6 | async-start | bytes 262144 | tf_op jit(solution)/shard_map/all_to_all | solution.py:46
  132.7 0.6 slice_bitcast_fusion
  133.3 4.6 %all-to-all-done.6 = f32[8,16,256]{2,1,0:T(8,128)S(1)} async-done(((f32[8,16,256]{2,1,0:T(8,128)}), f32[8,16,256]{2,1,0:T(8,128)S(1)}, u32[]{:S(2)}, u32[]{:S(2)}) %all-to-all-start.6) | async-done | bytes 131104 | tf_op jit(solution)/shard_map/all_to_all | solution.py:46
  137.9 0.7 copy.14
  (26 shorter events, 0.1 us)
Async XLA Ops:
  0.6 9.0 %copy-start = (bf16[1024,128]{1,0:T(8,128)(2,1)S(1)}, bf16[1024,128]{1,0:T(8,128)(2,1)}, u32[]{:S(2)}) copy-start(bf16[1024,128]{1,0:T(8,128)(2,1)} %param.9) | copy-start | bytes 786436
  0.6 25.6 %collective-permute-start = (bf16[128,128,128]{2,1,0:T(8,128)(2,1)}, bf16[128,128,128]{2,1,0:T(8,128)(2,1)}, u32[]{:S(2)}, u32[]{:S(2)}) collective-permute-start(bf16[128,128,128]{2,1,0:T(8,128)(2,1)} %bitcast.21), channel_id=1, source_target_pairs={{0,4},{4,0},{8,12},{12,8},{16,20},{20,16},{24,28},{28,24},{32,36},... | collective-permute-start | bytes 12582920 | tf_op jit(solution)/shard_map/ppermute | solution.py:174
  26.3 21.4 %collective-permute-start.3 = (bf16[16,128,128]{2,1,0:T(8,128)(2,1)S(1)}, bf16[16,128,128]{2,1,0:T(8,128)(2,1)S(1)}, u32[]{:S(2)}, u32[]{:S(2)}) collective-permute-start(bf16[16,128,128]{2,1,0:T(8,128)(2,1)S(1)} %bitcast.24), channel_id=1, source_target_pairs={{0,128},{64,192},{128,256},{192,320},{256,384},{320,448},{384,0},{... | collective-permute-start | bytes 1572872 | tf_op jit(solution)/shard_map/ppermute | solution.py:51
  30.5 19.1 %collective-permute-start.4 = (bf16[16,128,128]{2,1,0:T(8,128)(2,1)S(1)}, bf16[16,128,128]{2,1,0:T(8,128)(2,1)S(1)}, u32[]{:S(2)}, u32[]{:S(2)}) collective-permute-start(bf16[16,128,128]{2,1,0:T(8,128)(2,1)S(1)} %bitcast.25), channel_id=1, source_target_pairs={{0,384},{64,448},{128,0},{192,64},{256,128},{320,192},{384,256},{4... | collective-permute-start | bytes 1572872 | tf_op jit(solution)/shard_map/ppermute | solution.py:51
  34.1 31.5 %collective-permute-start.1 = (bf16[16,128,128]{2,1,0:T(8,128)(2,1)S(1)}, bf16[16,128,128]{2,1,0:T(8,128)(2,1)S(1)}, u32[]{:S(2)}, u32[]{:S(2)}) collective-permute-start(bf16[16,128,128]{2,1,0:T(8,128)(2,1)S(1)} %bitcast.26), channel_id=1, source_target_pairs={{0,64},{64,128},{128,192},{192,256},{256,320},{320,384},{384,448},... | collective-permute-start | bytes 1572872 | tf_op jit(solution)/shard_map/ppermute | solution.py:51
  36.9 28.7 %collective-permute-start.2 = (bf16[16,128,128]{2,1,0:T(8,128)(2,1)S(1)}, bf16[16,128,128]{2,1,0:T(8,128)(2,1)S(1)}, u32[]{:S(2)}, u32[]{:S(2)}) collective-permute-start(bf16[16,128,128]{2,1,0:T(8,128)(2,1)S(1)} %bitcast.27), channel_id=1, source_target_pairs={{0,448},{64,0},{128,64},{192,128},{256,192},{320,256},{384,320},{4... | collective-permute-start | bytes 1572872 | tf_op jit(solution)/shard_map/ppermute | solution.py:51
  40.6 25.0 %collective-permute-start.5 = (bf16[16,128,128]{2,1,0:T(8,128)(2,1)S(1)}, bf16[16,128,128]{2,1,0:T(8,128)(2,1)}, u32[]{:S(2)}, u32[]{:S(2)}) collective-permute-start(bf16[16,128,128]{2,1,0:T(8,128)(2,1)S(1)} %bitcast.28), channel_id=1, source_target_pairs={{0,256},{64,320},{128,384},{192,448},{256,0},{320,64},{384,128},{4... | collective-permute-start | bytes 1572872 | tf_op jit(solution)/shard_map/ppermute | solution.py:51
  47.7 25.6 %collective-permute-start.6 = (bf16[16,128,128]{2,1,0:T(8,128)(2,1)S(1)}, bf16[16,128,128]{2,1,0:T(8,128)(2,1)S(1)}, u32[]{:S(2)}, u32[]{:S(2)}) collective-permute-start(bf16[16,128,128]{2,1,0:T(8,128)(2,1)S(1)} %collective-permute-done.3.b3), channel_id=1, source_target_pairs={{0,64},{64,128},{128,192},{192,256},{256,320},{320,384},{384,448},... | collective-permute-start | bytes 1572872 | tf_op jit(solution)/shard_map/ppermute | solution.py:51
  49.6 23.7 %collective-permute-start.7 = (bf16[16,128,128]{2,1,0:T(8,128)(2,1)S(1)}, bf16[16,128,128]{2,1,0:T(8,128)(2,1)}, u32[]{:S(2)}, u32[]{:S(2)}) collective-permute-start(bf16[16,128,128]{2,1,0:T(8,128)(2,1)S(1)} %collective-permute-done.4.b4), channel_id=1, source_target_pairs={{0,448},{64,0},{128,64},{192,128},{256,192},{320,256},{384,320},{4... | collective-permute-start | bytes 1572872 | tf_op jit(solution)/shard_map/ppermute | solution.py:51
  56.9 7.5 %all-to-all-start = ((s32[2,1,128]{2,1,0:T(1,128)}), s32[2,1,128]{2,1,0:T(1,128)S(1)}, u32[]{:S(2)}, u32[]{:S(2)}) async-start(s32[2,1,128]{2,1,0:T(1,128)} %broadcast_in_dim.53), calls=%async_computation | async-start | bytes 2048 | tf_op jit(solution)/shard_map/all_to_all | solution.py:187
  65.6 2.2 %copy-start.1 = (bf16[1,1,128,128,128]{4,3,2,1,0:T(8,128)(2,1)S(1)}, bf16[1,1,128,128,128]{4,3,2,1,0:T(8,128)(2,1)}, u32[]{:S(2)}) copy-start(bf16[1,1,128,128,128]{4,3,2,1,0:T(8,128)(2,1)} %param.13) | copy-start | bytes 12582916
  67.8 5.5 %copy-start.2 = (bf16[1,1,128,128,128]{4,3,2,1,0:T(8,128)(2,1)S(1)}, bf16[1,1,128,128,128]{4,3,2,1,0:T(8,128)(2,1)}, u32[]{:S(2)}) copy-start(bf16[1,1,128,128,128]{4,3,2,1,0:T(8,128)(2,1)} %param.13) | copy-start | bytes 12582916
  73.3 17.3 %copy-start.3 = (bf16[256,256]{1,0:T(8,128)(2,1)S(1)}, bf16[256,256]{1,0:T(8,128)(2,1)}, u32[]{:S(2)}) copy-start(bf16[256,256]{1,0:T(8,128)(2,1)} %cotangent.1) | copy-start | bytes 393220
  73.3 17.3 %copy-start.4 = (bf16[128,256]{1,0:T(8,128)(2,1)S(1)}, bf16[128,256]{1,0:T(8,128)(2,1)}, u32[]{:S(2)}) copy-start(bf16[128,256]{1,0:T(8,128)(2,1)} %weight.1) | copy-start | bytes 196612
  73.3 17.3 %copy-start.5 = (f32[256]{0:T(256)S(1)}, f32[256]{0:T(256)}, u32[]{:S(2)}) copy-start(f32[256]{0:T(256)} %param.11) | copy-start | bytes 3076
  126.4 11.5 %all-to-all-start.6 = ((f32[8,16,256]{2,1,0:T(8,128)}), f32[8,16,256]{2,1,0:T(8,128)S(1)}, u32[]{:S(2)}, u32[]{:S(2)}) async-start(f32[8,16,256]{2,1,0:T(8,128)} %broadcast_in_dim.57), calls=%async_computation.6 | async-start | bytes 262144 | tf_op jit(solution)/shard_map/all_to_all | solution.py:46

commit v5 on v4

v5 whole, which is shorter than its diff:
```python
import jax
import jax.numpy as jnp
from jax import lax
from jax.experimental import pallas as pl
from jax.experimental.pallas import tpu as pltpu
from jax.sharding import PartitionSpec as P

FIN = 128
HID = 256
TILE = 128
TR = 8
CT = 2
SIDE = 8
NARROW = 4
SLOTS = 128
BLOCK = SIDE * CT
STEP = 8
SEGMENTS = 8
EARLY = 5
LIST = 256
SPARE = TR
BF16 = jnp.bfloat16
F32 = jnp.float32
I32 = jnp.int32


def wide_index(z, y, core):
    return (z * SIDE + y) * 2 + core


RANGE = range(SIDE)
ALONG_Y = [[[wide_index(z, y, c) for y in RANGE] for z in RANGE] for c in (0, 1)]
ALONG_Z = [[[wide_index(z, y, c) for z in RANGE] for y in RANGE] for c in (0, 1)]
FIRST = ALONG_Y[0] + ALONG_Z[1]
SECOND = ALONG_Z[0] + ALONG_Y[1]
GROUPS_Y = ALONG_Y[0] + ALONG_Y[1]
GROUPS_Z = ALONG_Z[0] + ALONG_Z[1]
COLUMN = [
    [wide_index(z, y, c) * NARROW + x for c in (0, 1) for x in range(NARROW)] for z in RANGE for y in RANGE
]
OTHER_CORE = [(i, i ^ 1) for i in range(2 * SIDE * SIDE)]


def to_all(block, axes, groups):
    return lax.all_to_all(jnp.broadcast_to(block[None], (8, *block.shape)), axes, 0, 0, axis_index_groups=groups)


def shift(block, by):
    pairs = [(line[i], line[(i + (by if i % 2 == 0 else -by)) % SIDE]) for line in SECOND for i in RANGE]
    return lax.ppermute(block, "wide", pairs)


def column(vector):
    n = vector.shape[1]
    eye = lax.broadcasted_iota(I32, (n, n), 0) == lax.broadcasted_iota(I32, (n, n), 1)
    return jnp.sum(jnp.where(eye, vector, 0), axis=1, keepdims=True)


def make_list(place, slots):
    core, at = place[0], place[1]
    code, pick = slots[0:1], slots[1:2]
    source = lax.shift_right_arithmetic(code, 3)
    valid = (code >= 0) & ((source & 1) == core)
    rows = lax.broadcasted_iota(I32, (SLOTS, SLOTS), 0)
    kinds = lax.broadcasted_iota(I32, (SLOTS, SLOTS), 1)
    lanes = lax.broadcasted_iota(I32, (1, SLOTS), 1)
    picked = jnp.sum(jnp.where(rows == source, column(pick), 0), axis=0, keepdims=True)
    z, y = lax.shift_right_arithmetic(source, 4), lax.shift_right_arithmetic(source, 1) & 7
    along, across = jnp.where(core == 0, z, y), jnp.where(core == 0, y, z)
    tile = across * 2 + picked
    ahead = jnp.where(at % 2 == 0, along - at, at - along) & 7
    segment = jnp.zeros_like(ahead)
    for kind, distance in enumerate((1, 7, 6, 2, 3, 5, 4)):
        segment = jnp.where(ahead == distance, kind + 1, segment)
    segment = jnp.where(valid, segment, SEGMENTS)
    entry = lanes + SLOTS * tile + SLOTS * BLOCK * (code & 7)
    segments = column(segment)
    sizes = jnp.sum((segments == kinds).astype(I32), axis=0, keepdims=True)
    sizes = lax.shift_right_arithmetic(sizes + STEP - 1, 3) * STEP
    size = column(jnp.where(lanes < SEGMENTS, sizes, 0))
    start = jnp.sum(jnp.where(rows < kinds, size, 0), axis=0, keepdims=True)
    earlier = (segments == segment) & (rows < kinds)
    place_of = jnp.sum(earlier.astype(I32), axis=0, keepdims=True)
    place_of += jnp.sum(jnp.where(rows == segment, column(start), 0), axis=0, keepdims=True)
    place_of = jnp.where(valid, place_of, LIST)
    spare = SLOTS * BLOCK * SPARE
    hit = column(place_of) == lax.broadcasted_iota(I32, (SLOTS, LIST), 1)
    entries = spare + jnp.sum(jnp.where(hit, column(entry) - spare, 0), axis=0, keepdims=True)
    return entries, lax.shift_right_arithmetic(start, 3)


def add_products(entries, starts, owner, values, blocks, first, acc):
    for i, block in enumerate(blocks):

        def step(k, carry, block=block):
            done = []
            for u in range(STEP):
                e = entries[owner, k * STEP + u]
                tile, row = (e >> 7) & (BLOCK - 1), e >> 11
                done.append((row, jnp.dot(values[e & (SLOTS - 1)], block[tile], preferred_element_type=F32)))
            for row, product in done:
                acc[row] += product
            return carry

        lax.fori_loop(starts[owner, first + i], starts[owner, first + i + 1], step, 0)


def own_kernel(place, slots, own, other, b0, b1, b2, b3, b4, acc, own_here, other_here, lists, starts, entries, bounds, sems):
    copies = [
        pltpu.make_async_copy(own, own_here, sems.at[0]),
        pltpu.make_async_copy(other, other_here, sems.at[1]),
    ]
    copies[0].start()
    copies[1].start()
    lists[...], starts[...] = make_list(place, slots[...])
    scalars = [
        pltpu.make_async_copy(lists, entries, sems.at[2]),
        pltpu.make_async_copy(starts, bounds, sems.at[3]),
    ]
    scalars[0].start()
    scalars[1].start()
    acc[...] = jnp.zeros_like(acc)
    scalars[0].wait()
    scalars[1].wait()
    copies[0].wait()
    add_products(entries, bounds, 0, own_here, (b0, b1, b2, b3, b4), 0, acc)
    copies[1].wait()


def other_kernel(place, slots, other, own_list, own_start, b0, b1, b2, b3, b4, acc, lists, starts, entries, bounds, sems):
    lists[0:1, :], starts[0:1, :] = own_list[...], own_start[...]
    lists[1:2, :], starts[1:2, :] = make_list(place, slots[...])
    scalars = [
        pltpu.make_async_copy(lists, entries, sems.at[0]),
        pltpu.make_async_copy(starts, bounds, sems.at[1]),
    ]
    scalars[0].start()
    scalars[1].start()
    acc[...] = jnp.zeros_like(acc)
    scalars[0].wait()
    scalars[1].wait()
    add_products(entries, bounds, 1, other, (b0, b1, b2, b3, b4), 0, acc)


def late_kernel(place, lists, starts, own, other, b5, b6, b7, own_before, other_before, out, own_acc, other_acc):
    own_acc[...] = own_before[...]
    other_acc[...] = other_before[...]
    add_products(lists, starts, 0, own, (b5, b6, b7), EARLY, own_acc)
    add_products(lists, starts, 1, other, (b5, b6, b7), EARLY, other_acc)
    core = place[0]
    out[core] = own_acc[0:TR].astype(BF16)
    out[1 - core] = other_acc[0:TR].astype(BF16)


def dense_kernel(parts, weight, bias, cotangent, hidden, grads):
    total = parts[0].astype(F32)
    for i in range(1, 8):
        total += parts[i].astype(F32)
    aggregated = total.astype(BF16)
    preact = jnp.dot(aggregated, weight[...], preferred_element_type=F32) + bias[...]
    sig = jax.nn.sigmoid(preact)
    hidden[...] = (preact * sig).astype(BF16)
    dpreact = cotangent[...].astype(F32) * (sig * (1.0 + preact * (1.0 - sig)))
    weight_part = lax.dot_general(
        aggregated, dpreact.astype(BF16), (((0,), (0,)), ((), ())), preferred_element_type=F32
    ).astype(BF16)
    bias_part = jnp.sum(dpreact, axis=0, keepdims=True)
    rows = lax.broadcasted_iota(I32, (16, TILE), 0)
    left = jnp.broadcast_to(bias_part[:, :TILE], (16, TILE))
    right = jnp.broadcast_to(bias_part[:, TILE:], (16, TILE))
    biases = jnp.where(rows == 0, left, jnp.where(rows == 1, right, 0.0)).astype(BF16)
    for i in range(8):
        grads[i, 0:16, :] = weight_part[16 * i : 16 * i + 16, :TILE]
        grads[i, 16:32, :] = weight_part[16 * i : 16 * i + 16, TILE:]
        grads[i, 32:48, :] = biases


VMEM = pl.BlockSpec(memory_space=pltpu.VMEM)
SMEM = pl.BlockSpec(memory_space=pltpu.SMEM)
HBM = pl.BlockSpec(memory_space=pltpu.HBM)


def total(shares):
    return jnp.sum(shares.astype(F32), axis=0)


def local(features, weight, bias, cotangent, tile_values, tile_row, tile_source, tile_count, pick):
    index = lax.axis_index("wide")
    core = lax.rem(index, 2)
    both = ("wide", "narrow")
    mine = lax.dynamic_slice_in_dim(features, lax.axis_index("narrow") * (CT * TILE), CT * TILE, 0)
    own_values = tile_values[0, 0]
    other_values = lax.ppermute(own_values, "wide", OTHER_CORE)
    own = to_all(mine, "wide", FIRST).reshape(BLOCK, TILE, FIN)
    own, other_values = lax.optimization_barrier((own, other_values))
    two_a, two_b = shift(own, 2), shift(own, -2)
    one_a, one_b = shift(own, 1), shift(own, -1)
    three_a, three_b = shift(two_a, 1), shift(two_b, -1)
    four = shift(two_a, 2)

    live = jnp.arange(SLOTS, dtype=I32) < tile_count[0, 0]
    code = jnp.where(live, tile_row[0, 0] + TR * tile_source[0, 0], -1)
    first_row = jnp.arange(2, dtype=I32)[:, None] == 0
    slots = jnp.where(first_row, code[None, :], pick[0])
    other_slots = lax.ppermute(slots, "wide", OTHER_CORE)
    place = jnp.stack([core, jnp.where(core == 0, index // 16, lax.rem(index // 2, 8))])

    sums = jax.ShapeDtypeStruct((TR + 1, TILE, FIN), F32)
    here = jax.ShapeDtypeStruct(own_values.shape, BF16)
    lists = lambda n: jax.ShapeDtypeStruct((n, LIST), I32)
    starts = lambda n: jax.ShapeDtypeStruct((n, SLOTS), I32)
    own_sums, own_here, other_here, own_list, own_start = pl.pallas_call(
        own_kernel,
        out_shape=(sums, here, here, lists(1), starts(1)),
        in_specs=[SMEM, VMEM] + [HBM] * 2 + [VMEM] * 5,
        out_specs=(VMEM,) * 5,
        scratch_shapes=[
            pltpu.SMEM((1, LIST), I32),
            pltpu.SMEM((1, SLOTS), I32),
            pltpu.SemaphoreType.DMA((4,)),
        ],
        compiler_params=pltpu.CompilerParams(vmem_limit_bytes=42 << 20),
        cost_estimate=pl.CostEstimate(flops=SLOTS * TILE**3, bytes_accessed=8 << 20, transcendentals=0),
        name="own",
    )(place, slots, own_values, other_values, own, one_a, one_b, two_a, two_b)
    other_sums, all_lists, all_starts = pl.pallas_call(
        other_kernel,
        out_shape=(sums, lists(2), starts(2)),
        in_specs=[SMEM] + [VMEM] * 9,
        out_specs=(VMEM,) * 3,
        scratch_shapes=[
            pltpu.SMEM((2, LIST), I32),
            pltpu.SMEM((2, SLOTS), I32),
            pltpu.SemaphoreType.DMA((2,)),
        ],
        compiler_params=pltpu.CompilerParams(vmem_limit_bytes=16 << 20),
        cost_estimate=pl.CostEstimate(flops=SLOTS * TILE**3, bytes_accessed=8 << 20, transcendentals=0),
        name="other",
    )(place, other_slots, other_here, own_list, own_start, own, one_a, one_b, two_a, two_b)
    partial = pl.pallas_call(
        late_kernel,
        out_shape=jax.ShapeDtypeStruct((2, TR, TILE, FIN), BF16),
        in_specs=[SMEM] * 3 + [VMEM] * 7,
        out_specs=VMEM,
        scratch_shapes=[pltpu.VMEM(sums.shape, F32), pltpu.VMEM(sums.shape, F32)],
        compiler_params=pltpu.CompilerParams(vmem_limit_bytes=16 << 20),
        cost_estimate=pl.CostEstimate(flops=SLOTS * TILE**3, bytes_accessed=8 << 20, transcendentals=0),
        name="late",
    )(place, all_lists, all_starts, own_here, other_here, three_a, three_b, four, own_sums, other_sums)

    rows = TR * TILE // NARROW
    parts = lax.all_to_all(partial.reshape(8, rows, FIN), both, 0, 0, axis_index_groups=COLUMN)
    hidden, grads = pl.pallas_call(
        dense_kernel,
        out_shape=(
            jax.ShapeDtypeStruct((rows, HID), BF16),
            jax.ShapeDtypeStruct((8, 48, TILE), BF16),
        ),
        in_specs=[VMEM] * 4,
        out_specs=(VMEM, VMEM),
        compiler_params=pltpu.CompilerParams(vmem_limit_bytes=16 << 20),
        cost_estimate=pl.CostEstimate(flops=4 * rows * FIN * HID, bytes_accessed=2 << 20, transcendentals=rows * HID),
        name="dense",
    )(parts, weight, bias.reshape(1, HID), cotangent)

    share = total(lax.all_to_all(grads, both, 0, 0, axis_index_groups=COLUMN))[:40]
    share = total(to_all(share, "wide", GROUPS_Y))
    share = total(to_all(share, "wide", GROUPS_Z))
    chunk = jnp.concatenate([share[0:16], share[16:32]], axis=1)
    grad_weight = to_all(chunk, both, COLUMN).reshape(FIN, HID)
    return hidden, grad_weight, share[32:34].reshape(HID)


def solution(mesh):
    placed = (
        P("wide", None),
        P(),
        P(),
        P(("wide", "narrow"), None),
        P("wide", "narrow", None, None, None),
        P("wide", "narrow", None),
        P("wide", "narrow", None),
        P("wide", "narrow"),
        P("wide", "narrow", None),
    )
    return jax.shard_map(
        local,
        mesh=mesh,
        in_specs=placed,
        out_specs=(P(("wide", "narrow"), None), P(), P()),
        check_vma=False,
    )
```

time: 139 us -> 134 us (0.964)
  blocking collectives: 65.5 us -> 62.5 us
  local copies, waits for them, and re-layouts: 4.78 us -> 2.02 us
    all_to_all x1 -> x0, starting transfers between devices: 6.55 us -> none  [local(): lax.all_to_all(jnp.broadcast_to(code, (2, SLOTS)), 'wide', 0, 0, axis_ind...]
    ppermute x0 -> x1, starting transfers between devices: none -> 5.33 us  [local(): other_slots = lax.ppermute(slots, 'wide', OTHER_CORE)]
    all_to_all x3, blocking collectives: 42.5 us -> 40.3 us  [to_all(): lax.all_to_all(jnp.broadcast_to(block[None], (8, *block.shape)), axes, 0,...]
    unnamed x13 -> x9, local copies, waits for them, and re-layouts: 2.87 us -> 0.68 us
    ppermute x7, starting transfers between devices: 27.8 us -> 29.5 us  [shift(): return lax.ppermute(block, 'wide', pairs)]
  transfers between devices with their start and end apart: 10 -> 10, of which waited for: 2 -> 1; matrix products, arithmetic and copies ran while one was open for 2% -> 2% of each run, Pallas kernels for 5% -> 6%
where the time goes in v5:
time: 134 us; the launch traced here: 133 us
  blocking collectives  62.5 us (47%)
  starting transfers between devices  50.1 us (37%)
  Pallas kernels  11.1 us (8%)
  waiting for transfers between devices  4.62 us (3%)
  local copies, waits for them, and re-layouts  2.02 us (2%)
  between operations  1.59 us (1%)
  other arithmetic  1.54 us (1%)
    all_to_all x3, blocking collectives, to_all(): lax.all_to_all(jnp.broadcast_to(block[None], (8, *block.shape)), axes, 0,...  40.3 us
    ppermute x7, starting transfers between devices, shift(): return lax.ppermute(block, 'wide', pairs)  29.5 us
    all_to_all x1, blocking collectives, local(): lax.all_to_all(partial.reshape(8, rows, FIN), both, 0, 0, axis_index_grou...  14.1 us
    ppermute x1, starting transfers between devices, local(): other_values = lax.ppermute(own_values, 'wide', OTHER_CORE)  8.92 us
    all_to_all x1, blocking collectives, local(): lax.all_to_all(grads, both, 0, 0, axis_index_groups=COLUMN)  8.22 us
    all_to_all x1, starting transfers between devices, to_all(): lax.all_to_all(jnp.broadcast_to(block[None], (8, *block.shape)), axes, 0,...  6.34 us
    ppermute x1, starting transfers between devices, local(): other_slots = lax.ppermute(slots, 'wide', OTHER_CORE)  5.33 us
    all_to_all x1, waiting for transfers between devices, to_all(): lax.all_to_all(jnp.broadcast_to(block[None], (8, *block.shape)), axes, 0,...  4.59 us
  transfers between devices with their start and end apart: 10, of which 1 were waited for; matrix products, arithmetic and copies ran while one was open for 2% of the time, Pallas kernels for 6%

profile of v5, /device:TPU:1, one launch (start us, length us, event | category | flops | bytes accessed | tf_op | source)
XLA Modules:
  0.0 133.4 jit_solution(12117252474909304350)
XLA Ops:
  0.6 0.0 copy-start
  0.6 8.9 %collective-permute-start.1 = (bf16[128,128,128]{2,1,0:T(8,128)(2,1)}, bf16[128,128,128]{2,1,0:T(8,128)(2,1)}, u32[]{:S(2)}, u32[]{:S(2)}) collective-permute-start(bf16[128,128,128]{2,1,0:T(8,128)(2,1)} %bitcast.22), channel_id=1, source_target_pairs={{0,4},{4,0},{8,12},{12,8},{16,20},{20,16},{24,28},{28,24},{32,36},... | collective-permute-start | bytes 12582920 | tf_op jit(solution)/shard_map/ppermute | solution.py:193
  9.6 0.1 broadcast_in_dim.61
  9.7 16.6 %all_to_all.30 = bf16[8,256,128]{2,1,0:T(8,128)(2,1)S(1)} all-to-all(bf16[8,256,128]{2,1,0:T(8,128)(2,1)S(1)} %broadcast_in_dim.61), channel_id=1, replica_groups={{0,8,16,24,32,40,48,56},{64,72,80,88,96,104,112,120},{128,136,144,152,1..., dimensions={0} | all-to-all | bytes 1048576 | tf_op jit(solution)/shard_map/all_to_all | solution.py:45
  26.3 0.0 collective-permute-done.1.other
  26.3 4.2 %collective-permute-start.4 = (bf16[16,128,128]{2,1,0:T(8,128)(2,1)S(1)}, bf16[16,128,128]{2,1,0:T(8,128)(2,1)S(1)}, u32[]{:S(2)}, u32[]{:S(2)}) collective-permute-start(bf16[16,128,128]{2,1,0:T(8,128)(2,1)S(1)} %bitcast.14), channel_id=1, source_target_pairs={{0,128},{64,448},{128,256},{192,64},{256,384},{320,192},{384,0},{4... | collective-permute-start | bytes 1572872 | tf_op jit(solution)/shard_map/ppermute | solution.py:50
  30.5 3.6 %collective-permute-start.5 = (bf16[16,128,128]{2,1,0:T(8,128)(2,1)S(1)}, bf16[16,128,128]{2,1,0:T(8,128)(2,1)S(1)}, u32[]{:S(2)}, u32[]{:S(2)}) collective-permute-start(bf16[16,128,128]{2,1,0:T(8,128)(2,1)S(1)} %bitcast.15), channel_id=1, source_target_pairs={{0,384},{64,192},{128,0},{192,320},{256,128},{320,448},{384,256},{... | collective-permute-start | bytes 1572872 | tf_op jit(solution)/shard_map/ppermute | solution.py:50
  34.1 2.3 %collective-permute-start.2 = (bf16[16,128,128]{2,1,0:T(8,128)(2,1)S(1)}, bf16[16,128,128]{2,1,0:T(8,128)(2,1)S(1)}, u32[]{:S(2)}, u32[]{:S(2)}) collective-permute-start(bf16[16,128,128]{2,1,0:T(8,128)(2,1)S(1)} %bitcast.16), channel_id=1, source_target_pairs={{0,64},{64,0},{128,192},{192,128},{256,320},{320,256},{384,448},{4... | collective-permute-start | bytes 1572872 | tf_op jit(solution)/shard_map/ppermute | solution.py:50
  36.5 4.3 %collective-permute-start.3 = (bf16[16,128,128]{2,1,0:T(8,128)(2,1)S(1)}, bf16[16,128,128]{2,1,0:T(8,128)(2,1)S(1)}, u32[]{:S(2)}, u32[]{:S(2)}) collective-permute-start(bf16[16,128,128]{2,1,0:T(8,128)(2,1)S(1)} %bitcast.17), channel_id=1, source_target_pairs={{0,448},{64,128},{128,64},{192,256},{256,192},{320,384},{384,320},... | collective-permute-start | bytes 1572872 | tf_op jit(solution)/shard_map/ppermute | solution.py:50
  40.8 5.4 %collective-permute-start.6 = (bf16[16,128,128]{2,1,0:T(8,128)(2,1)S(1)}, bf16[16,128,128]{2,1,0:T(8,128)(2,1)S(1)}, u32[]{:S(2)}, u32[]{:S(2)}) collective-permute-start(bf16[16,128,128]{2,1,0:T(8,128)(2,1)S(1)} %collective-permute-done.4.b3), channel_id=1, source_target_pairs={{0,64},{64,0},{128,192},{192,128},{256,320},{320,256},{384,448},{4... | collective-permute-start | bytes 1572872 | tf_op jit(solution)/shard_map/ppermute | solution.py:50
  46.2 3.4 %collective-permute-start.8 = (bf16[16,128,128]{2,1,0:T(8,128)(2,1)S(1)}, bf16[16,128,128]{2,1,0:T(8,128)(2,1)S(1)}, u32[]{:S(2)}, u32[]{:S(2)}) collective-permute-start(bf16[16,128,128]{2,1,0:T(8,128)(2,1)S(1)} %collective-permute-done.4.b3), channel_id=1, source_target_pairs={{0,128},{64,448},{128,256},{192,64},{256,384},{320,192},{384,0},{4... | collective-permute-start | bytes 1572872 | tf_op jit(solution)/shard_map/ppermute | solution.py:50
  49.7 6.3 %collective-permute-start.7 = (bf16[16,128,128]{2,1,0:T(8,128)(2,1)S(1)}, bf16[16,128,128]{2,1,0:T(8,128)(2,1)S(1)}, u32[]{:S(2)}, u32[]{:S(2)}) collective-permute-start(bf16[16,128,128]{2,1,0:T(8,128)(2,1)S(1)} %collective-permute-done.5.b4), channel_id=1, source_target_pairs={{0,448},{64,128},{128,64},{192,256},{256,192},{320,384},{384,320},... | collective-permute-start | bytes 1572872 | tf_op jit(solution)/shard_map/ppermute | solution.py:50
  55.9 0.1 pad_add_fusion.place
  56.6 0.7 compare_select_fusion
  57.3 0.7 broadcast_select_fusion.slots
  58.1 5.3 %collective-permute-start = (s32[2,128]{1,0:T(2,128)S(1)}, s32[2,128]{1,0:T(2,128)S(1)}, u32[]{:S(2)}, u32[]{:S(2)}) collective-permute-start(s32[2,128]{1,0:T(2,128)S(1)} %broadcast_select_fusion.slots), channel_id=1, source_target_pairs={{0,4},{4,0},{8,12},{12,8},{16,20},{20,16},{24,28},{28,24},{32,36},... | collective-permute-start | bytes 3080 | tf_op jit(solution)/shard_map/ppermute | solution.py:205
  63.4 4.5 %own.1 = (f32[9,128,128]{2,1,0:T(8,128)S(1)}, bf16[128,128,128]{2,1,0:T(8,128)(2,1)S(1)}, bf16[128,128,128]{2,1,0:T(8,128)(2,1)S(1)}, s32[1,256]{1,0:T(1,128)S(1)}, s32[1,128]{1,0:T(1,128)S(1)}) custom-call(s32[2]{0:T(128)S(1)} %pad_add_fusion.place, s32[2,128]{1,0:T(2,128)S(1)} %broadcast_select_fusion.slots, bf16[128,128,128]{2,1,0:T(8,128)(2,1)} %bitcast.23, ...), custom_call_target="tpu_custom_call" | custom-call | flops 268435456 | bytes 8388608 | tf_op jit(solution)/shard_map/own/pallas_call | solution.py:212
  67.9 2.9 %other.1 = (f32[9,128,128]{2,1,0:T(8,128)S(1)}, s32[2,256]{1,0:T(2,128)S(1)}, s32[2,128]{1,0:T(2,128)S(1)}) custom-call(s32[2]{0:T(128)S(1)} %pad_add_fusion.place, s32[2,128]{1,0:T(2,128)S(1)} %collective-permute-done.slots, bf16[128,128,128]{2,1,0:T(8,128)(2,1)S(1)} %get-tuple-element.17.other, s32[1,256]{1,0:T(1,128)S(1)} %get-tuple-element.18.own_list, ...), custom_call_target="tpu_custom_call" | custom-call | flops 268435456 | bytes 8388608 | tf_op jit(solution)/shard_map/other/pallas_call | solution.py:226
  70.8 0.0 copy-start.1
  70.8 0.0 copy-start.2
  70.8 0.0 copy-start.3
  70.8 2.8 %late.1 = bf16[2,8,128,128]{3,2,1,0:T(8,128)(2,1)S(1)} custom-call(s32[2]{0:T(128)S(1)} %pad_add_fusion.place, s32[2,256]{1,0:T(2,128)S(1)} %get-tuple-element.20.lists, s32[2,128]{1,0:T(2,128)S(1)} %get-tuple-element.21.starts, bf16[128,128,128]{2,1,0:T(8,128)(2,1)S(1)} %get-tuple-element.22.own, bf16[128,128,128]{2,1,0:T(8,128)(2,1)S(1)} %get-tuple-element.17.other, ...), custom_call_target="tpu_custom_call" | custom-call | flops 268435456 | bytes 8388608 | tf_op jit(solution)/shard_map/late/pallas_call | solution.py:240
  73.7 14.1 %all_to_all.31.parts = bf16[8,256,128]{2,1,0:T(8,128)(2,1)S(1)} all-to-all(bf16[8,256,128]{2,1,0:T(8,128)(2,1)S(1)} %bitcast.20), channel_id=1, replica_groups={{0,1,2,3,4,5,6,7},{8,9,10,11,12,13,14,15},{16,17,18,19,20,21,22,23},{24..., dimensions={0} | all-to-all | bytes 1048576 | tf_op jit(solution)/shard_map/all_to_all | solution.py:252
  87.7 0.9 dense.1
  88.6 8.2 %all_to_all.32 = bf16[8,48,128]{2,1,0:T(8,128)(2,1)S(1)} all-to-all(bf16[8,48,128]{2,1,0:T(8,128)(2,1)S(1)} %get-tuple-element.26), channel_id=1, replica_groups={{0,1,2,3,4,5,6,7},{8,9,10,11,12,13,14,15},{16,17,18,19,20,21,22,23},{24..., dimensions={0} | all-to-all | bytes 196608 | tf_op jit(solution)/shard_map/all_to_all | solution.py:266
  96.9 11.3 %all_to_all.33 = f32[8,40,128]{2,1,0:T(8,128)S(1)} all-to-all(f32[8,40,128]{2,1,0:T(8,128)S(1)} %broadcast_in_dim.62), channel_id=1, replica_groups={{0,8,16,24,32,40,48,56},{64,72,80,88,96,104,112,120},{128,136,144,152,1..., dimensions={0} | all-to-all | bytes 327680 | tf_op jit(solution)/shard_map/all_to_all | solution.py:45
  108.2 12.4 %all_to_all.34 = f32[8,40,128]{2,1,0:T(8,128)S(1)} all-to-all(f32[8,40,128]{2,1,0:T(8,128)S(1)} %broadcast_in_dim.63), channel_id=1, replica_groups={{0,64,128,192,256,320,384,448},{8,72,136,200,264,328,392,456},{16,80,14..., dimensions={0} | all-to-all | bytes 327680 | tf_op jit(solution)/shard_map/all_to_all | solution.py:45
  120.6 0.7 broadcast_in_dim.64
  121.3 6.3 %all-to-all-start.5 = ((f32[8,16,256]{2,1,0:T(8,128)}), f32[8,16,256]{2,1,0:T(8,128)S(1)}, u32[]{:S(2)}, u32[]{:S(2)}) async-start(f32[8,16,256]{2,1,0:T(8,128)} %broadcast_in_dim.64), calls=%async_computation.5 | async-start | bytes 262144 | tf_op jit(solution)/shard_map/all_to_all | solution.py:45
  127.6 0.6 slice_bitcast_fusion
  128.2 4.6 %all-to-all-done.5 = f32[8,16,256]{2,1,0:T(8,128)S(1)} async-done(((f32[8,16,256]{2,1,0:T(8,128)}), f32[8,16,256]{2,1,0:T(8,128)S(1)}, u32[]{:S(2)}, u32[]{:S(2)}) %all-to-all-start.5) | async-done | bytes 131104 | tf_op jit(solution)/shard_map/all_to_all | solution.py:45
  132.8 0.7 copy.14
  (22 shorter events, 0.1 us)
Async XLA Ops:
  0.6 9.0 %copy-start = (bf16[1024,128]{1,0:T(8,128)(2,1)S(1)}, bf16[1024,128]{1,0:T(8,128)(2,1)}, u32[]{:S(2)}) copy-start(bf16[1024,128]{1,0:T(8,128)(2,1)} %param.9) | copy-start | bytes 786436
  0.6 25.6 %collective-permute-start.1 = (bf16[128,128,128]{2,1,0:T(8,128)(2,1)}, bf16[128,128,128]{2,1,0:T(8,128)(2,1)}, u32[]{:S(2)}, u32[]{:S(2)}) collective-permute-start(bf16[128,128,128]{2,1,0:T(8,128)(2,1)} %bitcast.22), channel_id=1, source_target_pairs={{0,4},{4,0},{8,12},{12,8},{16,20},{20,16},{24,28},{28,24},{32,36},... | collective-permute-start | bytes 12582920 | tf_op jit(solution)/shard_map/ppermute | solution.py:193
  26.3 14.5 %collective-permute-start.4 = (bf16[16,128,128]{2,1,0:T(8,128)(2,1)S(1)}, bf16[16,128,128]{2,1,0:T(8,128)(2,1)S(1)}, u32[]{:S(2)}, u32[]{:S(2)}) collective-permute-start(bf16[16,128,128]{2,1,0:T(8,128)(2,1)S(1)} %bitcast.14), channel_id=1, source_target_pairs={{0,128},{64,448},{128,256},{192,64},{256,384},{320,192},{384,0},{4... | collective-permute-start | bytes 1572872 | tf_op jit(solution)/shard_map/ppermute | solution.py:50
  30.5 19.1 %collective-permute-start.5 = (bf16[16,128,128]{2,1,0:T(8,128)(2,1)S(1)}, bf16[16,128,128]{2,1,0:T(8,128)(2,1)S(1)}, u32[]{:S(2)}, u32[]{:S(2)}) collective-permute-start(bf16[16,128,128]{2,1,0:T(8,128)(2,1)S(1)} %bitcast.15), channel_id=1, source_target_pairs={{0,384},{64,192},{128,0},{192,320},{256,128},{320,448},{384,256},{... | collective-permute-start | bytes 1572872 | tf_op jit(solution)/shard_map/ppermute | solution.py:50
  34.1 23.9 %collective-permute-start.2 = (bf16[16,128,128]{2,1,0:T(8,128)(2,1)S(1)}, bf16[16,128,128]{2,1,0:T(8,128)(2,1)S(1)}, u32[]{:S(2)}, u32[]{:S(2)}) collective-permute-start(bf16[16,128,128]{2,1,0:T(8,128)(2,1)S(1)} %bitcast.16), channel_id=1, source_target_pairs={{0,64},{64,0},{128,192},{192,128},{256,320},{320,256},{384,448},{4... | collective-permute-start | bytes 1572872 | tf_op jit(solution)/shard_map/ppermute | solution.py:50
  36.5 26.9 %collective-permute-start.3 = (bf16[16,128,128]{2,1,0:T(8,128)(2,1)S(1)}, bf16[16,128,128]{2,1,0:T(8,128)(2,1)S(1)}, u32[]{:S(2)}, u32[]{:S(2)}) collective-permute-start(bf16[16,128,128]{2,1,0:T(8,128)(2,1)S(1)} %bitcast.17), channel_id=1, source_target_pairs={{0,448},{64,128},{128,64},{192,256},{256,192},{320,384},{384,320},... | collective-permute-start | bytes 1572872 | tf_op jit(solution)/shard_map/ppermute | solution.py:50
  40.8 30.0 %collective-permute-start.6 = (bf16[16,128,128]{2,1,0:T(8,128)(2,1)S(1)}, bf16[16,128,128]{2,1,0:T(8,128)(2,1)S(1)}, u32[]{:S(2)}, u32[]{:S(2)}) collective-permute-start(bf16[16,128,128]{2,1,0:T(8,128)(2,1)S(1)} %collective-permute-done.4.b3), channel_id=1, source_target_pairs={{0,64},{64,0},{128,192},{192,128},{256,320},{320,256},{384,448},{4... | collective-permute-start | bytes 1572872 | tf_op jit(solution)/shard_map/ppermute | solution.py:50
  46.2 24.6 %collective-permute-start.8 = (bf16[16,128,128]{2,1,0:T(8,128)(2,1)S(1)}, bf16[16,128,128]{2,1,0:T(8,128)(2,1)S(1)}, u32[]{:S(2)}, u32[]{:S(2)}) collective-permute-start(bf16[16,128,128]{2,1,0:T(8,128)(2,1)S(1)} %collective-permute-done.4.b3), channel_id=1, source_target_pairs={{0,128},{64,448},{128,256},{192,64},{256,384},{320,192},{384,0},{4... | collective-permute-start | bytes 1572872 | tf_op jit(solution)/shard_map/ppermute | solution.py:50
  49.7 21.1 %collective-permute-start.7 = (bf16[16,128,128]{2,1,0:T(8,128)(2,1)S(1)}, bf16[16,128,128]{2,1,0:T(8,128)(2,1)S(1)}, u32[]{:S(2)}, u32[]{:S(2)}) collective-permute-start(bf16[16,128,128]{2,1,0:T(8,128)(2,1)S(1)} %collective-permute-done.5.b4), channel_id=1, source_target_pairs={{0,448},{64,128},{128,64},{192,256},{256,192},{320,384},{384,320},... | collective-permute-start | bytes 1572872 | tf_op jit(solution)/shard_map/ppermute | solution.py:50
  58.1 9.8 %collective-permute-start = (s32[2,128]{1,0:T(2,128)S(1)}, s32[2,128]{1,0:T(2,128)S(1)}, u32[]{:S(2)}, u32[]{:S(2)}) collective-permute-start(s32[2,128]{1,0:T(2,128)S(1)} %broadcast_select_fusion.slots), channel_id=1, source_target_pairs={{0,4},{4,0},{8,12},{12,8},{16,20},{20,16},{24,28},{28,24},{32,36},... | collective-permute-start | bytes 3080 | tf_op jit(solution)/shard_map/ppermute | solution.py:205
  70.8 16.9 %copy-start.1 = (bf16[256,256]{1,0:T(8,128)(2,1)S(1)}, bf16[256,256]{1,0:T(8,128)(2,1)}, u32[]{:S(2)}) copy-start(bf16[256,256]{1,0:T(8,128)(2,1)} %cotangent.1) | copy-start | bytes 393220
  70.8 16.9 %copy-start.2 = (bf16[128,256]{1,0:T(8,128)(2,1)S(1)}, bf16[128,256]{1,0:T(8,128)(2,1)}, u32[]{:S(2)}) copy-start(bf16[128,256]{1,0:T(8,128)(2,1)} %weight.1) | copy-start | bytes 196612
  70.8 16.9 %copy-start.3 = (f32[256]{0:T(256)S(1)}, f32[256]{0:T(256)}, u32[]{:S(2)}) copy-start(f32[256]{0:T(256)} %param.11) | copy-start | bytes 3076
  121.3 11.5 %all-to-all-start.5 = ((f32[8,16,256]{2,1,0:T(8,128)}), f32[8,16,256]{2,1,0:T(8,128)S(1)}, u32[]{:S(2)}, u32[]{:S(2)}) async-start(f32[8,16,256]{2,1,0:T(8,128)} %broadcast_in_dim.64), calls=%async_computation.5 | async-start | bytes 262144 | tf_op jit(solution)/shard_map/all_to_all | solution.py:45

commit v6 on v5

--- a/solution.py
+++ b/solution.py
@@ -33,16 +33,27 @@
 ALONG_Z = [[[wide_index(z, y, c) for z in RANGE] for y in RANGE] for c in (0, 1)]
 FIRST = ALONG_Y[0] + ALONG_Z[1]
 SECOND = ALONG_Z[0] + ALONG_Y[1]
-GROUPS_Y = ALONG_Y[0] + ALONG_Y[1]
-GROUPS_Z = ALONG_Z[0] + ALONG_Z[1]
 COLUMN = [
     [wide_index(z, y, c) * NARROW + x for c in (0, 1) for x in range(NARROW)] for z in RANGE for y in RANGE
 ]
+PIECES = 16
+NEAR = [
+    [wide_index(z, 2 * k + j, c) * NARROW + x for j in (0, 1) for c in (0, 1) for x in range(NARROW)]
+    for z in RANGE
+    for k in range(SIDE // 2)
+]
+FAR = [
+    [wide_index(z, 2 * k + j, c) * NARROW + x for z in RANGE for k in range(SIDE // 2)]
+    for j in (0, 1)
+    for c in (0, 1)
+    for x in range(NARROW)
+]
 OTHER_CORE = [(i, i ^ 1) for i in range(2 * SIDE * SIDE)]
 
 
 def to_all(block, axes, groups):
-    return lax.all_to_all(jnp.broadcast_to(block[None], (8, *block.shape)), axes, 0, 0, axis_index_groups=groups)
+    copies = jnp.broadcast_to(block[None], (len(groups[0]), *block.shape))
+    return lax.all_to_all(copies, axes, 0, 0, axis_index_groups=groups)
 
 
 def shift(block, by):
@@ -163,16 +174,16 @@
     dpreact = cotangent[...].astype(F32) * (sig * (1.0 + preact * (1.0 - sig)))
     weight_part = lax.dot_general(
         aggregated, dpreact.astype(BF16), (((0,), (0,)), ((), ())), preferred_element_type=F32
-    ).astype(BF16)
+    )
     bias_part = jnp.sum(dpreact, axis=0, keepdims=True)
-    rows = lax.broadcasted_iota(I32, (16, TILE), 0)
-    left = jnp.broadcast_to(bias_part[:, :TILE], (16, TILE))
-    right = jnp.broadcast_to(bias_part[:, TILE:], (16, TILE))
-    biases = jnp.where(rows == 0, left, jnp.where(rows == 1, right, 0.0)).astype(BF16)
-    for i in range(8):
-        grads[i, 0:16, :] = weight_part[16 * i : 16 * i + 16, :TILE]
-        grads[i, 16:32, :] = weight_part[16 * i : 16 * i + 16, TILE:]
-        grads[i, 32:48, :] = biases
+    rows = lax.broadcasted_iota(I32, (8, TILE), 0)
+    left = jnp.broadcast_to(bias_part[:, :TILE], (8, TILE))
+    right = jnp.broadcast_to(bias_part[:, TILE:], (8, TILE))
+    biases = jnp.where(rows == 0, left, jnp.where(rows == 1, right, 0.0))
+    for i in range(PIECES):
+        grads[i, 0:8, :] = weight_part[8 * i : 8 * i + 8, :TILE]
+        grads[i, 8:16, :] = weight_part[8 * i : 8 * i + 8, TILE:]
+        grads[i, 16:24, :] = biases
 
 
 VMEM = pl.BlockSpec(memory_space=pltpu.VMEM)
@@ -254,7 +265,7 @@
         dense_kernel,
         out_shape=(
             jax.ShapeDtypeStruct((rows, HID), BF16),
-            jax.ShapeDtypeStruct((8, 48, TILE), BF16),
+            jax.ShapeDtypeStruct((PIECES, 24, TILE), F32),
         ),
         in_specs=[VMEM] * 4,
         out_specs=(VMEM, VMEM),
@@ -263,12 +274,11 @@
         name="dense",
     )(parts, weight, bias.reshape(1, HID), cotangent)
 
-    share = total(lax.all_to_all(grads, both, 0, 0, axis_index_groups=COLUMN))[:40]
-    share = total(to_all(share, "wide", GROUPS_Y))
-    share = total(to_all(share, "wide", GROUPS_Z))
-    chunk = jnp.concatenate([share[0:16], share[16:32]], axis=1)
-    grad_weight = to_all(chunk, both, COLUMN).reshape(FIN, HID)
-    return hidden, grad_weight, share[32:34].reshape(HID)
+    share = total(lax.all_to_all(grads, both, 0, 0, axis_index_groups=NEAR)).astype(BF16)
+    share = total(to_all(share, both, FAR))
+    piece = jnp.concatenate([share[0:8], share[8:16]], axis=1)
+    grad_weight = to_all(piece, both, NEAR).reshape(FIN, HID)
+    return hidden, grad_weight, share[16:18].reshape(HID)
 
 
 def solution(mesh):

time: 134 us -> 129 us (0.963)
  blocking collectives: 62.5 us -> 58.5 us
    all_to_all x4 -> x3, blocking collectives: 48.5 us -> 43.3 us  [the longest x2 32.8 us: to_all(): return lax.all_to_all(copies, axes, 0, 0, axis_index_groups=groups)]
  transfers between devices with their start and end apart: 10 -> 10, of which waited for: 1 -> 1; matrix products, arithmetic and copies ran while one was open for 2% -> 2% of each run, Pallas kernels for 6% -> 5%
where the time goes in v6:
time: 129 us
  blocking collectives  58.5 us (45%)
  starting transfers between devices  49.3 us (38%)
  Pallas kernels  9.95 us (8%)
  waiting for transfers between devices  5.68 us (4%)
  local copies, waits for them, and re-layouts  2.02 us (2%)
  between operations  1.57 us (1%)
  other arithmetic  1.55 us (1%)
    all_to_all x2, blocking collectives, to_all(): return lax.all_to_all(copies, axes, 0, 0, axis_index_groups=groups)  32.8 us
    ppermute x7, starting transfers between devices, shift(): return lax.ppermute(block, 'wide', pairs)  29.5 us
    all_to_all x1, blocking collectives, local(): lax.all_to_all(partial.reshape(8, rows, FIN), both, 0, 0, axis_index_grou...  15.2 us
    all_to_all x1, blocking collectives, local(): lax.all_to_all(grads, both, 0, 0, axis_index_groups=NEAR)  10.5 us
    ppermute x1, starting transfers between devices, local(): other_values = lax.ppermute(own_values, 'wide', OTHER_CORE)  8.92 us
    all_to_all x1, waiting for transfers between devices, to_all(): return lax.all_to_all(copies, axes, 0, 0, axis_index_groups=groups)  5.65 us
    all_to_all x1, starting transfers between devices, to_all(): return lax.all_to_all(copies, axes, 0, 0, axis_index_groups=groups)  5.57 us
    ppermute x1, starting transfers between devices, local(): other_slots = lax.ppermute(slots, 'wide', OTHER_CORE)  5.33 us
  transfers between devices with their start and end apart: 10, of which 1 were waited for; matrix products, arithmetic and copies ran while one was open for 2% of the time, Pallas kernels for 5%

profile of v6, /device:TPU:1, one launch (start us, length us, event | category | flops | bytes accessed | tf_op | source)
XLA Modules:
  0.0 128.6 jit_solution(13567519187791081272)
XLA Ops:
  0.6 0.0 copy-start
  0.6 8.9 %collective-permute-start.1 = (bf16[128,128,128]{2,1,0:T(8,128)(2,1)}, bf16[128,128,128]{2,1,0:T(8,128)(2,1)}, u32[]{:S(2)}, u32[]{:S(2)}) collective-permute-start(bf16[128,128,128]{2,1,0:T(8,128)(2,1)} %bitcast.22), channel_id=1, source_target_pairs={{0,4},{4,0},{8,12},{12,8},{16,20},{20,16},{24,28},{28,24},{32,36},... | collective-permute-start | bytes 12582920 | tf_op jit(solution)/shard_map/ppermute | solution.py:204
  9.6 0.1 broadcast_in_dim.55
  9.7 16.6 %all_to_all.25 = bf16[8,256,128]{2,1,0:T(8,128)(2,1)S(1)} all-to-all(bf16[8,256,128]{2,1,0:T(8,128)(2,1)S(1)} %broadcast_in_dim.55), channel_id=1, replica_groups={{0,8,16,24,32,40,48,56},{64,72,80,88,96,104,112,120},{128,136,144,152,1..., dimensions={0} | all-to-all | bytes 1048576 | tf_op jit(solution)/shard_map/all_to_all | solution.py:56
  26.3 0.0 collective-permute-done.1.other
  26.3 4.2 %collective-permute-start.4 = (bf16[16,128,128]{2,1,0:T(8,128)(2,1)S(1)}, bf16[16,128,128]{2,1,0:T(8,128)(2,1)S(1)}, u32[]{:S(2)}, u32[]{:S(2)}) collective-permute-start(bf16[16,128,128]{2,1,0:T(8,128)(2,1)S(1)} %bitcast.14), channel_id=1, source_target_pairs={{0,128},{64,448},{128,256},{192,64},{256,384},{320,192},{384,0},{4... | collective-permute-start | bytes 1572872 | tf_op jit(solution)/shard_map/ppermute | solution.py:61
  30.5 3.6 %collective-permute-start.5 = (bf16[16,128,128]{2,1,0:T(8,128)(2,1)S(1)}, bf16[16,128,128]{2,1,0:T(8,128)(2,1)S(1)}, u32[]{:S(2)}, u32[]{:S(2)}) collective-permute-start(bf16[16,128,128]{2,1,0:T(8,128)(2,1)S(1)} %bitcast.15), channel_id=1, source_target_pairs={{0,384},{64,192},{128,0},{192,320},{256,128},{320,448},{384,256},{... | collective-permute-start | bytes 1572872 | tf_op jit(solution)/shard_map/ppermute | solution.py:61
  34.1 2.3 %collective-permute-start.2 = (bf16[16,128,128]{2,1,0:T(8,128)(2,1)S(1)}, bf16[16,128,128]{2,1,0:T(8,128)(2,1)S(1)}, u32[]{:S(2)}, u32[]{:S(2)}) collective-permute-start(bf16[16,128,128]{2,1,0:T(8,128)(2,1)S(1)} %bitcast.16), channel_id=1, source_target_pairs={{0,64},{64,0},{128,192},{192,128},{256,320},{320,256},{384,448},{4... | collective-permute-start | bytes 1572872 | tf_op jit(solution)/shard_map/ppermute | solution.py:61
  36.5 4.3 %collective-permute-start.3 = (bf16[16,128,128]{2,1,0:T(8,128)(2,1)S(1)}, bf16[16,128,128]{2,1,0:T(8,128)(2,1)S(1)}, u32[]{:S(2)}, u32[]{:S(2)}) collective-permute-start(bf16[16,128,128]{2,1,0:T(8,128)(2,1)S(1)} %bitcast.17), channel_id=1, source_target_pairs={{0,448},{64,128},{128,64},{192,256},{256,192},{320,384},{384,320},... | collective-permute-start | bytes 1572872 | tf_op jit(solution)/shard_map/ppermute | solution.py:61
  40.8 0.0 collective-permute-done.4.b3
  40.8 5.4 %collective-permute-start.6 = (bf16[16,128,128]{2,1,0:T(8,128)(2,1)S(1)}, bf16[16,128,128]{2,1,0:T(8,128)(2,1)S(1)}, u32[]{:S(2)}, u32[]{:S(2)}) collective-permute-start(bf16[16,128,128]{2,1,0:T(8,128)(2,1)S(1)} %collective-permute-done.4.b3), channel_id=1, source_target_pairs={{0,64},{64,0},{128,192},{192,128},{256,320},{320,256},{384,448},{4... | collective-permute-start | bytes 1572872 | tf_op jit(solution)/shard_map/ppermute | solution.py:61
  46.2 3.4 %collective-permute-start.8 = (bf16[16,128,128]{2,1,0:T(8,128)(2,1)S(1)}, bf16[16,128,128]{2,1,0:T(8,128)(2,1)S(1)}, u32[]{:S(2)}, u32[]{:S(2)}) collective-permute-start(bf16[16,128,128]{2,1,0:T(8,128)(2,1)S(1)} %collective-permute-done.4.b3), channel_id=1, source_target_pairs={{0,128},{64,448},{128,256},{192,64},{256,384},{320,192},{384,0},{4... | collective-permute-start | bytes 1572872 | tf_op jit(solution)/shard_map/ppermute | solution.py:61
  49.7 6.3 %collective-permute-start.7 = (bf16[16,128,128]{2,1,0:T(8,128)(2,1)S(1)}, bf16[16,128,128]{2,1,0:T(8,128)(2,1)S(1)}, u32[]{:S(2)}, u32[]{:S(2)}) collective-permute-start(bf16[16,128,128]{2,1,0:T(8,128)(2,1)S(1)} %collective-permute-done.5.b4), channel_id=1, source_target_pairs={{0,448},{64,128},{128,64},{192,256},{256,192},{320,384},{384,320},... | collective-permute-start | bytes 1572872 | tf_op jit(solution)/shard_map/ppermute | solution.py:61
  55.9 0.1 pad_add_fusion.place
  56.6 0.7 compare_select_fusion
  57.3 0.7 broadcast_select_fusion.slots
  58.1 5.3 %collective-permute-start = (s32[2,128]{1,0:T(2,128)S(1)}, s32[2,128]{1,0:T(2,128)S(1)}, u32[]{:S(2)}, u32[]{:S(2)}) collective-permute-start(s32[2,128]{1,0:T(2,128)S(1)} %broadcast_select_fusion.slots), channel_id=1, source_target_pairs={{0,4},{4,0},{8,12},{12,8},{16,20},{20,16},{24,28},{28,24},{32,36},... | collective-permute-start | bytes 3080 | tf_op jit(solution)/shard_map/ppermute | solution.py:216
  63.4 4.1 %own.1 = (f32[9,128,128]{2,1,0:T(8,128)S(1)}, bf16[128,128,128]{2,1,0:T(8,128)(2,1)S(1)}, bf16[128,128,128]{2,1,0:T(8,128)(2,1)S(1)}, s32[1,256]{1,0:T(1,128)S(1)}, s32[1,128]{1,0:T(1,128)S(1)}) custom-call(s32[2]{0:T(128)S(1)} %pad_add_fusion.place, s32[2,128]{1,0:T(2,128)S(1)} %broadcast_select_fusion.slots, bf16[128,128,128]{2,1,0:T(8,128)(2,1)} %bitcast.23, ...), custom_call_target="tpu_custom_call" | custom-call | flops 268435456 | bytes 8388608 | tf_op jit(solution)/shard_map/own/pallas_call | solution.py:223
  67.5 2.9 %other.1 = (f32[9,128,128]{2,1,0:T(8,128)S(1)}, s32[2,256]{1,0:T(2,128)S(1)}, s32[2,128]{1,0:T(2,128)S(1)}) custom-call(s32[2]{0:T(128)S(1)} %pad_add_fusion.place, s32[2,128]{1,0:T(2,128)S(1)} %collective-permute-done.slots, bf16[128,128,128]{2,1,0:T(8,128)(2,1)S(1)} %get-tuple-element.17.other, s32[1,256]{1,0:T(1,128)S(1)} %get-tuple-element.18.own_list, ...), custom_call_target="tpu_custom_call" | custom-call | flops 268435456 | bytes 8388608 | tf_op jit(solution)/shard_map/other/pallas_call | solution.py:237
  70.4 0.0 copy-start.1
  70.4 0.0 copy-start.2
  70.4 0.0 copy-start.3
  70.4 2.1 %late.1 = bf16[2,8,128,128]{3,2,1,0:T(8,128)(2,1)S(1)} custom-call(s32[2]{0:T(128)S(1)} %pad_add_fusion.place, s32[2,256]{1,0:T(2,128)S(1)} %get-tuple-element.20.lists, s32[2,128]{1,0:T(2,128)S(1)} %get-tuple-element.21.starts, bf16[128,128,128]{2,1,0:T(8,128)(2,1)S(1)} %get-tuple-element.22.own, bf16[128,128,128]{2,1,0:T(8,128)(2,1)S(1)} %get-tuple-element.17.other, ...), custom_call_target="tpu_custom_call" | custom-call | flops 268435456 | bytes 8388608 | tf_op jit(solution)/shard_map/late/pallas_call | solution.py:251
  72.6 15.2 %all_to_all.26.parts = bf16[8,256,128]{2,1,0:T(8,128)(2,1)S(1)} all-to-all(bf16[8,256,128]{2,1,0:T(8,128)(2,1)S(1)} %bitcast.20), channel_id=1, replica_groups={{0,1,2,3,4,5,6,7},{8,9,10,11,12,13,14,15},{16,17,18,19,20,21,22,23},{24..., dimensions={0} | all-to-all | bytes 1048576 | tf_op jit(solution)/shard_map/all_to_all | solution.py:263
  87.7 0.9 dense.1
  88.6 10.5 %all_to_all.27 = f32[16,24,128]{2,1,0:T(8,128)S(1)} all-to-all(f32[16,24,128]{2,1,0:T(8,128)S(1)} %get-tuple-element.26), channel_id=1, replica_groups={{0,1,2,3,4,5,6,7,8,9,10,11,12,13,14,15},{16,17,18,19,20,21,22,23,24,25,..., dimensions={0} | all-to-all | bytes 393216 | tf_op jit(solution)/shard_map/all_to_all | solution.py:277
  99.2 16.2 %all_to_all.28 = bf16[32,24,128]{2,1,0:T(8,128)(2,1)S(1)} all-to-all(bf16[32,24,128]{2,1,0:T(8,128)(2,1)S(1)} %broadcast_in_dim.56), channel_id=1, replica_groups={{0,16,32,48,64,80,96,112,128,144,160,176,192,208,224,240,256,272,288,30..., dimensions={0} | all-to-all | bytes 393216 | tf_op jit(solution)/shard_map/all_to_all | solution.py:56
  115.5 0.7 broadcast_in_dim.57
  116.1 5.6 %all-to-all-start.4 = ((f32[16,8,256]{2,1,0:T(8,128)}), f32[16,8,256]{2,1,0:T(8,128)S(1)}, u32[]{:S(2)}, u32[]{:S(2)}) async-start(f32[16,8,256]{2,1,0:T(8,128)} %broadcast_in_dim.57), calls=%async_computation.4 | async-start | bytes 262144 | tf_op jit(solution)/shard_map/all_to_all | solution.py:56
  121.7 0.6 slice_bitcast_fusion
  122.3 5.7 %all-to-all-done.4 = f32[16,8,256]{2,1,0:T(8,128)S(1)} async-done(((f32[16,8,256]{2,1,0:T(8,128)}), f32[16,8,256]{2,1,0:T(8,128)S(1)}, u32[]{:S(2)}, u32[]{:S(2)}) %all-to-all-start.4) | async-done | bytes 131104 | tf_op jit(solution)/shard_map/all_to_all | solution.py:56
  127.9 0.7 copy.14
  (18 shorter events, 0.1 us)
Async XLA Ops:
  0.6 9.0 %copy-start = (bf16[1024,128]{1,0:T(8,128)(2,1)S(1)}, bf16[1024,128]{1,0:T(8,128)(2,1)}, u32[]{:S(2)}) copy-start(bf16[1024,128]{1,0:T(8,128)(2,1)} %param.9) | copy-start | bytes 786436
  0.6 25.6 %collective-permute-start.1 = (bf16[128,128,128]{2,1,0:T(8,128)(2,1)}, bf16[128,128,128]{2,1,0:T(8,128)(2,1)}, u32[]{:S(2)}, u32[]{:S(2)}) collective-permute-start(bf16[128,128,128]{2,1,0:T(8,128)(2,1)} %bitcast.22), channel_id=1, source_target_pairs={{0,4},{4,0},{8,12},{12,8},{16,20},{20,16},{24,28},{28,24},{32,36},... | collective-permute-start | bytes 12582920 | tf_op jit(solution)/shard_map/ppermute | solution.py:204
  26.3 14.5 %collective-permute-start.4 = (bf16[16,128,128]{2,1,0:T(8,128)(2,1)S(1)}, bf16[16,128,128]{2,1,0:T(8,128)(2,1)S(1)}, u32[]{:S(2)}, u32[]{:S(2)}) collective-permute-start(bf16[16,128,128]{2,1,0:T(8,128)(2,1)S(1)} %bitcast.14), channel_id=1, source_target_pairs={{0,128},{64,448},{128,256},{192,64},{256,384},{320,192},{384,0},{4... | collective-permute-start | bytes 1572872 | tf_op jit(solution)/shard_map/ppermute | solution.py:61
  30.5 19.1 %collective-permute-start.5 = (bf16[16,128,128]{2,1,0:T(8,128)(2,1)S(1)}, bf16[16,128,128]{2,1,0:T(8,128)(2,1)S(1)}, u32[]{:S(2)}, u32[]{:S(2)}) collective-permute-start(bf16[16,128,128]{2,1,0:T(8,128)(2,1)S(1)} %bitcast.15), channel_id=1, source_target_pairs={{0,384},{64,192},{128,0},{192,320},{256,128},{320,448},{384,256},{... | collective-permute-start | bytes 1572872 | tf_op jit(solution)/shard_map/ppermute | solution.py:61
  34.1 23.9 %collective-permute-start.2 = (bf16[16,128,128]{2,1,0:T(8,128)(2,1)S(1)}, bf16[16,128,128]{2,1,0:T(8,128)(2,1)S(1)}, u32[]{:S(2)}, u32[]{:S(2)}) collective-permute-start(bf16[16,128,128]{2,1,0:T(8,128)(2,1)S(1)} %bitcast.16), channel_id=1, source_target_pairs={{0,64},{64,0},{128,192},{192,128},{256,320},{320,256},{384,448},{4... | collective-permute-start | bytes 1572872 | tf_op jit(solution)/shard_map/ppermute | solution.py:61
  36.5 26.9 %collective-permute-start.3 = (bf16[16,128,128]{2,1,0:T(8,128)(2,1)S(1)}, bf16[16,128,128]{2,1,0:T(8,128)(2,1)S(1)}, u32[]{:S(2)}, u32[]{:S(2)}) collective-permute-start(bf16[16,128,128]{2,1,0:T(8,128)(2,1)S(1)} %bitcast.17), channel_id=1, source_target_pairs={{0,448},{64,128},{128,64},{192,256},{256,192},{320,384},{384,320},... | collective-permute-start | bytes 1572872 | tf_op jit(solution)/shard_map/ppermute | solution.py:61
  40.8 29.6 %collective-permute-start.6 = (bf16[16,128,128]{2,1,0:T(8,128)(2,1)S(1)}, bf16[16,128,128]{2,1,0:T(8,128)(2,1)S(1)}, u32[]{:S(2)}, u32[]{:S(2)}) collective-permute-start(bf16[16,128,128]{2,1,0:T(8,128)(2,1)S(1)} %collective-permute-done.4.b3), channel_id=1, source_target_pairs={{0,64},{64,0},{128,192},{192,128},{256,320},{320,256},{384,448},{4... | collective-permute-start | bytes 1572872 | tf_op jit(solution)/shard_map/ppermute | solution.py:61
  46.2 24.2 %collective-permute-start.8 = (bf16[16,128,128]{2,1,0:T(8,128)(2,1)S(1)}, bf16[16,128,128]{2,1,0:T(8,128)(2,1)S(1)}, u32[]{:S(2)}, u32[]{:S(2)}) collective-permute-start(bf16[16,128,128]{2,1,0:T(8,128)(2,1)S(1)} %collective-permute-done.4.b3), channel_id=1, source_target_pairs={{0,128},{64,448},{128,256},{192,64},{256,384},{320,192},{384,0},{4... | collective-permute-start | bytes 1572872 | tf_op jit(solution)/shard_map/ppermute | solution.py:61
  49.7 20.7 %collective-permute-start.7 = (bf16[16,128,128]{2,1,0:T(8,128)(2,1)S(1)}, bf16[16,128,128]{2,1,0:T(8,128)(2,1)S(1)}, u32[]{:S(2)}, u32[]{:S(2)}) collective-permute-start(bf16[16,128,128]{2,1,0:T(8,128)(2,1)S(1)} %collective-permute-done.5.b4), channel_id=1, source_target_pairs={{0,448},{64,128},{128,64},{192,256},{256,192},{320,384},{384,320},... | collective-permute-start | bytes 1572872 | tf_op jit(solution)/shard_map/ppermute | solution.py:61
  58.1 9.4 %collective-permute-start = (s32[2,128]{1,0:T(2,128)S(1)}, s32[2,128]{1,0:T(2,128)S(1)}, u32[]{:S(2)}, u32[]{:S(2)}) collective-permute-start(s32[2,128]{1,0:T(2,128)S(1)} %broadcast_select_fusion.slots), channel_id=1, source_target_pairs={{0,4},{4,0},{8,12},{12,8},{16,20},{20,16},{24,28},{28,24},{32,36},... | collective-permute-start | bytes 3080 | tf_op jit(solution)/shard_map/ppermute | solution.py:216
  70.4 17.3 %copy-start.1 = (bf16[256,256]{1,0:T(8,128)(2,1)S(1)}, bf16[256,256]{1,0:T(8,128)(2,1)}, u32[]{:S(2)}) copy-start(bf16[256,256]{1,0:T(8,128)(2,1)} %cotangent.1) | copy-start | bytes 393220
  70.4 17.3 %copy-start.2 = (bf16[128,256]{1,0:T(8,128)(2,1)S(1)}, bf16[128,256]{1,0:T(8,128)(2,1)}, u32[]{:S(2)}) copy-start(bf16[128,256]{1,0:T(8,128)(2,1)} %weight.1) | copy-start | bytes 196612
  70.4 17.3 %copy-start.3 = (f32[256]{0:T(256)S(1)}, f32[256]{0:T(256)}, u32[]{:S(2)}) copy-start(f32[256]{0:T(256)} %param.11) | copy-start | bytes 3076
  116.1 11.8 %all-to-all-start.4 = ((f32[16,8,256]{2,1,0:T(8,128)}), f32[16,8,256]{2,1,0:T(8,128)S(1)}, u32[]{:S(2)}, u32[]{:S(2)}) async-start(f32[16,8,256]{2,1,0:T(8,128)} %broadcast_in_dim.57), calls=%async_computation.4 | async-start | bytes 262144 | tf_op jit(solution)/shard_map/all_to_all | solution.py:56

commit v7 on v6

--- a/solution.py
+++ b/solution.py
@@ -17,6 +17,7 @@
 STEP = 8
 SEGMENTS = 8
 EARLY = 5
+LAST = 7
 LIST = 256
 SPARE = TR
 BF16 = jnp.bfloat16
@@ -31,8 +32,8 @@
 RANGE = range(SIDE)
 ALONG_Y = [[[wide_index(z, y, c) for y in RANGE] for z in RANGE] for c in (0, 1)]
 ALONG_Z = [[[wide_index(z, y, c) for z in RANGE] for y in RANGE] for c in (0, 1)]
-FIRST = ALONG_Y[0] + ALONG_Z[1]
-SECOND = ALONG_Z[0] + ALONG_Y[1]
+FIRST = ALONG_Z[0] + ALONG_Y[1]
+SECOND = ALONG_Y[0] + ALONG_Z[1]
 COLUMN = [
     [wide_index(z, y, c) * NARROW + x for c in (0, 1) for x in range(NARROW)] for z in RANGE for y in RANGE
 ]
@@ -77,11 +78,11 @@
     lanes = lax.broadcasted_iota(I32, (1, SLOTS), 1)
     picked = jnp.sum(jnp.where(rows == source, column(pick), 0), axis=0, keepdims=True)
     z, y = lax.shift_right_arithmetic(source, 4), lax.shift_right_arithmetic(source, 1) & 7
-    along, across = jnp.where(core == 0, z, y), jnp.where(core == 0, y, z)
+    along, across = jnp.where(core == 0, y, z), jnp.where(core == 0, z, y)
     tile = across * 2 + picked
     ahead = jnp.where(at % 2 == 0, along - at, at - along) & 7
     segment = jnp.zeros_like(ahead)
-    for kind, distance in enumerate((1, 7, 6, 2, 3, 5, 4)):
+    for kind, distance in enumerate((1, 7, 6, 2, 3, 4, 5)):
         segment = jnp.where(ahead == distance, kind + 1, segment)
     segment = jnp.where(valid, segment, SEGMENTS)
     entry = lanes + SLOTS * tile + SLOTS * BLOCK * (code & 7)
@@ -116,48 +117,51 @@
         lax.fori_loop(starts[owner, first + i], starts[owner, first + i + 1], step, 0)
 
 
-def own_kernel(place, slots, own, other, b0, b1, b2, b3, b4, acc, own_here, other_here, lists, starts, entries, bounds, sems):
-    copies = [
-        pltpu.make_async_copy(own, own_here, sems.at[0]),
-        pltpu.make_async_copy(other, other_here, sems.at[1]),
-    ]
-    copies[0].start()
-    copies[1].start()
+def own_kernel(place, slots, own, b0, b1, b2, b3, b4, acc, own_here, lists, starts, entries, bounds, sems):
+    copy = pltpu.make_async_copy(own, own_here, sems.at[0])
+    copy.start()
     lists[...], starts[...] = make_list(place, slots[...])
     scalars = [
-        pltpu.make_async_copy(lists, entries, sems.at[2]),
-        pltpu.make_async_copy(starts, bounds, sems.at[3]),
+        pltpu.make_async_copy(lists, entries, sems.at[1]),
+        pltpu.make_async_copy(starts, bounds, sems.at[2]),
     ]
     scalars[0].start()
     scalars[1].start()
     acc[...] = jnp.zeros_like(acc)
     scalars[0].wait()
     scalars[1].wait()
-    copies[0].wait()
+    copy.wait()
     add_products(entries, bounds, 0, own_here, (b0, b1, b2, b3, b4), 0, acc)
-    copies[1].wait()
-
-
-def other_kernel(place, slots, other, own_list, own_start, b0, b1, b2, b3, b4, acc, lists, starts, entries, bounds, sems):
+
+
+def other_kernel(
+    place, slots, other, own, own_list, own_start, own_before, b0, b1, b2, b3, b4, b5, b6,
+    own_acc, other_acc, other_here, lists, starts, entries, bounds, sems,
+):
+    copy = pltpu.make_async_copy(other, other_here, sems.at[0])
+    copy.start()
     lists[0:1, :], starts[0:1, :] = own_list[...], own_start[...]
     lists[1:2, :], starts[1:2, :] = make_list(place, slots[...])
     scalars = [
-        pltpu.make_async_copy(lists, entries, sems.at[0]),
-        pltpu.make_async_copy(starts, bounds, sems.at[1]),
+        pltpu.make_async_copy(lists, entries, sems.at[1]),
+        pltpu.make_async_copy(starts, bounds, sems.at[2]),
     ]
     scalars[0].start()
     scalars[1].start()
-    acc[...] = jnp.zeros_like(acc)
+    own_acc[...] = own_before[...]
+    other_acc[...] = jnp.zeros_like(other_acc)
     scalars[0].wait()
     scalars[1].wait()
-    add_products(entries, bounds, 1, other, (b0, b1, b2, b3, b4), 0, acc)
-
-
-def late_kernel(place, lists, starts, own, other, b5, b6, b7, own_before, other_before, out, own_acc, other_acc):
+    add_products(entries, bounds, 0, own, (b5, b6), EARLY, own_acc)
+    copy.wait()
+    add_products(entries, bounds, 1, other_here, (b0, b1, b2, b3, b4, b5, b6), 0, other_acc)
+
+
+def late_kernel(place, lists, starts, own, other, b7, own_before, other_before, out, own_acc, other_acc):
     own_acc[...] = own_before[...]
     other_acc[...] = other_before[...]
-    add_products(lists, starts, 0, own, (b5, b6, b7), EARLY, own_acc)
-    add_products(lists, starts, 1, other, (b5, b6, b7), EARLY, other_acc)
+    add_products(lists, starts, 0, own, (b7,), LAST, own_acc)
+    add_products(lists, starts, 1, other, (b7,), LAST, other_acc)
     core = place[0]
     out[core] = own_acc[0:TR].astype(BF16)
     out[1 - core] = other_acc[0:TR].astype(BF16)
@@ -214,50 +218,53 @@
     first_row = jnp.arange(2, dtype=I32)[:, None] == 0
     slots = jnp.where(first_row, code[None, :], pick[0])
     other_slots = lax.ppermute(slots, "wide", OTHER_CORE)
-    place = jnp.stack([core, jnp.where(core == 0, index // 16, lax.rem(index // 2, 8))])
+    place = jnp.stack([core, jnp.where(core == 0, lax.rem(index // 2, 8), index // 16)])
 
     sums = jax.ShapeDtypeStruct((TR + 1, TILE, FIN), F32)
     here = jax.ShapeDtypeStruct(own_values.shape, BF16)
     lists = lambda n: jax.ShapeDtypeStruct((n, LIST), I32)
     starts = lambda n: jax.ShapeDtypeStruct((n, SLOTS), I32)
-    own_sums, own_here, other_here, own_list, own_start = pl.pallas_call(
+    own_sums, own_here, own_list, own_start = pl.pallas_call(
         own_kernel,
-        out_shape=(sums, here, here, lists(1), starts(1)),
-        in_specs=[SMEM, VMEM] + [HBM] * 2 + [VMEM] * 5,
-        out_specs=(VMEM,) * 5,
+        out_shape=(sums, here, lists(1), starts(1)),
+        in_specs=[SMEM, VMEM, HBM] + [VMEM] * 5,
+        out_specs=(VMEM,) * 4,
         scratch_shapes=[
             pltpu.SMEM((1, LIST), I32),
             pltpu.SMEM((1, SLOTS), I32),
-            pltpu.SemaphoreType.DMA((4,)),
+            pltpu.SemaphoreType.DMA((3,)),
         ],
-        compiler_params=pltpu.CompilerParams(vmem_limit_bytes=42 << 20),
+        compiler_params=pltpu.CompilerParams(vmem_limit_bytes=45 << 20),
         cost_estimate=pl.CostEstimate(flops=SLOTS * TILE**3, bytes_accessed=8 << 20, transcendentals=0),
         name="own",
-    )(place, slots, own_values, other_values, own, one_a, one_b, two_a, two_b)
-    other_sums, all_lists, all_starts = pl.pallas_call(
+    )(place, slots, own_values, own, one_a, one_b, two_a, two_b)
+    own_sums, other_sums, other_here, all_lists, all_starts = pl.pallas_call(
         other_kernel,
-        out_shape=(sums, lists(2), starts(2)),
-        in_specs=[SMEM] + [VMEM] * 9,
-        out_specs=(VMEM,) * 3,
+        out_shape=(sums, sums, here, lists(2), starts(2)),
+        in_specs=[SMEM, VMEM, HBM] + [VMEM] * 11,
+        out_specs=(VMEM,) * 5,
         scratch_shapes=[
             pltpu.SMEM((2, LIST), I32),
             pltpu.SMEM((2, SLOTS), I32),
-            pltpu.SemaphoreType.DMA((2,)),
+            pltpu.SemaphoreType.DMA((3,)),
         ],
-        compiler_params=pltpu.CompilerParams(vmem_limit_bytes=16 << 20),
+        compiler_params=pltpu.CompilerParams(vmem_limit_bytes=24 << 20),
         cost_estimate=pl.CostEstimate(flops=SLOTS * TILE**3, bytes_accessed=8 << 20, transcendentals=0),
         name="other",
-    )(place, other_slots, other_here, own_list, own_start, own, one_a, one_b, two_a, two_b)
+    )(
+        place, other_slots, other_values, own_here, own_list, own_start, own_sums,
+        own, one_a, one_b, two_a, two_b, three_a, four,
+    )
     partial = pl.pallas_call(
         late_kernel,
         out_shape=jax.ShapeDtypeStruct((2, TR, TILE, FIN), BF16),
-        in_specs=[SMEM] * 3 + [VMEM] * 7,
+        in_specs=[SMEM] * 3 + [VMEM] * 5,
         out_specs=VMEM,
         scratch_shapes=[pltpu.VMEM(sums.shape, F32), pltpu.VMEM(sums.shape, F32)],
         compiler_params=pltpu.CompilerParams(vmem_limit_bytes=16 << 20),
         cost_estimate=pl.CostEstimate(flops=SLOTS * TILE**3, bytes_accessed=8 << 20, transcendentals=0),
         name="late",
-    )(place, all_lists, all_starts, own_here, other_here, three_a, three_b, four, own_sums, other_sums)
+    )(place, all_lists, all_starts, own_here, other_here, three_b, own_sums, other_sums)
 
     rows = TR * TILE // NARROW
     parts = lax.all_to_all(partial.reshape(8, rows, FIN), both, 0, 0, axis_index_groups=COLUMN)
@@ -277,8 +284,9 @@
     share = total(lax.all_to_all(grads, both, 0, 0, axis_index_groups=NEAR)).astype(BF16)
     share = total(to_all(share, both, FAR))
     piece = jnp.concatenate([share[0:8], share[8:16]], axis=1)
+    piece, grad_bias = lax.optimization_barrier((piece, share[16:18].reshape(HID)))
     grad_weight = to_all(piece, both, NEAR).reshape(FIN, HID)
-    return hidden, grad_weight, share[16:18].reshape(HID)
+    return hidden, grad_weight, grad_bias
 
 
 def solution(mesh):

time: 129 us -> 127 us (0.984)
  blocking collectives: 58.5 us -> 65 us
  waiting for transfers between devices: 5.68 us -> 0.02 us
  starting transfers between devices: 49.3 us -> 45.8 us
    all_to_all x2 -> x3, blocking collectives: 32.8 us -> 41.4 us  [to_all(): return lax.all_to_all(copies, axes, 0, 0, axis_index_groups=groups)]
    all_to_all x1 -> x0, waiting for transfers between devices: 5.65 us -> none  [to_all(): return lax.all_to_all(copies, axes, 0, 0, axis_index_groups=groups)]
    all_to_all x1 -> x0, starting transfers between devices: 5.57 us -> none  [to_all(): return lax.all_to_all(copies, axes, 0, 0, axis_index_groups=groups)]
    ppermute x7, starting transfers between devices: 29.5 us -> 31.5 us  [shift(): return lax.ppermute(block, 'wide', pairs)]
    all_to_all x1, blocking collectives: 15.2 us -> 13.1 us  [local(): lax.all_to_all(partial.reshape(8, rows, FIN), both, 0, 0, axis_index_grou...]
    pallas_call x2, Pallas kernels: 6.93 us -> 8.64 us  [the longest x1 4.67 us: local(): pl.pallas_call(other_kernel, out_shape=(sums, sums, here, lists(2), start...]
  transfers between devices with their start and end apart: 10 -> 9, of which waited for: 1 -> 0; matrix products, arithmetic and copies ran while one was open for 2% -> 1% of each run, Pallas kernels for 5% -> 7%
where the time goes in v7:
time: 127 us; the launch traced here: 126 us
  blocking collectives  65 us (51%)
  starting transfers between devices  45.8 us (36%)
  Pallas kernels  10.7 us (8%)
  between operations  1.56 us (1%)
  other arithmetic  1.55 us (1%)
  local copies, waits for them, and re-layouts  1.37 us (1%)
    all_to_all x3, blocking collectives, to_all(): return lax.all_to_all(copies, axes, 0, 0, axis_index_groups=groups)  41.4 us
    ppermute x7, starting transfers between devices, shift(): return lax.ppermute(block, 'wide', pairs)  31.5 us
    all_to_all x1, blocking collectives, local(): lax.all_to_all(partial.reshape(8, rows, FIN), both, 0, 0, axis_index_grou...  13.1 us
    all_to_all x1, blocking collectives, local(): lax.all_to_all(grads, both, 0, 0, axis_index_groups=NEAR)  10.4 us
    ppermute x1, starting transfers between devices, local(): other_values = lax.ppermute(own_values, 'wide', OTHER_CORE)  8.92 us
    ppermute x1, starting transfers between devices, local(): other_slots = lax.ppermute(slots, 'wide', OTHER_CORE)  5.37 us
    pallas_call x1, Pallas kernels, local(): pl.pallas_call(other_kernel, out_shape=(sums, sums, here, lists(2), start...  4.67 us
    pallas_call x1, Pallas kernels, local(): pl.pallas_call(own_kernel, out_shape=(sums, here, lists(1), starts(1)), i...  3.97 us
  transfers between devices with their start and end apart: 9, of which 0 were waited for; matrix products, arithmetic and copies ran while one was open for 1% of the time, Pallas kernels for 7%

profile of v7, /device:TPU:1, one launch (start us, length us, event | category | flops | bytes accessed | tf_op | source)
XLA Modules:
  0.0 126.1 jit_solution(14053551247428131632)
XLA Ops:
  0.6 0.0 copy-start
  0.6 8.9 %collective-permute-start.1 = (bf16[128,128,128]{2,1,0:T(8,128)(2,1)}, bf16[128,128,128]{2,1,0:T(8,128)(2,1)}, u32[]{:S(2)}, u32[]{:S(2)}) collective-permute-start(bf16[128,128,128]{2,1,0:T(8,128)(2,1)} %bitcast.22), channel_id=1, source_target_pairs={{0,4},{4,0},{8,12},{12,8},{16,20},{20,16},{24,28},{28,24},{32,36},... | collective-permute-start | bytes 12582920 | tf_op jit(solution)/shard_map/ppermute | solution.py:208
  9.6 0.1 broadcast_in_dim.55
  9.7 14.5 %all_to_all.25 = bf16[8,256,128]{2,1,0:T(8,128)(2,1)S(1)} all-to-all(bf16[8,256,128]{2,1,0:T(8,128)(2,1)S(1)} %broadcast_in_dim.55), channel_id=1, replica_groups={{0,64,128,192,256,320,384,448},{8,72,136,200,264,328,392,456},{16,80,14..., dimensions={0} | all-to-all | bytes 1048576 | tf_op jit(solution)/shard_map/all_to_all | solution.py:57
  24.2 0.0 collective-permute-done.1.other
  24.2 4.9 %collective-permute-start.4 = (bf16[16,128,128]{2,1,0:T(8,128)(2,1)S(1)}, bf16[16,128,128]{2,1,0:T(8,128)(2,1)S(1)}, u32[]{:S(2)}, u32[]{:S(2)}) collective-permute-start(bf16[16,128,128]{2,1,0:T(8,128)(2,1)S(1)} %bitcast.14), channel_id=1, source_target_pairs={{0,16},{8,56},{16,32},{24,8},{32,48},{40,24},{48,0},{56,40},{64,80... | collective-permute-start | bytes 1572872 | tf_op jit(solution)/shard_map/ppermute | solution.py:62
  29.2 6.5 %collective-permute-start.5 = (bf16[16,128,128]{2,1,0:T(8,128)(2,1)S(1)}, bf16[16,128,128]{2,1,0:T(8,128)(2,1)S(1)}, u32[]{:S(2)}, u32[]{:S(2)}) collective-permute-start(bf16[16,128,128]{2,1,0:T(8,128)(2,1)S(1)} %bitcast.15), channel_id=1, source_target_pairs={{0,48},{8,24},{16,0},{24,40},{32,16},{40,56},{48,32},{56,8},{64,11... | collective-permute-start | bytes 1572872 | tf_op jit(solution)/shard_map/ppermute | solution.py:62
  35.7 3.1 %collective-permute-start.2 = (bf16[16,128,128]{2,1,0:T(8,128)(2,1)S(1)}, bf16[16,128,128]{2,1,0:T(8,128)(2,1)S(1)}, u32[]{:S(2)}, u32[]{:S(2)}) collective-permute-start(bf16[16,128,128]{2,1,0:T(8,128)(2,1)S(1)} %bitcast.16), channel_id=1, source_target_pairs={{0,8},{8,0},{16,24},{24,16},{32,40},{40,32},{48,56},{56,48},{64,72... | collective-permute-start | bytes 1572872 | tf_op jit(solution)/shard_map/ppermute | solution.py:62
  38.8 4.3 %collective-permute-start.3 = (bf16[16,128,128]{2,1,0:T(8,128)(2,1)S(1)}, bf16[16,128,128]{2,1,0:T(8,128)(2,1)S(1)}, u32[]{:S(2)}, u32[]{:S(2)}) collective-permute-start(bf16[16,128,128]{2,1,0:T(8,128)(2,1)S(1)} %bitcast.17), channel_id=1, source_target_pairs={{0,56},{8,16},{16,8},{24,32},{32,24},{40,48},{48,40},{56,0},{64,12... | collective-permute-start | bytes 1572872 | tf_op jit(solution)/shard_map/ppermute | solution.py:62
  43.1 5.5 %collective-permute-start.6 = (bf16[16,128,128]{2,1,0:T(8,128)(2,1)S(1)}, bf16[16,128,128]{2,1,0:T(8,128)(2,1)S(1)}, u32[]{:S(2)}, u32[]{:S(2)}) collective-permute-start(bf16[16,128,128]{2,1,0:T(8,128)(2,1)S(1)} %collective-permute-done.4.b3), channel_id=1, source_target_pairs={{0,8},{8,0},{16,24},{24,16},{32,40},{40,32},{48,56},{56,48},{64,72... | collective-permute-start | bytes 1572872 | tf_op jit(solution)/shard_map/ppermute | solution.py:62
  48.6 1.9 %collective-permute-start.7 = (bf16[16,128,128]{2,1,0:T(8,128)(2,1)S(1)}, bf16[16,128,128]{2,1,0:T(8,128)(2,1)S(1)}, u32[]{:S(2)}, u32[]{:S(2)}) collective-permute-start(bf16[16,128,128]{2,1,0:T(8,128)(2,1)S(1)} %collective-permute-done.4.b3), channel_id=1, source_target_pairs={{0,16},{8,56},{16,32},{24,8},{32,48},{40,24},{48,0},{56,40},{64,80... | collective-permute-start | bytes 1572872 | tf_op jit(solution)/shard_map/ppermute | solution.py:62
  50.5 5.4 %collective-permute-start.8 = (bf16[16,128,128]{2,1,0:T(8,128)(2,1)S(1)}, bf16[16,128,128]{2,1,0:T(8,128)(2,1)S(1)}, u32[]{:S(2)}, u32[]{:S(2)}) collective-permute-start(bf16[16,128,128]{2,1,0:T(8,128)(2,1)S(1)} %collective-permute-done.5.b4), channel_id=1, source_target_pairs={{0,56},{8,16},{16,8},{24,32},{32,24},{40,48},{48,40},{56,0},{64,12... | collective-permute-start | bytes 1572872 | tf_op jit(solution)/shard_map/ppermute | solution.py:62
  55.9 0.1 pad_add_fusion.place
  56.6 0.7 compare_select_fusion
  57.3 0.7 broadcast_select_fusion.slots
  58.0 5.4 %collective-permute-start = (s32[2,128]{1,0:T(2,128)S(1)}, s32[2,128]{1,0:T(2,128)S(1)}, u32[]{:S(2)}, u32[]{:S(2)}) collective-permute-start(s32[2,128]{1,0:T(2,128)S(1)} %broadcast_select_fusion.slots), channel_id=1, source_target_pairs={{0,4},{4,0},{8,12},{12,8},{16,20},{20,16},{24,28},{28,24},{32,36},... | collective-permute-start | bytes 3080 | tf_op jit(solution)/shard_map/ppermute | solution.py:220
  63.4 0.0 collective-permute-done.3.b2
  63.4 4.0 %own.1 = (f32[9,128,128]{2,1,0:T(8,128)S(1)}, bf16[128,128,128]{2,1,0:T(8,128)(2,1)S(1)}, s32[1,256]{1,0:T(1,128)S(1)}, s32[1,128]{1,0:T(1,128)S(1)}) custom-call(s32[2]{0:T(128)S(1)} %pad_add_fusion.place, s32[2,128]{1,0:T(2,128)S(1)} %broadcast_select_fusion.slots, bf16[128,128,128]{2,1,0:T(8,128)(2,1)} %bitcast.23, bf16[16,128,128]{2,1,0:T(8,128)(2,1)S(1)} %bitcast.18, ...), custom_call_target="tpu_custom_call" | custom-call | flops 268435456 | bytes 8388608 | tf_op jit(solution)/shard_map/own/pallas_call | solution.py:227
  67.4 0.0 collective-permute-done.slots
  67.4 0.0 collective-permute-done.7.b6
  67.4 4.7 %other.1 = (f32[9,128,128]{2,1,0:T(8,128)S(1)}, f32[9,128,128]{2,1,0:T(8,128)S(1)}, bf16[128,128,128]{2,1,0:T(8,128)(2,1)S(1)}, s32[2,256]{1,0:T(2,128)S(1)}, s32[2,128]{1,0:T(2,128)S(1)}) custom-call(s32[2]{0:T(128)S(1)} %pad_add_fusion.place, s32[2,128]{1,0:T(2,128)S(1)} %collective-permute-done.slots, ...), custom_call_target="tpu_custom_call" | custom-call | flops 268435456 | bytes 8388608 | tf_op jit(solution)/shard_map/other/pallas_call | solution.py:241
  72.1 0.0 copy-start.1
  72.1 0.0 copy-start.2
  72.2 0.0 copy-start.3
  72.2 1.2 late.1
  73.4 13.1 %all_to_all.26.parts = bf16[8,256,128]{2,1,0:T(8,128)(2,1)S(1)} all-to-all(bf16[8,256,128]{2,1,0:T(8,128)(2,1)S(1)} %bitcast.20), channel_id=1, replica_groups={{0,1,2,3,4,5,6,7},{8,9,10,11,12,13,14,15},{16,17,18,19,20,21,22,23},{24..., dimensions={0} | all-to-all | bytes 1048576 | tf_op jit(solution)/shard_map/all_to_all | solution.py:270
  86.5 0.9 dense.1
  87.4 10.4 %all_to_all.27 = f32[16,24,128]{2,1,0:T(8,128)S(1)} all-to-all(f32[16,24,128]{2,1,0:T(8,128)S(1)} %get-tuple-element.30), channel_id=1, replica_groups={{0,1,2,3,4,5,6,7,8,9,10,11,12,13,14,15},{16,17,18,19,20,21,22,23,24,25,..., dimensions={0} | all-to-all | bytes 393216 | tf_op jit(solution)/shard_map/all_to_all | solution.py:284
  97.9 15.7 %all_to_all.28 = bf16[32,24,128]{2,1,0:T(8,128)(2,1)S(1)} all-to-all(bf16[32,24,128]{2,1,0:T(8,128)(2,1)S(1)} %broadcast_in_dim.56), channel_id=1, replica_groups={{0,16,32,48,64,80,96,112,128,144,160,176,192,208,224,240,256,272,288,30..., dimensions={0} | all-to-all | bytes 393216 | tf_op jit(solution)/shard_map/all_to_all | solution.py:57
  113.7 0.6 slice_bitcast_fusion
  114.3 11.2 %all_to_all.29 = f32[16,8,256]{2,1,0:T(8,128)S(1)} all-to-all(f32[16,8,256]{2,1,0:T(8,128)S(1)} %broadcast_in_dim.57), channel_id=1, replica_groups={{0,1,2,3,4,5,6,7,8,9,10,11,12,13,14,15},{16,17,18,19,20,21,22,23,24,25,..., dimensions={0} | all-to-all | bytes 262144 | tf_op jit(solution)/shard_map/all_to_all | solution.py:57
  125.4 0.7 copy.14
  (17 shorter events, 0.1 us)
Async XLA Ops:
  0.6 9.0 %copy-start = (bf16[1024,128]{1,0:T(8,128)(2,1)S(1)}, bf16[1024,128]{1,0:T(8,128)(2,1)}, u32[]{:S(2)}) copy-start(bf16[1024,128]{1,0:T(8,128)(2,1)} %param.9) | copy-start | bytes 786436
  0.6 23.6 %collective-permute-start.1 = (bf16[128,128,128]{2,1,0:T(8,128)(2,1)}, bf16[128,128,128]{2,1,0:T(8,128)(2,1)}, u32[]{:S(2)}, u32[]{:S(2)}) collective-permute-start(bf16[128,128,128]{2,1,0:T(8,128)(2,1)} %bitcast.22), channel_id=1, source_target_pairs={{0,4},{4,0},{8,12},{12,8},{16,20},{20,16},{24,28},{28,24},{32,36},... | collective-permute-start | bytes 12582920 | tf_op jit(solution)/shard_map/ppermute | solution.py:208
  24.2 18.9 %collective-permute-start.4 = (bf16[16,128,128]{2,1,0:T(8,128)(2,1)S(1)}, bf16[16,128,128]{2,1,0:T(8,128)(2,1)S(1)}, u32[]{:S(2)}, u32[]{:S(2)}) collective-permute-start(bf16[16,128,128]{2,1,0:T(8,128)(2,1)S(1)} %bitcast.14), channel_id=1, source_target_pairs={{0,16},{8,56},{16,32},{24,8},{32,48},{40,24},{48,0},{56,40},{64,80... | collective-permute-start | bytes 1572872 | tf_op jit(solution)/shard_map/ppermute | solution.py:62
  29.2 21.3 %collective-permute-start.5 = (bf16[16,128,128]{2,1,0:T(8,128)(2,1)S(1)}, bf16[16,128,128]{2,1,0:T(8,128)(2,1)S(1)}, u32[]{:S(2)}, u32[]{:S(2)}) collective-permute-start(bf16[16,128,128]{2,1,0:T(8,128)(2,1)S(1)} %bitcast.15), channel_id=1, source_target_pairs={{0,48},{8,24},{16,0},{24,40},{32,16},{40,56},{48,32},{56,8},{64,11... | collective-permute-start | bytes 1572872 | tf_op jit(solution)/shard_map/ppermute | solution.py:62
  35.7 22.3 %collective-permute-start.2 = (bf16[16,128,128]{2,1,0:T(8,128)(2,1)S(1)}, bf16[16,128,128]{2,1,0:T(8,128)(2,1)S(1)}, u32[]{:S(2)}, u32[]{:S(2)}) collective-permute-start(bf16[16,128,128]{2,1,0:T(8,128)(2,1)S(1)} %bitcast.16), channel_id=1, source_target_pairs={{0,8},{8,0},{16,24},{24,16},{32,40},{40,32},{48,56},{56,48},{64,72... | collective-permute-start | bytes 1572872 | tf_op jit(solution)/shard_map/ppermute | solution.py:62
  38.8 24.6 %collective-permute-start.3 = (bf16[16,128,128]{2,1,0:T(8,128)(2,1)S(1)}, bf16[16,128,128]{2,1,0:T(8,128)(2,1)S(1)}, u32[]{:S(2)}, u32[]{:S(2)}) collective-permute-start(bf16[16,128,128]{2,1,0:T(8,128)(2,1)S(1)} %bitcast.17), channel_id=1, source_target_pairs={{0,56},{8,16},{16,8},{24,32},{32,24},{40,48},{48,40},{56,0},{64,12... | collective-permute-start | bytes 1572872 | tf_op jit(solution)/shard_map/ppermute | solution.py:62
  43.1 24.3 %collective-permute-start.6 = (bf16[16,128,128]{2,1,0:T(8,128)(2,1)S(1)}, bf16[16,128,128]{2,1,0:T(8,128)(2,1)S(1)}, u32[]{:S(2)}, u32[]{:S(2)}) collective-permute-start(bf16[16,128,128]{2,1,0:T(8,128)(2,1)S(1)} %collective-permute-done.4.b3), channel_id=1, source_target_pairs={{0,8},{8,0},{16,24},{24,16},{32,40},{40,32},{48,56},{56,48},{64,72... | collective-permute-start | bytes 1572872 | tf_op jit(solution)/shard_map/ppermute | solution.py:62
  48.6 18.8 %collective-permute-start.7 = (bf16[16,128,128]{2,1,0:T(8,128)(2,1)S(1)}, bf16[16,128,128]{2,1,0:T(8,128)(2,1)S(1)}, u32[]{:S(2)}, u32[]{:S(2)}) collective-permute-start(bf16[16,128,128]{2,1,0:T(8,128)(2,1)S(1)} %collective-permute-done.4.b3), channel_id=1, source_target_pairs={{0,16},{8,56},{16,32},{24,8},{32,48},{40,24},{48,0},{56,40},{64,80... | collective-permute-start | bytes 1572872 | tf_op jit(solution)/shard_map/ppermute | solution.py:62
  50.5 21.6 %collective-permute-start.8 = (bf16[16,128,128]{2,1,0:T(8,128)(2,1)S(1)}, bf16[16,128,128]{2,1,0:T(8,128)(2,1)S(1)}, u32[]{:S(2)}, u32[]{:S(2)}) collective-permute-start(bf16[16,128,128]{2,1,0:T(8,128)(2,1)S(1)} %collective-permute-done.5.b4), channel_id=1, source_target_pairs={{0,56},{8,16},{16,8},{24,32},{32,24},{40,48},{48,40},{56,0},{64,12... | collective-permute-start | bytes 1572872 | tf_op jit(solution)/shard_map/ppermute | solution.py:62
  58.0 9.4 %collective-permute-start = (s32[2,128]{1,0:T(2,128)S(1)}, s32[2,128]{1,0:T(2,128)S(1)}, u32[]{:S(2)}, u32[]{:S(2)}) collective-permute-start(s32[2,128]{1,0:T(2,128)S(1)} %broadcast_select_fusion.slots), channel_id=1, source_target_pairs={{0,4},{4,0},{8,12},{12,8},{16,20},{20,16},{24,28},{28,24},{32,36},... | collective-permute-start | bytes 3080 | tf_op jit(solution)/shard_map/ppermute | solution.py:220
  72.1 14.4 %copy-start.1 = (bf16[256,256]{1,0:T(8,128)(2,1)S(1)}, bf16[256,256]{1,0:T(8,128)(2,1)}, u32[]{:S(2)}) copy-start(bf16[256,256]{1,0:T(8,128)(2,1)} %cotangent.1) | copy-start | bytes 393220
  72.1 14.4 %copy-start.2 = (bf16[128,256]{1,0:T(8,128)(2,1)S(1)}, bf16[128,256]{1,0:T(8,128)(2,1)}, u32[]{:S(2)}) copy-start(bf16[128,256]{1,0:T(8,128)(2,1)} %weight.1) | copy-start | bytes 196612
  72.2 14.4 %copy-start.3 = (f32[256]{0:T(256)S(1)}, f32[256]{0:T(256)}, u32[]{:S(2)}) copy-start(f32[256]{0:T(256)} %param.11) | copy-start | bytes 3076

commit v8 on v7

--- a/solution.py
+++ b/solution.py
@@ -14,7 +14,7 @@
 NARROW = 4
 SLOTS = 128
 BLOCK = SIDE * CT
-STEP = 8
+STEP = 4
 SEGMENTS = 8
 EARLY = 5
 LAST = 7
@@ -88,7 +88,7 @@
     entry = lanes + SLOTS * tile + SLOTS * BLOCK * (code & 7)
     segments = column(segment)
     sizes = jnp.sum((segments == kinds).astype(I32), axis=0, keepdims=True)
-    sizes = lax.shift_right_arithmetic(sizes + STEP - 1, 3) * STEP
+    sizes = lax.shift_right_arithmetic(sizes + STEP - 1, 2) * STEP
     size = column(jnp.where(lanes < SEGMENTS, sizes, 0))
     start = jnp.sum(jnp.where(rows < kinds, size, 0), axis=0, keepdims=True)
     earlier = (segments == segment) & (rows < kinds)
@@ -98,28 +98,42 @@
     spare = SLOTS * BLOCK * SPARE
     hit = column(place_of) == lax.broadcasted_iota(I32, (SLOTS, LIST), 1)
     entries = spare + jnp.sum(jnp.where(hit, column(entry) - spare, 0), axis=0, keepdims=True)
-    return entries, lax.shift_right_arithmetic(start, 3)
+    return entries, lax.shift_right_arithmetic(start, 2)
 
 
 def add_products(entries, starts, owner, values, blocks, first, acc):
     for i, block in enumerate(blocks):
-
-        def step(k, carry, block=block):
+        begin, end = starts[owner, first + i], starts[owner, first + i + 1]
+
+        def add(at, n, block=block):
             done = []
-            for u in range(STEP):
-                e = entries[owner, k * STEP + u]
+            for u in range(n):
+                e = entries[owner, at + u]
                 tile, row = (e >> 7) & (BLOCK - 1), e >> 11
                 done.append((row, jnp.dot(values[e & (SLOTS - 1)], block[tile], preferred_element_type=F32)))
             for row, product in done:
                 acc[row] += product
+
+        def two(k, carry, begin=begin, add=add):
+            add((begin + 2 * k) * STEP, 2 * STEP)
             return carry
 
-        lax.fori_loop(starts[owner, first + i], starts[owner, first + i + 1], step, 0)
-
-
-def own_kernel(place, slots, own, b0, b1, b2, b3, b4, acc, own_here, lists, starts, entries, bounds, sems):
+        def one(k, carry, end=end, add=add):
+            add((end - 1) * STEP, STEP)
+            return carry
+
+        lax.fori_loop(0, (end - begin) >> 1, two, 0)
+        lax.fori_loop(0, (end - begin) & 1, one, 0)
+
+
+def own_kernel(
+    place, slots, own, other, b0, b1, b2, b3, b4,
+    acc, own_here, other_here, lists, starts, entries, bounds, sems,
+):
     copy = pltpu.make_async_copy(own, own_here, sems.at[0])
+    other_copy = pltpu.make_async_copy(other, other_here, sems.at[3])
     copy.start()
+    other_copy.start()
     lists[...], starts[...] = make_list(place, slots[...])
     scalars = [
         pltpu.make_async_copy(lists, entries, sems.at[1]),
@@ -132,19 +146,18 @@
     scalars[1].wait()
     copy.wait()
     add_products(entries, bounds, 0, own_here, (b0, b1, b2, b3, b4), 0, acc)
+    other_copy.wait()
 
 
 def other_kernel(
     place, slots, other, own, own_list, own_start, own_before, b0, b1, b2, b3, b4, b5, b6,
-    own_acc, other_acc, other_here, lists, starts, entries, bounds, sems,
+    own_acc, other_acc, lists, starts, entries, bounds, sems,
 ):
-    copy = pltpu.make_async_copy(other, other_here, sems.at[0])
-    copy.start()
     lists[0:1, :], starts[0:1, :] = own_list[...], own_start[...]
     lists[1:2, :], starts[1:2, :] = make_list(place, slots[...])
     scalars = [
-        pltpu.make_async_copy(lists, entries, sems.at[1]),
-        pltpu.make_async_copy(starts, bounds, sems.at[2]),
+        pltpu.make_async_copy(lists, entries, sems.at[0]),
+        pltpu.make_async_copy(starts, bounds, sems.at[1]),
     ]
     scalars[0].start()
     scalars[1].start()
@@ -153,8 +166,7 @@
     scalars[0].wait()
     scalars[1].wait()
     add_products(entries, bounds, 0, own, (b5, b6), EARLY, own_acc)
-    copy.wait()
-    add_products(entries, bounds, 1, other_here, (b0, b1, b2, b3, b4, b5, b6), 0, other_acc)
+    add_products(entries, bounds, 1, other, (b0, b1, b2, b3, b4, b5, b6), 0, other_acc)
 
 
 def late_kernel(place, lists, starts, own, other, b7, own_before, other_before, out, own_acc, other_acc):
@@ -224,35 +236,35 @@
     here = jax.ShapeDtypeStruct(own_values.shape, BF16)
     lists = lambda n: jax.ShapeDtypeStruct((n, LIST), I32)
     starts = lambda n: jax.ShapeDtypeStruct((n, SLOTS), I32)
-    own_sums, own_here, own_list, own_start = pl.pallas_call(
+    own_sums, own_here, other_here, own_list, own_start = pl.pallas_call(
         own_kernel,
-        out_shape=(sums, here, lists(1), starts(1)),
-        in_specs=[SMEM, VMEM, HBM] + [VMEM] * 5,
-        out_specs=(VMEM,) * 4,
+        out_shape=(sums, here, here, lists(1), starts(1)),
+        in_specs=[SMEM, VMEM] + [HBM] * 2 + [VMEM] * 5,
+        out_specs=(VMEM,) * 5,
         scratch_shapes=[
             pltpu.SMEM((1, LIST), I32),
             pltpu.SMEM((1, SLOTS), I32),
-            pltpu.SemaphoreType.DMA((3,)),
+            pltpu.SemaphoreType.DMA((4,)),
         ],
-        compiler_params=pltpu.CompilerParams(vmem_limit_bytes=45 << 20),
+        compiler_params=pltpu.CompilerParams(vmem_limit_bytes=41 << 20),
         cost_estimate=pl.CostEstimate(flops=SLOTS * TILE**3, bytes_accessed=8 << 20, transcendentals=0),
         name="own",
-    )(place, slots, own_values, own, one_a, one_b, two_a, two_b)
-    own_sums, other_sums, other_here, all_lists, all_starts = pl.pallas_call(
+    )(place, slots, own_values, other_values, own, one_a, one_b, two_a, two_b)
+    own_sums, other_sums, all_lists, all_starts = pl.pallas_call(
         other_kernel,
-        out_shape=(sums, sums, here, lists(2), starts(2)),
-        in_specs=[SMEM, VMEM, HBM] + [VMEM] * 11,
-        out_specs=(VMEM,) * 5,
+        out_shape=(sums, sums, lists(2), starts(2)),
+        in_specs=[SMEM] + [VMEM] * 13,
+        out_specs=(VMEM,) * 4,
         scratch_shapes=[
             pltpu.SMEM((2, LIST), I32),
             pltpu.SMEM((2, SLOTS), I32),
-            pltpu.SemaphoreType.DMA((3,)),
+            pltpu.SemaphoreType.DMA((2,)),
         ],
         compiler_params=pltpu.CompilerParams(vmem_limit_bytes=24 << 20),
         cost_estimate=pl.CostEstimate(flops=SLOTS * TILE**3, bytes_accessed=8 << 20, transcendentals=0),
         name="other",
     )(
-        place, other_slots, other_values, own_here, own_list, own_start, own_sums,
+        place, other_slots, other_here, own_here, own_list, own_start, own_sums,
         own, one_a, one_b, two_a, two_b, three_a, four,
     )
     partial = pl.pallas_call(
@@ -281,7 +293,7 @@
         name="dense",
     )(parts, weight, bias.reshape(1, HID), cotangent)
 
-    share = total(lax.all_to_all(grads, both, 0, 0, axis_index_groups=NEAR)).astype(BF16)
+    share = total(lax.all_to_all(grads.astype(BF16), both, 0, 0, axis_index_groups=NEAR)).astype(BF16)
     share = total(to_all(share, both, FAR))
     piece = jnp.concatenate([share[0:8], share[8:16]], axis=1)
     piece, grad_bias = lax.optimization_barrier((piece, share[16:18].reshape(HID)))

time: 127 us -> 126 us (level)
    all_to_all x1, blocking collectives: 10.4 us -> 9.08 us  [local(): lax.all_to_all(grads.astype(BF16), both, 0, 0, axis_index_groups=NEAR)]
  transfers between devices with their start and end apart: 9 -> 9, of which waited for: 0 -> 0; matrix products, arithmetic and copies ran while one was open for 1% -> 1% of each run, Pallas kernels for 7% -> 6%
where the time goes in v8:
time: 126 us; the launch traced here: 125 us
  blocking collectives  64.5 us (51%)
  starting transfers between devices  45.8 us (36%)
  Pallas kernels  10.2 us (8%)
  other arithmetic  1.57 us (1%)
  between operations  1.57 us (1%)
  local copies, waits for them, and re-layouts  1.37 us (1%)
    all_to_all x3, blocking collectives, to_all(): return lax.all_to_all(copies, axes, 0, 0, axis_index_groups=groups)  41.8 us
    ppermute x7, starting transfers between devices, shift(): return lax.ppermute(block, 'wide', pairs)  31.5 us
    all_to_all x1, blocking collectives, local(): lax.all_to_all(partial.reshape(8, rows, FIN), both, 0, 0, axis_index_grou...  13.6 us
    all_to_all x1, blocking collectives, local(): lax.all_to_all(grads.astype(BF16), both, 0, 0, axis_index_groups=NEAR)  9.08 us
    ppermute x1, starting transfers between devices, local(): other_values = lax.ppermute(own_values, 'wide', OTHER_CORE)  8.92 us
    ppermute x1, starting transfers between devices, local(): other_slots = lax.ppermute(slots, 'wide', OTHER_CORE)  5.37 us
    pallas_call x1, Pallas kernels, local(): pl.pallas_call(own_kernel, out_shape=(sums, here, here, lists(1), starts(...  4.05 us
    pallas_call x1, Pallas kernels, local(): pl.pallas_call(other_kernel, out_shape=(sums, sums, lists(2), starts(2)),...  3.9 us
  transfers between devices with their start and end apart: 9, of which 0 were waited for; matrix products, arithmetic and copies ran while one was open for 1% of the time, Pallas kernels for 6%

profile of v8, /device:TPU:1, one launch (start us, length us, event | category | flops | bytes accessed | tf_op | source)
XLA Modules:
  0.0 125.1 jit_solution(9227306752572376031)
XLA Ops:
  0.6 0.0 copy-start
  0.6 8.9 %collective-permute-start.1 = (bf16[128,128,128]{2,1,0:T(8,128)(2,1)}, bf16[128,128,128]{2,1,0:T(8,128)(2,1)}, u32[]{:S(2)}, u32[]{:S(2)}) collective-permute-start(bf16[128,128,128]{2,1,0:T(8,128)(2,1)} %bitcast.22), channel_id=1, source_target_pairs={{0,4},{4,0},{8,12},{12,8},{16,20},{20,16},{24,28},{28,24},{32,36},... | collective-permute-start | bytes 12582920 | tf_op jit(solution)/shard_map/ppermute | solution.py:220
  9.6 0.1 broadcast_in_dim.55
  9.7 14.5 %all_to_all.25 = bf16[8,256,128]{2,1,0:T(8,128)(2,1)S(1)} all-to-all(bf16[8,256,128]{2,1,0:T(8,128)(2,1)S(1)} %broadcast_in_dim.55), channel_id=1, replica_groups={{0,64,128,192,256,320,384,448},{8,72,136,200,264,328,392,456},{16,80,14..., dimensions={0} | all-to-all | bytes 1048576 | tf_op jit(solution)/shard_map/all_to_all | solution.py:57
  24.2 0.0 collective-permute-done.1.other
  24.2 4.9 %collective-permute-start.4 = (bf16[16,128,128]{2,1,0:T(8,128)(2,1)S(1)}, bf16[16,128,128]{2,1,0:T(8,128)(2,1)S(1)}, u32[]{:S(2)}, u32[]{:S(2)}) collective-permute-start(bf16[16,128,128]{2,1,0:T(8,128)(2,1)S(1)} %bitcast.14), channel_id=1, source_target_pairs={{0,16},{8,56},{16,32},{24,8},{32,48},{40,24},{48,0},{56,40},{64,80... | collective-permute-start | bytes 1572872 | tf_op jit(solution)/shard_map/ppermute | solution.py:62
  29.2 6.5 %collective-permute-start.5 = (bf16[16,128,128]{2,1,0:T(8,128)(2,1)S(1)}, bf16[16,128,128]{2,1,0:T(8,128)(2,1)S(1)}, u32[]{:S(2)}, u32[]{:S(2)}) collective-permute-start(bf16[16,128,128]{2,1,0:T(8,128)(2,1)S(1)} %bitcast.15), channel_id=1, source_target_pairs={{0,48},{8,24},{16,0},{24,40},{32,16},{40,56},{48,32},{56,8},{64,11... | collective-permute-start | bytes 1572872 | tf_op jit(solution)/shard_map/ppermute | solution.py:62
  35.7 3.1 %collective-permute-start.2 = (bf16[16,128,128]{2,1,0:T(8,128)(2,1)S(1)}, bf16[16,128,128]{2,1,0:T(8,128)(2,1)S(1)}, u32[]{:S(2)}, u32[]{:S(2)}) collective-permute-start(bf16[16,128,128]{2,1,0:T(8,128)(2,1)S(1)} %bitcast.16), channel_id=1, source_target_pairs={{0,8},{8,0},{16,24},{24,16},{32,40},{40,32},{48,56},{56,48},{64,72... | collective-permute-start | bytes 1572872 | tf_op jit(solution)/shard_map/ppermute | solution.py:62
  38.8 4.3 %collective-permute-start.3 = (bf16[16,128,128]{2,1,0:T(8,128)(2,1)S(1)}, bf16[16,128,128]{2,1,0:T(8,128)(2,1)S(1)}, u32[]{:S(2)}, u32[]{:S(2)}) collective-permute-start(bf16[16,128,128]{2,1,0:T(8,128)(2,1)S(1)} %bitcast.17), channel_id=1, source_target_pairs={{0,56},{8,16},{16,8},{24,32},{32,24},{40,48},{48,40},{56,0},{64,12... | collective-permute-start | bytes 1572872 | tf_op jit(solution)/shard_map/ppermute | solution.py:62
  43.1 5.5 %collective-permute-start.6 = (bf16[16,128,128]{2,1,0:T(8,128)(2,1)S(1)}, bf16[16,128,128]{2,1,0:T(8,128)(2,1)S(1)}, u32[]{:S(2)}, u32[]{:S(2)}) collective-permute-start(bf16[16,128,128]{2,1,0:T(8,128)(2,1)S(1)} %collective-permute-done.4.b3), channel_id=1, source_target_pairs={{0,8},{8,0},{16,24},{24,16},{32,40},{40,32},{48,56},{56,48},{64,72... | collective-permute-start | bytes 1572872 | tf_op jit(solution)/shard_map/ppermute | solution.py:62
  48.6 1.9 %collective-permute-start.7 = (bf16[16,128,128]{2,1,0:T(8,128)(2,1)S(1)}, bf16[16,128,128]{2,1,0:T(8,128)(2,1)S(1)}, u32[]{:S(2)}, u32[]{:S(2)}) collective-permute-start(bf16[16,128,128]{2,1,0:T(8,128)(2,1)S(1)} %collective-permute-done.4.b3), channel_id=1, source_target_pairs={{0,16},{8,56},{16,32},{24,8},{32,48},{40,24},{48,0},{56,40},{64,80... | collective-permute-start | bytes 1572872 | tf_op jit(solution)/shard_map/ppermute | solution.py:62
  50.5 5.4 %collective-permute-start.8 = (bf16[16,128,128]{2,1,0:T(8,128)(2,1)S(1)}, bf16[16,128,128]{2,1,0:T(8,128)(2,1)S(1)}, u32[]{:S(2)}, u32[]{:S(2)}) collective-permute-start(bf16[16,128,128]{2,1,0:T(8,128)(2,1)S(1)} %collective-permute-done.5.b4), channel_id=1, source_target_pairs={{0,56},{8,16},{16,8},{24,32},{32,24},{40,48},{48,40},{56,0},{64,12... | collective-permute-start | bytes 1572872 | tf_op jit(solution)/shard_map/ppermute | solution.py:62
  55.9 0.1 pad_add_fusion.place
  56.6 0.7 compare_select_fusion
  57.3 0.7 broadcast_select_fusion.slots
  58.0 5.4 %collective-permute-start = (s32[2,128]{1,0:T(2,128)S(1)}, s32[2,128]{1,0:T(2,128)S(1)}, u32[]{:S(2)}, u32[]{:S(2)}) collective-permute-start(s32[2,128]{1,0:T(2,128)S(1)} %broadcast_select_fusion.slots), channel_id=1, source_target_pairs={{0,4},{4,0},{8,12},{12,8},{16,20},{20,16},{24,28},{28,24},{32,36},... | collective-permute-start | bytes 3080 | tf_op jit(solution)/shard_map/ppermute | solution.py:232
  63.4 0.0 collective-permute-done.3.b2
  63.4 4.1 %own.1 = (f32[9,128,128]{2,1,0:T(8,128)S(1)}, bf16[128,128,128]{2,1,0:T(8,128)(2,1)S(1)}, bf16[128,128,128]{2,1,0:T(8,128)(2,1)S(1)}, s32[1,256]{1,0:T(1,128)S(1)}, s32[1,128]{1,0:T(1,128)S(1)}) custom-call(s32[2]{0:T(128)S(1)} %pad_add_fusion.place, s32[2,128]{1,0:T(2,128)S(1)} %broadcast_select_fusion.slots, bf16[128,128,128]{2,1,0:T(8,128)(2,1)} %bitcast.23, ...), custom_call_target="tpu_custom_call" | custom-call | flops 268435456 | bytes 8388608 | tf_op jit(solution)/shard_map/own/pallas_call | solution.py:239
  67.5 0.0 collective-permute-done.slots
  67.5 0.0 collective-permute-done.7.b6
  67.5 3.9 %other.1 = (f32[9,128,128]{2,1,0:T(8,128)S(1)}, f32[9,128,128]{2,1,0:T(8,128)S(1)}, s32[2,256]{1,0:T(2,128)S(1)}, s32[2,128]{1,0:T(2,128)S(1)}) custom-call(s32[2]{0:T(128)S(1)} %pad_add_fusion.place, s32[2,128]{1,0:T(2,128)S(1)} %collective-permute-done.slots, bf16[128,128,128]{2,1,0:T(8,128)(2,1)S(1)} %get-tuple-element.20.other, ...), custom_call_target="tpu_custom_call" | custom-call | flops 268435456 | bytes 8388608 | tf_op jit(solution)/shard_map/other/pallas_call | solution.py:253
  71.4 0.0 copy-start.1
  71.5 0.0 copy-start.2
  71.5 0.0 copy-start.3
  71.5 1.3 %late.1 = bf16[2,8,128,128]{3,2,1,0:T(8,128)(2,1)S(1)} custom-call(s32[2]{0:T(128)S(1)} %pad_add_fusion.place, s32[2,256]{1,0:T(2,128)S(1)} %get-tuple-element.25.lists, s32[2,128]{1,0:T(2,128)S(1)} %get-tuple-element.26.starts, bf16[128,128,128]{2,1,0:T(8,128)(2,1)S(1)} %get-tuple-element.21.own, bf16[128,128,128]{2,1,0:T(8,128)(2,1)S(1)} %get-tuple-element.20.other, ...), custom_call_target="tpu_custom_call" | custom-call | flops 268435456 | bytes 8388608 | tf_op jit(solution)/shard_map/late/pallas_call | solution.py:270
  72.8 13.6 %all_to_all.26.parts = bf16[8,256,128]{2,1,0:T(8,128)(2,1)S(1)} all-to-all(bf16[8,256,128]{2,1,0:T(8,128)(2,1)S(1)} %bitcast.20), channel_id=1, replica_groups={{0,1,2,3,4,5,6,7},{8,9,10,11,12,13,14,15},{16,17,18,19,20,21,22,23},{24..., dimensions={0} | all-to-all | bytes 1048576 | tf_op jit(solution)/shard_map/all_to_all | solution.py:282
  86.4 0.9 dense.1
  87.4 9.1 %all_to_all.27 = bf16[16,24,128]{2,1,0:T(8,128)(2,1)S(1)} all-to-all(bf16[16,24,128]{2,1,0:T(8,128)(2,1)S(1)} %convert_element_type.8), channel_id=1, replica_groups={{0,1,2,3,4,5,6,7,8,9,10,11,12,13,14,15},{16,17,18,19,20,21,22,23,24,25,..., dimensions={0} | all-to-all | bytes 196608 | tf_op jit(solution)/shard_map/all_to_all | solution.py:296
  96.5 16.0 %all_to_all.28 = bf16[32,24,128]{2,1,0:T(8,128)(2,1)S(1)} all-to-all(bf16[32,24,128]{2,1,0:T(8,128)(2,1)S(1)} %broadcast_in_dim.56), channel_id=1, replica_groups={{0,16,32,48,64,80,96,112,128,144,160,176,192,208,224,240,256,272,288,30..., dimensions={0} | all-to-all | bytes 393216 | tf_op jit(solution)/shard_map/all_to_all | solution.py:57
  112.6 0.6 slice_bitcast_fusion
  113.2 11.3 %all_to_all.29 = f32[16,8,256]{2,1,0:T(8,128)S(1)} all-to-all(f32[16,8,256]{2,1,0:T(8,128)S(1)} %broadcast_in_dim.57), channel_id=1, replica_groups={{0,1,2,3,4,5,6,7,8,9,10,11,12,13,14,15},{16,17,18,19,20,21,22,23,24,25,..., dimensions={0} | all-to-all | bytes 262144 | tf_op jit(solution)/shard_map/all_to_all | solution.py:57
  124.4 0.7 copy.14
  (18 shorter events, 0.2 us)
Async XLA Ops:
  0.6 9.0 %copy-start = (bf16[1024,128]{1,0:T(8,128)(2,1)S(1)}, bf16[1024,128]{1,0:T(8,128)(2,1)}, u32[]{:S(2)}) copy-start(bf16[1024,128]{1,0:T(8,128)(2,1)} %param.9) | copy-start | bytes 786436
  0.6 23.6 %collective-permute-start.1 = (bf16[128,128,128]{2,1,0:T(8,128)(2,1)}, bf16[128,128,128]{2,1,0:T(8,128)(2,1)}, u32[]{:S(2)}, u32[]{:S(2)}) collective-permute-start(bf16[128,128,128]{2,1,0:T(8,128)(2,1)} %bitcast.22), channel_id=1, source_target_pairs={{0,4},{4,0},{8,12},{12,8},{16,20},{20,16},{24,28},{28,24},{32,36},... | collective-permute-start | bytes 12582920 | tf_op jit(solution)/shard_map/ppermute | solution.py:220
  24.2 18.9 %collective-permute-start.4 = (bf16[16,128,128]{2,1,0:T(8,128)(2,1)S(1)}, bf16[16,128,128]{2,1,0:T(8,128)(2,1)S(1)}, u32[]{:S(2)}, u32[]{:S(2)}) collective-permute-start(bf16[16,128,128]{2,1,0:T(8,128)(2,1)S(1)} %bitcast.14), channel_id=1, source_target_pairs={{0,16},{8,56},{16,32},{24,8},{32,48},{40,24},{48,0},{56,40},{64,80... | collective-permute-start | bytes 1572872 | tf_op jit(solution)/shard_map/ppermute | solution.py:62
  29.2 21.3 %collective-permute-start.5 = (bf16[16,128,128]{2,1,0:T(8,128)(2,1)S(1)}, bf16[16,128,128]{2,1,0:T(8,128)(2,1)S(1)}, u32[]{:S(2)}, u32[]{:S(2)}) collective-permute-start(bf16[16,128,128]{2,1,0:T(8,128)(2,1)S(1)} %bitcast.15), channel_id=1, source_target_pairs={{0,48},{8,24},{16,0},{24,40},{32,16},{40,56},{48,32},{56,8},{64,11... | collective-permute-start | bytes 1572872 | tf_op jit(solution)/shard_map/ppermute | solution.py:62
  35.7 22.3 %collective-permute-start.2 = (bf16[16,128,128]{2,1,0:T(8,128)(2,1)S(1)}, bf16[16,128,128]{2,1,0:T(8,128)(2,1)S(1)}, u32[]{:S(2)}, u32[]{:S(2)}) collective-permute-start(bf16[16,128,128]{2,1,0:T(8,128)(2,1)S(1)} %bitcast.16), channel_id=1, source_target_pairs={{0,8},{8,0},{16,24},{24,16},{32,40},{40,32},{48,56},{56,48},{64,72... | collective-permute-start | bytes 1572872 | tf_op jit(solution)/shard_map/ppermute | solution.py:62
  38.8 24.6 %collective-permute-start.3 = (bf16[16,128,128]{2,1,0:T(8,128)(2,1)S(1)}, bf16[16,128,128]{2,1,0:T(8,128)(2,1)S(1)}, u32[]{:S(2)}, u32[]{:S(2)}) collective-permute-start(bf16[16,128,128]{2,1,0:T(8,128)(2,1)S(1)} %bitcast.17), channel_id=1, source_target_pairs={{0,56},{8,16},{16,8},{24,32},{32,24},{40,48},{48,40},{56,0},{64,12... | collective-permute-start | bytes 1572872 | tf_op jit(solution)/shard_map/ppermute | solution.py:62
  43.1 24.4 %collective-permute-start.6 = (bf16[16,128,128]{2,1,0:T(8,128)(2,1)S(1)}, bf16[16,128,128]{2,1,0:T(8,128)(2,1)S(1)}, u32[]{:S(2)}, u32[]{:S(2)}) collective-permute-start(bf16[16,128,128]{2,1,0:T(8,128)(2,1)S(1)} %collective-permute-done.4.b3), channel_id=1, source_target_pairs={{0,8},{8,0},{16,24},{24,16},{32,40},{40,32},{48,56},{56,48},{64,72... | collective-permute-start | bytes 1572872 | tf_op jit(solution)/shard_map/ppermute | solution.py:62
  48.6 18.9 %collective-permute-start.7 = (bf16[16,128,128]{2,1,0:T(8,128)(2,1)S(1)}, bf16[16,128,128]{2,1,0:T(8,128)(2,1)S(1)}, u32[]{:S(2)}, u32[]{:S(2)}) collective-permute-start(bf16[16,128,128]{2,1,0:T(8,128)(2,1)S(1)} %collective-permute-done.4.b3), channel_id=1, source_target_pairs={{0,16},{8,56},{16,32},{24,8},{32,48},{40,24},{48,0},{56,40},{64,80... | collective-permute-start | bytes 1572872 | tf_op jit(solution)/shard_map/ppermute | solution.py:62
  50.5 20.9 %collective-permute-start.8 = (bf16[16,128,128]{2,1,0:T(8,128)(2,1)S(1)}, bf16[16,128,128]{2,1,0:T(8,128)(2,1)S(1)}, u32[]{:S(2)}, u32[]{:S(2)}) collective-permute-start(bf16[16,128,128]{2,1,0:T(8,128)(2,1)S(1)} %collective-permute-done.5.b4), channel_id=1, source_target_pairs={{0,56},{8,16},{16,8},{24,32},{32,24},{40,48},{48,40},{56,0},{64,12... | collective-permute-start | bytes 1572872 | tf_op jit(solution)/shard_map/ppermute | solution.py:62
  58.0 9.5 %collective-permute-start = (s32[2,128]{1,0:T(2,128)S(1)}, s32[2,128]{1,0:T(2,128)S(1)}, u32[]{:S(2)}, u32[]{:S(2)}) collective-permute-start(s32[2,128]{1,0:T(2,128)S(1)} %broadcast_select_fusion.slots), channel_id=1, source_target_pairs={{0,4},{4,0},{8,12},{12,8},{16,20},{20,16},{24,28},{28,24},{32,36},... | collective-permute-start | bytes 3080 | tf_op jit(solution)/shard_map/ppermute | solution.py:232
  71.4 15.0 %copy-start.1 = (bf16[256,256]{1,0:T(8,128)(2,1)S(1)}, bf16[256,256]{1,0:T(8,128)(2,1)}, u32[]{:S(2)}) copy-start(bf16[256,256]{1,0:T(8,128)(2,1)} %cotangent.1) | copy-start | bytes 393220
  71.5 15.0 %copy-start.2 = (bf16[128,256]{1,0:T(8,128)(2,1)S(1)}, bf16[128,256]{1,0:T(8,128)(2,1)}, u32[]{:S(2)}) copy-start(bf16[128,256]{1,0:T(8,128)(2,1)} %weight.1) | copy-start | bytes 196612
  71.5 15.0 %copy-start.3 = (f32[256]{0:T(256)S(1)}, f32[256]{0:T(256)}, u32[]{:S(2)}) copy-start(f32[256]{0:T(256)} %param.11) | copy-start | bytes 3076

commit v9 on v8

--- a/solution.py
+++ b/solution.py
@@ -70,9 +70,10 @@
 
 def make_list(place, slots):
     core, at = place[0], place[1]
-    code, pick = slots[0:1], slots[1:2]
-    source = lax.shift_right_arithmetic(code, 3)
-    valid = (code >= 0) & ((source & 1) == core)
+    code = slots
+    source = lax.shift_right_arithmetic(code, 3) & (SLOTS - 1)
+    pick = lax.shift_right_arithmetic(code, 10) & 1
+    valid = (code < 2048) & ((source & 1) == core)
     rows = lax.broadcasted_iota(I32, (SLOTS, SLOTS), 0)
     kinds = lax.broadcasted_iota(I32, (SLOTS, SLOTS), 1)
     lanes = lax.broadcasted_iota(I32, (1, SLOTS), 1)
@@ -226,9 +227,7 @@
     four = shift(two_a, 2)
 
     live = jnp.arange(SLOTS, dtype=I32) < tile_count[0, 0]
-    code = jnp.where(live, tile_row[0, 0] + TR * tile_source[0, 0], -1)
-    first_row = jnp.arange(2, dtype=I32)[:, None] == 0
-    slots = jnp.where(first_row, code[None, :], pick[0])
+    slots = (tile_row[0] + TR * tile_source[0]) + (1024 * pick[0] + jnp.where(live, 0, 2048)[None])
     other_slots = lax.ppermute(slots, "wide", OTHER_CORE)
     place = jnp.stack([core, jnp.where(core == 0, lax.rem(index // 2, 8), index // 16)])
 

time: 126 us -> 126 us (level)
  Pallas kernels: 10.2 us -> 11.5 us
    select_n x2 -> x0, other arithmetic: 1.4 us -> none  [the longest x1 0.73 us: local(): slots = jnp.where(first_row, code[None, :], pick[0])]
  transfers between devices with their start and end apart: 9 -> 9, of which waited for: 0 -> 0; matrix products, arithmetic and copies ran while one was open for 1% -> 1% of each run, Pallas kernels for 6% -> 7%
where the time goes in v9:
time: 126 us; the launch traced here: 125 us
  blocking collectives  64 us (51%)
  starting transfers between devices  45.9 us (36%)
  Pallas kernels  11.5 us (9%)
  between operations  1.55 us (1%)
  local copies, waits for them, and re-layouts  1.37 us (1%)
    all_to_all x3, blocking collectives, to_all(): return lax.all_to_all(copies, axes, 0, 0, axis_index_groups=groups)  41.7 us
    ppermute x7, starting transfers between devices, shift(): return lax.ppermute(block, 'wide', pairs)  31.6 us
    all_to_all x1, blocking collectives, local(): lax.all_to_all(partial.reshape(8, rows, FIN), both, 0, 0, axis_index_grou...  13.2 us
    all_to_all x1, blocking collectives, local(): lax.all_to_all(grads.astype(BF16), both, 0, 0, axis_index_groups=NEAR)  9.08 us
    ppermute x1, starting transfers between devices, local(): other_values = lax.ppermute(own_values, 'wide', OTHER_CORE)  8.92 us
    ppermute x1, starting transfers between devices, local(): other_slots = lax.ppermute(slots, 'wide', OTHER_CORE)  5.37 us
    pallas_call x1, Pallas kernels, local(): pl.pallas_call(other_kernel, out_shape=(sums, sums, lists(2), starts(2)),...  4.72 us
    pallas_call x1, Pallas kernels, local(): pl.pallas_call(own_kernel, out_shape=(sums, here, here, lists(1), starts(...  4.46 us
  transfers between devices with their start and end apart: 9, of which 0 were waited for; matrix products, arithmetic and copies ran while one was open for 1% of the time, Pallas kernels for 7%

profile of v9, /device:TPU:1, one launch (start us, length us, event | category | flops | bytes accessed | tf_op | source)
XLA Modules:
  0.0 125.2 jit_solution(9973798248149290312)
XLA Ops:
  0.6 0.0 copy-start
  0.6 8.9 %collective-permute-start.1 = (bf16[128,128,128]{2,1,0:T(8,128)(2,1)}, bf16[128,128,128]{2,1,0:T(8,128)(2,1)}, u32[]{:S(2)}, u32[]{:S(2)}) collective-permute-start(bf16[128,128,128]{2,1,0:T(8,128)(2,1)} %bitcast.23), channel_id=1, source_target_pairs={{0,4},{4,0},{8,12},{12,8},{16,20},{20,16},{24,28},{28,24},{32,36},... | collective-permute-start | bytes 12582920 | tf_op jit(solution)/shard_map/ppermute | solution.py:221
  9.6 0.1 broadcast_in_dim.16
  9.7 14.5 %all_to_all.25 = bf16[8,256,128]{2,1,0:T(8,128)(2,1)S(1)} all-to-all(bf16[8,256,128]{2,1,0:T(8,128)(2,1)S(1)} %broadcast_in_dim.16), channel_id=1, replica_groups={{0,64,128,192,256,320,384,448},{8,72,136,200,264,328,392,456},{16,80,14..., dimensions={0} | all-to-all | bytes 1048576 | tf_op jit(solution)/shard_map/all_to_all | solution.py:57
  24.2 0.0 collective-permute-done.1.other
  24.2 4.9 %collective-permute-start.4 = (bf16[16,128,128]{2,1,0:T(8,128)(2,1)S(1)}, bf16[16,128,128]{2,1,0:T(8,128)(2,1)S(1)}, u32[]{:S(2)}, u32[]{:S(2)}) collective-permute-start(bf16[16,128,128]{2,1,0:T(8,128)(2,1)S(1)} %bitcast.15), channel_id=1, source_target_pairs={{0,16},{8,56},{16,32},{24,8},{32,48},{40,24},{48,0},{56,40},{64,80... | collective-permute-start | bytes 1572872 | tf_op jit(solution)/shard_map/ppermute | solution.py:62
  29.2 6.5 %collective-permute-start.5 = (bf16[16,128,128]{2,1,0:T(8,128)(2,1)S(1)}, bf16[16,128,128]{2,1,0:T(8,128)(2,1)S(1)}, u32[]{:S(2)}, u32[]{:S(2)}) collective-permute-start(bf16[16,128,128]{2,1,0:T(8,128)(2,1)S(1)} %bitcast.16), channel_id=1, source_target_pairs={{0,48},{8,24},{16,0},{24,40},{32,16},{40,56},{48,32},{56,8},{64,11... | collective-permute-start | bytes 1572872 | tf_op jit(solution)/shard_map/ppermute | solution.py:62
  35.7 3.1 %collective-permute-start.2 = (bf16[16,128,128]{2,1,0:T(8,128)(2,1)S(1)}, bf16[16,128,128]{2,1,0:T(8,128)(2,1)S(1)}, u32[]{:S(2)}, u32[]{:S(2)}) collective-permute-start(bf16[16,128,128]{2,1,0:T(8,128)(2,1)S(1)} %bitcast.17), channel_id=1, source_target_pairs={{0,8},{8,0},{16,24},{24,16},{32,40},{40,32},{48,56},{56,48},{64,72... | collective-permute-start | bytes 1572872 | tf_op jit(solution)/shard_map/ppermute | solution.py:62
  38.8 4.3 %collective-permute-start.3 = (bf16[16,128,128]{2,1,0:T(8,128)(2,1)S(1)}, bf16[16,128,128]{2,1,0:T(8,128)(2,1)S(1)}, u32[]{:S(2)}, u32[]{:S(2)}) collective-permute-start(bf16[16,128,128]{2,1,0:T(8,128)(2,1)S(1)} %bitcast.18), channel_id=1, source_target_pairs={{0,56},{8,16},{16,8},{24,32},{32,24},{40,48},{48,40},{56,0},{64,12... | collective-permute-start | bytes 1572872 | tf_op jit(solution)/shard_map/ppermute | solution.py:62
  43.1 0.0 collective-permute-done.4.b3
  43.1 5.5 %collective-permute-start.6 = (bf16[16,128,128]{2,1,0:T(8,128)(2,1)S(1)}, bf16[16,128,128]{2,1,0:T(8,128)(2,1)}, u32[]{:S(2)}, u32[]{:S(2)}) collective-permute-start(bf16[16,128,128]{2,1,0:T(8,128)(2,1)S(1)} %collective-permute-done.4.b3), channel_id=1, source_target_pairs={{0,8},{8,0},{16,24},{24,16},{32,40},{40,32},{48,56},{56,48},{64,72... | collective-permute-start | bytes 1572872 | tf_op jit(solution)/shard_map/ppermute | solution.py:62
  48.6 1.9 %collective-permute-start.7 = (bf16[16,128,128]{2,1,0:T(8,128)(2,1)S(1)}, bf16[16,128,128]{2,1,0:T(8,128)(2,1)}, u32[]{:S(2)}, u32[]{:S(2)}) collective-permute-start(bf16[16,128,128]{2,1,0:T(8,128)(2,1)S(1)} %collective-permute-done.4.b3), channel_id=1, source_target_pairs={{0,16},{8,56},{16,32},{24,8},{32,48},{40,24},{48,0},{56,40},{64,80... | collective-permute-start | bytes 1572872 | tf_op jit(solution)/shard_map/ppermute | solution.py:62
  50.5 0.0 collective-permute-done.5.b4
  50.5 5.4 %collective-permute-start.8 = (bf16[16,128,128]{2,1,0:T(8,128)(2,1)S(1)}, bf16[16,128,128]{2,1,0:T(8,128)(2,1)S(1)}, u32[]{:S(2)}, u32[]{:S(2)}) collective-permute-start(bf16[16,128,128]{2,1,0:T(8,128)(2,1)S(1)} %collective-permute-done.5.b4), channel_id=1, source_target_pairs={{0,56},{8,16},{16,8},{24,32},{32,24},{40,48},{48,40},{56,0},{64,12... | collective-permute-start | bytes 1572872 | tf_op jit(solution)/shard_map/ppermute | solution.py:62
  56.6 0.1 pad_add_fusion.place
  56.7 0.7 fusion.1.slots
  57.4 5.4 %collective-permute-start = (s32[1,128]{1,0:T(1,128)S(1)}, s32[1,128]{1,0:T(1,128)S(1)}, u32[]{:S(2)}, u32[]{:S(2)}) collective-permute-start(s32[1,128]{1,0:T(1,128)S(1)} %fusion.1.slots), channel_id=1, source_target_pairs={{0,4},{4,0},{8,12},{12,8},{16,20},{20,16},{24,28},{28,24},{32,36},... | collective-permute-start | bytes 1544 | tf_op jit(solution)/shard_map/ppermute | solution.py:231
  62.7 0.0 collective-permute-done.3.b2
  62.7 4.5 %own.1 = (f32[9,128,128]{2,1,0:T(8,128)S(1)}, bf16[128,128,128]{2,1,0:T(8,128)(2,1)S(1)}, bf16[128,128,128]{2,1,0:T(8,128)(2,1)S(1)}, s32[1,256]{1,0:T(1,128)S(1)}, s32[1,128]{1,0:T(1,128)S(1)}) custom-call(s32[2]{0:T(128)S(1)} %pad_add_fusion.place, s32[1,128]{1,0:T(1,128)S(1)} %fusion.1.slots, bf16[128,128,128]{2,1,0:T(8,128)(2,1)} %bitcast.24, ...), custom_call_target="tpu_custom_call" | custom-call | flops 268435456 | bytes 8388608 | tf_op jit(solution)/shard_map/own/pallas_call | solution.py:238
  67.2 0.0 collective-permute-done.7.b6
  67.3 4.7 %other.1 = (f32[9,128,128]{2,1,0:T(8,128)S(1)}, f32[9,128,128]{2,1,0:T(8,128)S(1)}, s32[2,256]{1,0:T(2,128)S(1)}, s32[2,128]{1,0:T(2,128)S(1)}) custom-call(s32[2]{0:T(128)S(1)} %pad_add_fusion.place, s32[1,128]{1,0:T(1,128)S(1)} %collective-permute-done.slots, bf16[128,128,128]{2,1,0:T(8,128)(2,1)S(1)} %get-tuple-element.20.other, ...), custom_call_target="tpu_custom_call" | custom-call | flops 268435456 | bytes 8388608 | tf_op jit(solution)/shard_map/other/pallas_call | solution.py:252
  72.0 0.0 copy-start.1
  72.0 0.0 copy-start.2
  72.0 0.0 copy-start.3
  72.0 1.4 %late.1 = bf16[2,8,128,128]{3,2,1,0:T(8,128)(2,1)S(1)} custom-call(s32[2]{0:T(128)S(1)} %pad_add_fusion.place, s32[2,256]{1,0:T(2,128)S(1)} %get-tuple-element.25.lists, s32[2,128]{1,0:T(2,128)S(1)} %get-tuple-element.26.starts, bf16[128,128,128]{2,1,0:T(8,128)(2,1)S(1)} %get-tuple-element.21.own, bf16[128,128,128]{2,1,0:T(8,128)(2,1)S(1)} %get-tuple-element.20.other, ...), custom_call_target="tpu_custom_call" | custom-call | flops 268435456 | bytes 8388608 | tf_op jit(solution)/shard_map/late/pallas_call | solution.py:269
  73.5 13.2 %all_to_all.26.parts = bf16[8,256,128]{2,1,0:T(8,128)(2,1)S(1)} all-to-all(bf16[8,256,128]{2,1,0:T(8,128)(2,1)S(1)} %bitcast.21), channel_id=1, replica_groups={{0,1,2,3,4,5,6,7},{8,9,10,11,12,13,14,15},{16,17,18,19,20,21,22,23},{24..., dimensions={0} | all-to-all | bytes 1048576 | tf_op jit(solution)/shard_map/all_to_all | solution.py:281
  86.7 0.9 dense.1
  87.6 9.1 %all_to_all.27 = bf16[16,24,128]{2,1,0:T(8,128)(2,1)S(1)} all-to-all(bf16[16,24,128]{2,1,0:T(8,128)(2,1)S(1)} %convert_element_type.8), channel_id=1, replica_groups={{0,1,2,3,4,5,6,7,8,9,10,11,12,13,14,15},{16,17,18,19,20,21,22,23,24,25,..., dimensions={0} | all-to-all | bytes 196608 | tf_op jit(solution)/shard_map/all_to_all | solution.py:295
  96.7 15.9 %all_to_all.28 = bf16[32,24,128]{2,1,0:T(8,128)(2,1)S(1)} all-to-all(bf16[32,24,128]{2,1,0:T(8,128)(2,1)S(1)} %broadcast_in_dim.30), channel_id=1, replica_groups={{0,16,32,48,64,80,96,112,128,144,160,176,192,208,224,240,256,272,288,30..., dimensions={0} | all-to-all | bytes 393216 | tf_op jit(solution)/shard_map/all_to_all | solution.py:57
  112.7 0.6 slice_bitcast_fusion
  113.3 11.3 %all_to_all.29 = f32[16,8,256]{2,1,0:T(8,128)S(1)} all-to-all(f32[16,8,256]{2,1,0:T(8,128)S(1)} %broadcast_in_dim.31), channel_id=1, replica_groups={{0,1,2,3,4,5,6,7,8,9,10,11,12,13,14,15},{16,17,18,19,20,21,22,23,24,25,..., dimensions={0} | all-to-all | bytes 262144 | tf_op jit(solution)/shard_map/all_to_all | solution.py:57
  124.5 0.7 copy.14
  (16 shorter events, 0.2 us)
Async XLA Ops:
  0.6 9.0 %copy-start = (bf16[1024,128]{1,0:T(8,128)(2,1)S(1)}, bf16[1024,128]{1,0:T(8,128)(2,1)}, u32[]{:S(2)}) copy-start(bf16[1024,128]{1,0:T(8,128)(2,1)} %param.9) | copy-start | bytes 786436
  0.6 23.6 %collective-permute-start.1 = (bf16[128,128,128]{2,1,0:T(8,128)(2,1)}, bf16[128,128,128]{2,1,0:T(8,128)(2,1)}, u32[]{:S(2)}, u32[]{:S(2)}) collective-permute-start(bf16[128,128,128]{2,1,0:T(8,128)(2,1)} %bitcast.23), channel_id=1, source_target_pairs={{0,4},{4,0},{8,12},{12,8},{16,20},{20,16},{24,28},{28,24},{32,36},... | collective-permute-start | bytes 12582920 | tf_op jit(solution)/shard_map/ppermute | solution.py:221
  24.2 18.8 %collective-permute-start.4 = (bf16[16,128,128]{2,1,0:T(8,128)(2,1)S(1)}, bf16[16,128,128]{2,1,0:T(8,128)(2,1)S(1)}, u32[]{:S(2)}, u32[]{:S(2)}) collective-permute-start(bf16[16,128,128]{2,1,0:T(8,128)(2,1)S(1)} %bitcast.15), channel_id=1, source_target_pairs={{0,16},{8,56},{16,32},{24,8},{32,48},{40,24},{48,0},{56,40},{64,80... | collective-permute-start | bytes 1572872 | tf_op jit(solution)/shard_map/ppermute | solution.py:62
  29.2 21.3 %collective-permute-start.5 = (bf16[16,128,128]{2,1,0:T(8,128)(2,1)S(1)}, bf16[16,128,128]{2,1,0:T(8,128)(2,1)S(1)}, u32[]{:S(2)}, u32[]{:S(2)}) collective-permute-start(bf16[16,128,128]{2,1,0:T(8,128)(2,1)S(1)} %bitcast.16), channel_id=1, source_target_pairs={{0,48},{8,24},{16,0},{24,40},{32,16},{40,56},{48,32},{56,8},{64,11... | collective-permute-start | bytes 1572872 | tf_op jit(solution)/shard_map/ppermute | solution.py:62
  35.7 21.7 %collective-permute-start.2 = (bf16[16,128,128]{2,1,0:T(8,128)(2,1)S(1)}, bf16[16,128,128]{2,1,0:T(8,128)(2,1)S(1)}, u32[]{:S(2)}, u32[]{:S(2)}) collective-permute-start(bf16[16,128,128]{2,1,0:T(8,128)(2,1)S(1)} %bitcast.17), channel_id=1, source_target_pairs={{0,8},{8,0},{16,24},{24,16},{32,40},{40,32},{48,56},{56,48},{64,72... | collective-permute-start | bytes 1572872 | tf_op jit(solution)/shard_map/ppermute | solution.py:62
  38.8 24.0 %collective-permute-start.3 = (bf16[16,128,128]{2,1,0:T(8,128)(2,1)S(1)}, bf16[16,128,128]{2,1,0:T(8,128)(2,1)S(1)}, u32[]{:S(2)}, u32[]{:S(2)}) collective-permute-start(bf16[16,128,128]{2,1,0:T(8,128)(2,1)S(1)} %bitcast.18), channel_id=1, source_target_pairs={{0,56},{8,16},{16,8},{24,32},{32,24},{40,48},{48,40},{56,0},{64,12... | collective-permute-start | bytes 1572872 | tf_op jit(solution)/shard_map/ppermute | solution.py:62
  43.1 24.1 %collective-permute-start.6 = (bf16[16,128,128]{2,1,0:T(8,128)(2,1)S(1)}, bf16[16,128,128]{2,1,0:T(8,128)(2,1)}, u32[]{:S(2)}, u32[]{:S(2)}) collective-permute-start(bf16[16,128,128]{2,1,0:T(8,128)(2,1)S(1)} %collective-permute-done.4.b3), channel_id=1, source_target_pairs={{0,8},{8,0},{16,24},{24,16},{32,40},{40,32},{48,56},{56,48},{64,72... | collective-permute-start | bytes 1572872 | tf_op jit(solution)/shard_map/ppermute | solution.py:62
  48.6 18.6 %collective-permute-start.7 = (bf16[16,128,128]{2,1,0:T(8,128)(2,1)S(1)}, bf16[16,128,128]{2,1,0:T(8,128)(2,1)}, u32[]{:S(2)}, u32[]{:S(2)}) collective-permute-start(bf16[16,128,128]{2,1,0:T(8,128)(2,1)S(1)} %collective-permute-done.4.b3), channel_id=1, source_target_pairs={{0,16},{8,56},{16,32},{24,8},{32,48},{40,24},{48,0},{56,40},{64,80... | collective-permute-start | bytes 1572872 | tf_op jit(solution)/shard_map/ppermute | solution.py:62
  50.5 21.4 %collective-permute-start.8 = (bf16[16,128,128]{2,1,0:T(8,128)(2,1)S(1)}, bf16[16,128,128]{2,1,0:T(8,128)(2,1)S(1)}, u32[]{:S(2)}, u32[]{:S(2)}) collective-permute-start(bf16[16,128,128]{2,1,0:T(8,128)(2,1)S(1)} %collective-permute-done.5.b4), channel_id=1, source_target_pairs={{0,56},{8,16},{16,8},{24,32},{32,24},{40,48},{48,40},{56,0},{64,12... | collective-permute-start | bytes 1572872 | tf_op jit(solution)/shard_map/ppermute | solution.py:62
  57.4 9.9 %collective-permute-start = (s32[1,128]{1,0:T(1,128)S(1)}, s32[1,128]{1,0:T(1,128)S(1)}, u32[]{:S(2)}, u32[]{:S(2)}) collective-permute-start(s32[1,128]{1,0:T(1,128)S(1)} %fusion.1.slots), channel_id=1, source_target_pairs={{0,4},{4,0},{8,12},{12,8},{16,20},{20,16},{24,28},{28,24},{32,36},... | collective-permute-start | bytes 1544 | tf_op jit(solution)/shard_map/ppermute | solution.py:231
  72.0 14.7 %copy-start.1 = (bf16[256,256]{1,0:T(8,128)(2,1)S(1)}, bf16[256,256]{1,0:T(8,128)(2,1)}, u32[]{:S(2)}) copy-start(bf16[256,256]{1,0:T(8,128)(2,1)} %cotangent.1) | copy-start | bytes 393220
  72.0 14.6 %copy-start.2 = (bf16[128,256]{1,0:T(8,128)(2,1)S(1)}, bf16[128,256]{1,0:T(8,128)(2,1)}, u32[]{:S(2)}) copy-start(bf16[128,256]{1,0:T(8,128)(2,1)} %weight.1) | copy-start | bytes 196612
  72.0 14.6 %copy-start.3 = (f32[256]{0:T(256)S(1)}, f32[256]{0:T(256)}, u32[]{:S(2)}) copy-start(f32[256]{0:T(256)} %param.11) | copy-start | bytes 3076
